TPU v7x, 32 devices: a whole 2x2x4 slice. The times are simulated.
32 devices in a mesh: lon: 8 (over z, y), lat: 4 (over x, core).
Axes of the slice: x: 2, y: 2, z: 4, core: 2. Of those that a mesh axis runs over, the one named last changes fastest.
Arguments:
- queries: bfloat16 [64, 128, 256], P('lat', 'lon'), may hold values from -11 to 11
- key_values: bfloat16 [2, 64, 128, 256], P(None, 'lat', 'lon'), may hold values from -11 to 11
- pole_mask: int32 [8], replicated, may hold values 0 or 1
- sea_mask: int32 [8, 16], replicated, may hold values 0 or 1
- reg_queries: bfloat16 [256, 256], replicated, may hold values from -21 to 21
- reg_keys: bfloat16 [256, 256], replicated, may hold values from -6 to 6
Outputs:
- attended: bfloat16 [64, 128, 256], P('lat', 'lon')
- reg_out: bfloat16 [256, 256], replicated
All inputs are finite; a program needn't handle non-finite values.
Results may differ from a plain program's by a relative error of at most 0.0048.
Values may be sent and summed in bfloat16 or wider, within the bound.
No kernel may reach another device: no remote copies, remote signals or barrier semaphores. Data moves between devices by JAX's collectives and lax.ppermute only.
A program may use at most 64 MiB of HBM per device.

v0:
```python
import jax
import jax.numpy as jnp
from jax import lax
from jax.sharding import PartitionSpec as P

HEADS = 4
HEAD_DIM = 64
NREG = 256
RADIUS = 6
TILE = 8
QROWS = 16


def extended_2(shard, sides, width):
    for axis, dim in sides:
        peers, length = (lax.axis_size(axis), shard.shape[dim])
        up = [(i, (i + 1) % peers) for i in range(peers)]
        down = [(j, i) for i, j in up]
        last = lax.slice_in_dim(shard, length - width, length, axis=dim)
        leading = lax.slice_in_dim(shard, 0, width, axis=dim)
        before = lax.ppermute(last, axis, up)
        after = lax.ppermute(leading, axis, down)
        shard = jnp.concatenate([before, shard, after], axis=dim)
    return shard


def key_window(pole_mask, sea_mask, lat_first, lon_first, ext_rows, ext_cols, grid_cols):
    lat_cells = lat_first + jnp.arange(ext_rows, dtype=jnp.int32) - RADIUS
    lon_cells = (lon_first + jnp.arange(ext_cols, dtype=jnp.int32) - RADIUS) % grid_cols
    row_pick = (
        lat_cells[:, None] // TILE == jnp.arange(pole_mask.shape[0], dtype=jnp.int32)[None, :]
    ).astype(jnp.float32)
    row_pick = row_pick * pole_mask.astype(jnp.float32)[None, :]
    col_pick = (
        lon_cells[:, None] // TILE == jnp.arange(sea_mask.shape[1], dtype=jnp.int32)[None, :]
    ).astype(jnp.float32)
    coverage = jnp.dot(jnp.dot(row_pick, sea_mask.astype(jnp.float32)), col_pick.T)
    return coverage > 0.5


def register_values(key_values, reg_queries):
    lat_rows, lon_cols, channels = key_values.shape[1:]
    scale_factor = HEAD_DIM ** (-0.5)
    local_keys = key_values[0].reshape(lat_rows * lon_cols, HEADS, HEAD_DIM)
    local_values = key_values[1].reshape(lat_rows * lon_cols, HEADS, HEAD_DIM)
    query_heads = reg_queries.reshape(NREG, HEADS, HEAD_DIM)
    scores = (
        jnp.einsum("rhd,khd->hrk", query_heads, local_keys, preferred_element_type=jnp.float32)
        * scale_factor
    )
    highest = lax.pmax(jnp.max(scores, axis=2), ("lon", "lat"))
    weights = jnp.exp(scores - highest[:, :, None])
    weight_sums = jnp.sum(weights, axis=2).T
    weighted = jnp.einsum(
        "hrk,khd->rhd",
        weights.astype(jnp.bfloat16),
        local_values,
        preferred_element_type=jnp.float32,
    )
    weighted = weighted.reshape(NREG, channels)
    total_sums, total_weighted = lax.psum((weight_sums, weighted), ("lon", "lat"))
    merged = (total_weighted.reshape(NREG, HEADS, HEAD_DIM) / total_sums[:, :, None]).astype(
        jnp.bfloat16
    )
    finished = merged.reshape(NREG, channels)
    return finished


def shards(queries, key_values, pole_mask, sea_mask, reg_queries, reg_keys):
    lat_rows, lon_cols, channels = queries.shape
    scale_factor = HEAD_DIM ** (-0.5)
    ext_rows = lat_rows + 2 * RADIUS
    ext_cols = lon_cols + 2 * RADIUS
    grid_cols = lon_cols * lax.axis_size("lon")
    extended = extended_2(key_values, (("lon", 2), ("lat", 1)), RADIUS)
    reg_vals = register_values(key_values, reg_queries)
    keep_window = key_window(
        pole_mask,
        sea_mask,
        lax.axis_index("lat") * lat_rows,
        lax.axis_index("lon") * lon_cols,
        ext_rows,
        ext_cols,
        grid_cols,
    )
    block_rows = QROWS
    query_count = block_rows * lon_cols
    key_count = (block_rows + 2 * RADIUS) * ext_cols
    query_index = jnp.arange(query_count, dtype=jnp.int32)
    key_index = jnp.arange(key_count, dtype=jnp.int32)
    query_lat = query_index // lon_cols
    query_lon = query_index % lon_cols
    key_lat = key_index // ext_cols
    key_lon = key_index % ext_cols
    nearby = (jnp.abs(key_lat[None, :] - RADIUS - query_lat[:, None]) <= RADIUS) & (
        jnp.abs(key_lon[None, :] - RADIUS - query_lon[:, None]) <= RADIUS
    )
    reg_key_heads = reg_keys.reshape(NREG, HEADS, HEAD_DIM)
    reg_value_heads = reg_vals.reshape(NREG, HEADS, HEAD_DIM)

    def one_block(first_row):
        block_queries = queries.reshape(query_count, HEADS, HEAD_DIM)
        block_keys = extended[0].reshape(key_count, HEADS, HEAD_DIM)
        block_values = extended[1].reshape(key_count, HEADS, HEAD_DIM)
        block_keep = keep_window.reshape(key_count)
        allowed = nearby & block_keep[None, :]
        near_scores = (
            jnp.einsum(
                "qhd,khd->hqk", block_queries, block_keys, preferred_element_type=jnp.float32
            )
            * scale_factor
        )
        near_scores = jnp.where(allowed[None], near_scores, -jnp.inf)
        reg_scores = (
            jnp.einsum(
                "qhd,rhd->hqr", block_queries, reg_key_heads, preferred_element_type=jnp.float32
            )
            * scale_factor
        )
        highest = jnp.maximum(jnp.max(near_scores, axis=2), jnp.max(reg_scores, axis=2))
        near_weights = jnp.exp(near_scores - highest[:, :, None])
        reg_weights = jnp.exp(reg_scores - highest[:, :, None])
        weight_sums = jnp.sum(near_weights, axis=2) + jnp.sum(reg_weights, axis=2)
        mixture = jnp.einsum(
            "hqk,khd->qhd",
            near_weights.astype(jnp.bfloat16),
            block_values,
            preferred_element_type=jnp.float32,
        )
        mixture = mixture + jnp.einsum(
            "hqr,rhd->qhd",
            reg_weights.astype(jnp.bfloat16),
            reg_value_heads,
            preferred_element_type=jnp.float32,
        )
        result = mixture / weight_sums.T[:, :, None]
        return result.astype(jnp.bfloat16).reshape(block_rows, lon_cols, channels)

    starts = jnp.arange(lat_rows // block_rows, dtype=jnp.int32) * block_rows
    blocks = lax.map(one_block, starts)
    return (blocks.reshape(lat_rows, lon_cols, channels), reg_vals)


def solution(mesh):
    return jax.shard_map(
        shards,
        mesh=mesh,
        in_specs=(P("lat", "lon", None), P(None, "lat", "lon", None), P(), P(), P(), P()),
        out_specs=(P("lat", "lon", None), P()),
        check_vma=False,
    )
```

profile of v0, /device:TPU:0, one launch (start us, length us, event | category | flops | bytes accessed | tf_op | source)
XLA Modules:
  0.0 199.1 jit_solution(11677986811757508790)
XLA Ops:
  7.2 1.0 fusion.62
  8.3 3.0 %collective-permute-start = (bf16[2,16,6,256]{3,2,1,0:T(8,128)(2,1)S(1)}, bf16[2,16,6,256]{3,2,1,0:T(8,128)(2,1)S(1)}, u32[]{:S(2)}, u32[]{:S(2)}) collective-permute-start(bf16[2,16,6,256]{3,2,1,0:T(8,128)(2,1)S(1)} %get-tuple-element.36), channel_id=1, source_target_pairs={{0,4},{4,8},{8,12},{12,16},{16,20},{20,24},{24,28},{28,0},{1,5},{5... | collective-permute-start | bytes 294920 | tf_op jit(solution)/shard_map/ppermute | solution.py:21
  11.3 3.1 %collective-permute-start.1 = (bf16[2,16,6,256]{3,2,1,0:T(8,128)(2,1)S(1)}, bf16[2,16,6,256]{3,2,1,0:T(8,128)(2,1)S(1)}, u32[]{:S(2)}, u32[]{:S(2)}) collective-permute-start(bf16[2,16,6,256]{3,2,1,0:T(8,128)(2,1)S(1)} %get-tuple-element.37), channel_id=1, source_target_pairs={{4,0},{8,4},{12,8},{16,12},{20,16},{24,20},{28,24},{0,28},{5,1},{9... | collective-permute-start | bytes 294920 | tf_op jit(solution)/shard_map/ppermute | solution.py:22
  14.4 1.0 fusion.61
  15.6 1.0 copy.27
  16.6 0.3 fusion.64
  16.9 38.0 %pmax.7 = f32[4,256]{1,0:T(4,128)S(1)} all-reduce(f32[4,256]{1,0:T(4,128)S(1)} %get-tuple-element.42), channel_id=1, replica_groups=mesh['lon'=8,'lat'=4] {'lon','lat'}, use_global_device_ids=true, to_apply=%region_3.0 | all-reduce | flops 1024 | bytes 8192 | tf_op jit(solution)/shard_map/pmax | solution.py:51
  55.0 1.0 fusion.25
  56.3 0.3 fusion.12
  57.2 41.5 %psum.15 = f32[256,4]{0,1:T(4,128)S(1)} all-reduce(f32[256,4]{0,1:T(4,128)S(1)} %bitcast.40), channel_id=1, replica_groups=mesh['lon'=8,'lat'=4] {'lon','lat'}, use_global_device_ids=true, to_apply=%region_6.7 | all-reduce | flops 1024 | bytes 8192 | tf_op jit(solution)/shard_map/psum | solution.py:61
  98.7 0.4 fusion.63
  99.3 1.7 collective-permute-start.3
  101.0 0.7 fusion.23
  101.8 80.2 %all-reduce.2.cloned.1.call-done = f32[256,256]{0,1:T(8,128)} async-done(((f32[256,256]{0,1:T(8,128)}), f32[256,256]{0,1:T(8,128)}) %all-reduce.2.cloned.1.call-update) | async-done | bytes 262160 | tf_op jit(solution)/shard_map/psum | solution.py:61
  182.0 1.0 fusion.29
  182.9 0.8 copy.33
  184.1 0.3 squeeze.9
  184.4 0.7 fusion.2
  185.1 1.6 copy-done.1
  186.8 0.7 fusion
  187.6 0.3 squeeze.8
  188.0 2.9 %fusion.3 = f32[4,64,256]{2,1,0:T(8,128)S(1)} fusion(f32[4,784,256]{2,1,0:T(8,128)} %copy-done.1, f32[4,256]{1,0:T(4,128)S(1)} %max.10, pred[256,784]{0,1:T(8,128)(4,1)S(1)} %fusion.23, bf16[784,4,64]{2,1,0:T(4,128)(2,1)S(1)} %squeeze.8), kind=kOutput, calls=%fused_computation.5 | convolution fusion | flops 105971712 | bytes 4079616 | tf_op jit(solution)/shard_map/while/body/eval_jaxpr/hqk,khd->qhd/dot_general | solution.py:124
  190.9 0.3 fusion.8
  191.4 0.9 reshape.255
  (38 shorter events, 2.1 us)
Async XLA Ops:
  7.2 49.1 %copy-start.6 = (s32[8]{0:T(128)S(1)}, s32[8]{0:T(128)}, u32[]{:S(2)}) copy-start(s32[8]{0:T(128)} %param.8) | copy-start | bytes 100
  7.2 49.1 %copy-start.5 = (s32[8,16]{1,0:T(8,128)S(1)}, s32[8,16]{1,0:T(8,128)}, u32[]{:S(2)}) copy-start(s32[8,16]{1,0:T(8,128)} %param.9) | copy-start | bytes 1540
  7.2 49.5 %copy-start.3 = (bf16[16,16,256]{2,1,0:T(8,128)(2,1)S(1)}, bf16[16,16,256]{2,1,0:T(8,128)(2,1)}, u32[]{:S(2)}) copy-start(bf16[16,16,256]{2,1,0:T(8,128)(2,1)} %param.6) | copy-start | bytes 393220
  7.2 174.8 %all-reduce.2.cloned.1.call-start = ((), (), s32[]{:S(2)}) async-start(), calls=%async_computation | async-start | bytes 524288 | tf_op jit(solution)/shard_map/psum | solution.py:61
  8.3 90.7 %collective-permute-start = (bf16[2,16,6,256]{3,2,1,0:T(8,128)(2,1)S(1)}, bf16[2,16,6,256]{3,2,1,0:T(8,128)(2,1)S(1)}, u32[]{:S(2)}, u32[]{:S(2)}) collective-permute-start(bf16[2,16,6,256]{3,2,1,0:T(8,128)(2,1)S(1)} %get-tuple-element.36), channel_id=1, source_target_pairs={{0,4},{4,8},{8,12},{12,16},{16,20},{20,24},{24,28},{28,0},{1,5},{5... | collective-permute-start | bytes 294920 | tf_op jit(solution)/shard_map/ppermute | solution.py:21
  11.3 87.7 %collective-permute-start.1 = (bf16[2,16,6,256]{3,2,1,0:T(8,128)(2,1)S(1)}, bf16[2,16,6,256]{3,2,1,0:T(8,128)(2,1)S(1)}, u32[]{:S(2)}, u32[]{:S(2)}) collective-permute-start(bf16[2,16,6,256]{3,2,1,0:T(8,128)(2,1)S(1)} %get-tuple-element.37), channel_id=1, source_target_pairs={{4,0},{8,4},{12,8},{16,12},{20,16},{24,20},{28,24},{0,28},{5,1},{9... | collective-permute-start | bytes 294920 | tf_op jit(solution)/shard_map/ppermute | solution.py:22
  15.4 41.7 %copy-start.4 = (bf16[256,256]{1,0:T(8,128)(2,1)S(1)}, bf16[256,256]{1,0:T(8,128)(2,1)}, u32[]{:S(2)}) copy-start(bf16[256,256]{1,0:T(8,128)(2,1)} %param.11) | copy-start | bytes 393220
  16.9 82.2 %copy-start = (bf16[2,16,16,256]{3,2,1,0:T(8,128)(2,1)S(1)}, bf16[2,16,16,256]{3,2,1,0:T(8,128)(2,1)}, u32[]{:S(2)}) copy-start(bf16[2,16,16,256]{3,2,1,0:T(8,128)(2,1)} %param.7) | copy-start | bytes 786436
  99.2 84.5 %collective-permute-start.2 = (bf16[2,6,28,256]{3,2,1,0:T(8,128)(2,1)S(1)}, bf16[2,6,28,256]{3,2,1,0:T(8,128)(2,1)S(1)}, u32[]{:S(2)}, u32[]{:S(2)}) collective-permute-start(bf16[2,6,28,256]{3,2,1,0:T(8,128)(2,1)S(1)} %get-tuple-element.32), channel_id=1, source_target_pairs={{0,1},{1,2},{2,3},{3,0},{4,5},{5,6},{6,7},{7,4},{8,9},{9,10},{10,1... | collective-permute-start | bytes 516104 | tf_op jit(solution)/shard_map/ppermute | solution.py:21
  99.3 84.4 %collective-permute-start.3 = (bf16[2,6,28,256]{3,2,1,0:T(8,128)(2,1)S(1)}, bf16[2,6,28,256]{3,2,1,0:T(8,128)(2,1)S(1)}, u32[]{:S(2)}, u32[]{:S(2)}) collective-permute-start(bf16[2,6,28,256]{3,2,1,0:T(8,128)(2,1)S(1)} %get-tuple-element.33), channel_id=1, source_target_pairs={{1,0},{2,1},{3,2},{0,3},{5,4},{6,5},{7,6},{4,7},{9,8},{10,9},{11,1... | collective-permute-start | bytes 516104 | tf_op jit(solution)/shard_map/ppermute | solution.py:22
  185.1 1.7 copy-start.1
  187.6 3.3 %copy-start.2 = (f32[256,256]{0,1:T(8,128)S(1)}, f32[256,256]{0,1:T(8,128)}, u32[]{:S(2)}) copy-start(f32[256,256]{0,1:T(8,128)} %all-reduce.2.cloned.1.call-done) | copy-start | bytes 786436
Sparse Core Ops, SparseCore 0:
  56.2 125.7 all-reduce.1
where the time goes:
time: 200 us; the launch traced here: 199 us
  waiting for transfers between devices  80.2 us (40%)
  blocking collectives  79.5 us (40%)
  between operations  14.3 us (7%)
  local copies, waits for them, and re-layouts  8.11 us (4%)
  starting transfers between devices  7.96 us (4%)
  matrix products  5.79 us (3%)
  other arithmetic  3.24 us (2%)
    psum x1, waiting for transfers between devices, register_values(): lax.psum((weight_sums, weighted), ('lon', 'lat'))  80.2 us
    psum x1, blocking collectives, register_values(): lax.psum((weight_sums, weighted), ('lon', 'lat'))  41.5 us
    pmax x1, blocking collectives, register_values(): highest = lax.pmax(jnp.max(scores, axis=2), ('lon', 'lat'))  38 us
    ppermute x2, starting transfers between devices, extended_2(): after = lax.ppermute(leading, axis, down)  4.85 us
  transfers between devices with their start and end apart: 5, of which 1 were waited for; matrix products, arithmetic and copies ran while one was open for 4% of the time, Pallas kernels for 0%

commit v1 on v0

v1 whole, which is shorter than its diff:
```python
import functools

import jax
import jax.numpy as jnp
from jax import lax
from jax.experimental import pallas as pl
from jax.experimental.pallas import tpu as pltpu
from jax.sharding import PartitionSpec as P

HEADS = 4
HEAD_DIM = 64
NREG = 256
RADIUS = 6
TILE = 8
PAIR = 2 * HEAD_DIM
SIDE = 8
STATS = 16
AUG = 128
MASKED = -8192.0
SCALE = HEAD_DIM ** (-0.5)

BF16 = jnp.bfloat16
F32 = jnp.float32
NT = (((1,), (1,)), ((), ()))
TN = (((0,), (0,)), ((), ()))
VMEM = pl.BlockSpec(memory_space=pltpu.VMEM)
SMEM = pl.BlockSpec(memory_space=pltpu.SMEM)


def dot(a, b, dims):
    return lax.dot_general(a, b, dims, preferred_element_type=F32)


def iota(shape, axis):
    return lax.broadcasted_iota(jnp.int32, shape, axis)


def call(kernel, out, args, specs, scratch=(), flops=0, limit=16):
    size = sum(a.size * a.dtype.itemsize for a in args)
    return pl.pallas_call(
        kernel,
        out_shape=out,
        in_specs=specs,
        out_specs=jax.tree.map(lambda _: VMEM, out),
        scratch_shapes=scratch,
        compiler_params=pltpu.CompilerParams(vmem_limit_bytes=limit * 2**20),
        cost_estimate=pl.CostEstimate(flops=flops, bytes_accessed=size, transcendentals=0),
    )(*args)


def pack(values, tops, sums, out_ref):
    rows = iota((STATS, values.shape[1]), 0)
    stats = jnp.zeros((STATS, values.shape[1]), F32)
    for j in range(2):
        high = sums[j].astype(BF16).astype(F32)
        for row, value in ((j, tops[j]), (2 + 2 * j, high), (3 + 2 * j, sums[j] - high)):
            stats = jnp.where(rows == row, value, stats)
    out_ref[:PAIR] = values.astype(BF16)
    out_ref[PAIR:] = stats.astype(BF16)


def register_kernel(place, own, other, queries, out_ref):
    lanes = pl.ds(pl.multiple_of(place[0] * PAIR, PAIR), PAIR)
    keys = jnp.concatenate([own[0, :, lanes], other[0, :, lanes]], axis=0)
    vals = jnp.concatenate([own[1, :, lanes], other[1, :, lanes]], axis=0)
    scaled = queries[:, lanes] * jnp.asarray(SCALE, BF16)
    first = iota(scaled.shape, 1) < HEAD_DIM
    parts, tops, sums = [], [], []
    for j in range(2):
        mine = jnp.where(first == (j == 0), scaled, jnp.zeros_like(scaled))
        scores = dot(keys, mine, NT)
        top = jnp.max(scores, axis=0, keepdims=True).astype(BF16).astype(F32)
        weights = jnp.exp(scores - top)
        sums.append(jnp.sum(weights, axis=0, keepdims=True))
        tops.append(top)
        parts.append(dot(vals, weights.astype(BF16), TN))
    upper = iota(parts[0].shape, 0) < HEAD_DIM
    pack(jnp.where(upper, parts[0], parts[1]), tops, sums, out_ref)


def merge_kernel(bits, last, place, *refs):
    payloads, out_ref = refs[:-1], refs[-1]
    found = [(r[:PAIR].astype(F32), r[PAIR:].astype(F32)) for r in payloads]
    for level, bit in enumerate(bits):
        swap = place[1 + bit] == 1
        step = 1 << level
        for low in range(len(found)):
            if not low & step:
                a, b = found[low], found[low + step]
                found[low] = tuple(jnp.where(swap, v, u) for u, v in zip(a, b))
                found[low + step] = tuple(jnp.where(swap, u, v) for u, v in zip(a, b))
    upper = iota((PAIR, found[0][0].shape[1]), 0) < HEAD_DIM
    tops, sums, factors = [], [], []
    for j in range(2):
        each = [stats[j : j + 1] for _, stats in found]
        top = functools.reduce(jnp.maximum, each)
        factor = [jnp.exp(e - top) for e in each]
        totals = [
            f * (stats[2 + 2 * j : 3 + 2 * j] + stats[3 + 2 * j : 4 + 2 * j])
            for f, (_, stats) in zip(factor, found)
        ]
        tops.append(top)
        sums.append(functools.reduce(jnp.add, totals))
        factors.append(factor)
    merged = functools.reduce(
        jnp.add,
        [values * jnp.where(upper, f, g) for f, g, (values, _) in zip(*factors, found)],
    )
    if last:
        out_ref[...] = (merged / jnp.where(upper, sums[0], sums[1])).astype(BF16)
    else:
        pack(merged, tops, sums, out_ref)


def segments(rows, cols):
    return (
        (rows * cols, cols, 0, 0),
        (RADIUS * cols, cols, "core", 0),
        (rows * SIDE, SIDE, 0, "a"),
        (rows * SIDE, SIDE, 0, "b"),
        (RADIUS * SIDE, SIDE, "core", "a"),
        (RADIUS * SIDE, SIDE, "core", "b"),
        (RADIUS * cols, cols, "cross", 0),
        (RADIUS * SIDE, SIDE, "cross", "a"),
        (RADIUS * SIDE, SIDE, "cross", "b"),
    )


def mask_kernel(rows, cols, nbits, place, pole, sea, out_ref):
    lat, lon = place[1 + nbits], place[2 + nbits]
    lat_odd, lon_odd = lat % 2, lon % 2
    starts = {
        0: 0,
        "core": jnp.where(lat_odd == 0, rows, -RADIUS),
        "cross": jnp.where(lat_odd == 0, -RADIUS, rows),
        "a": jnp.where(lon_odd == 0, cols, -SIDE),
        "b": jnp.where(lon_odd == 0, -SIDE, cols),
    }
    bands, tiles = sea.shape
    down, across = rows // TILE, cols // TILE
    lane = iota((1, AUG), 1)
    closed = jnp.zeros((1, AUG), F32)
    for i in range(down + 2):
        band = lat * down - 1 + i
        inside = (band >= 0) & (band < bands)
        band = jnp.clip(band, 0, bands - 1)
        for j in range(across + 2):
            tile = (lon * across - 1 + j + tiles) % tiles
            open_ = inside & (pole[band] * sea[band, tile] > 0)
            at = rows + cols + i * (across + 2) + j
            closed = jnp.where(lane == at, jnp.where(open_, 0.0, MASKED), closed)
    offset = 0
    for count, width, down_name, across_name in segments(rows, cols):
        index = iota((count, AUG), 0)
        row = starts[down_name] + index // width
        col = starts[across_name] + index % width
        lanes = iota((count, AUG), 1)
        apart = jnp.where(lanes < rows, lanes - row, lanes - rows - col)
        far = (lanes < rows + cols) & (jnp.abs(apart) > RADIUS)
        cell = ((row + TILE) // TILE) * (across + 2) + (col + TILE) // TILE
        value = jnp.where(lanes - (rows + cols) == cell, closed, 0.0)
        out_ref[offset : offset + count] = jnp.where(far, MASKED, value).astype(BF16)
        offset += count


def near_kernel(rows, cols, nbits, place, q_ref, own, core, a, b, corner, cross, mask, reg_keys,
                acc_ref, scale_ref, reg_ref, kbuf, vbuf):
    cells = mask.shape[0]
    lat = place[1 + nbits]
    taken = pl.ds(pl.multiple_of(jnp.where(lat % 2 == 0, 0, (rows - RADIUS) * cols), 16), RADIUS * cols)
    offset = 0
    for ref, index in ((own, slice(None)), (core, taken), (a, slice(None)), (b, slice(None)),
                       (corner, slice(None)), (cross, slice(None))):
        keys, vals = ref[0, index], ref[1, index]
        end = offset + keys.shape[0]
        for p in range(2):
            kbuf[p, offset:end, :PAIR] = keys[:, p * PAIR : (p + 1) * PAIR]
        vbuf[offset:end] = vals
        offset = end
    for p in range(2):
        kbuf[p, :cells, PAIR:] = mask[...]
        kbuf[p, cells:, :PAIR] = reg_keys[:, p * PAIR : (p + 1) * PAIR]
        kbuf[p, cells:, PAIR:] = jnp.zeros((NREG, AUG), BF16)
    count = rows * cols
    query = iota((count, AUG), 0)
    lane = iota((count, AUG), 1)
    tiles = (rows // TILE + 2) * (cols // TILE + 2)
    hot = (lane == query // cols) | (lane - rows == query % cols)
    hot = hot | ((lane >= rows + cols) & (lane < rows + cols + tiles))
    hot = jnp.where(hot, 1.0, 0.0).astype(BF16)
    first = iota((count, PAIR), 1) < HEAD_DIM
    for p in range(2):
        scaled = q_ref[:, p * PAIR : (p + 1) * PAIR] * jnp.asarray(SCALE, BF16)
        mixed, totals = [], []
        for j in range(2):
            mine = jnp.where(first == (j == 0), scaled, jnp.zeros_like(scaled))
            scores = dot(jnp.concatenate([mine, hot], axis=1), kbuf[p], NT)
            weights = jnp.exp(scores - jnp.max(scores, axis=1, keepdims=True))
            totals.append(jnp.sum(weights, axis=1, keepdims=True))
            rounded = weights.astype(BF16)
            reg_ref[2 * p + j] = rounded[:, cells:]
            mixed.append(
                jnp.dot(rounded[:, :cells], vbuf[:, p * PAIR : (p + 1) * PAIR], preferred_element_type=F32)
            )
        acc_ref[:, p * PAIR : (p + 1) * PAIR] = jnp.where(first, *mixed)
        scale_ref[:, p * PAIR : (p + 1) * PAIR] = 1.0 / jnp.where(first, *totals)


def final_kernel(place, acc, scale, reg_weights, mine, other, out_ref, reg_out_ref):
    here = place[0] == 0
    first = iota((acc.shape[0], PAIR), 1) < HEAD_DIM
    for p in range(2):
        lanes = slice(p * PAIR, (p + 1) * PAIR)
        vals = jnp.where(here == (p == 0), mine[...], other[...])
        added = jnp.where(first, dot(reg_weights[2 * p], vals, NT), dot(reg_weights[2 * p + 1], vals, NT))
        out_ref[:, lanes] = ((acc[:, lanes] + added) * scale[:, lanes]).astype(BF16)
        reg_out_ref[:, lanes] = vals.astype(F32).T.astype(BF16)


def shards(queries, key_values, pole_mask, sea_mask, reg_queries, reg_keys):
    rows, cols, channels = queries.shape
    lats, lons = lax.axis_size("lat"), lax.axis_size("lon")
    devices = lats * lons
    assert lats == 4 and lons & (lons - 1) == 0 and lons > 1
    nbits = devices.bit_length() - 1
    lat, lon = lax.axis_index("lat"), lax.axis_index("lon")
    flat = lon * lats + lat
    bits = [(flat >> b) & 1 for b in range(nbits)]
    half = functools.reduce(jnp.bitwise_xor, bits)
    place = jnp.stack([half, *bits, lat, lon]).astype(jnp.int32)
    everyone = ("lon", "lat")

    def swap(x, mask):
        return lax.ppermute(x, everyone, [(i, i ^ mask) for i in range(devices)])

    cells = rows * cols
    own = key_values.reshape(2, cells, channels)
    core = swap(own, 1)

    near_cols = lax.dynamic_slice_in_dim(key_values, (1 - lon % 2) * (cols - SIDE), SIDE, 2)
    far_cols = lax.dynamic_slice_in_dim(key_values, (lon % 2) * (cols - SIDE), SIDE, 2)
    side_a = swap(near_cols, lats)
    side_b = lax.ppermute(
        far_cols, "lon", [(i, (i + 1 if i % 2 else i - 1) % lons) for i in range(lons)]
    )

    payload = call(
        register_kernel,
        jax.ShapeDtypeStruct((PAIR + STATS, NREG), BF16),
        (place, own, core, reg_queries),
        [SMEM, VMEM, VMEM, VMEM],
        flops=4 * 2 * cells * NREG * 2 * PAIR,
    )

    core_first = (1 - lat % 2) * (rows - RADIUS)
    cross_first = (lat % 2) * (rows - RADIUS)

    def edge(shard, start):
        taken = lax.dynamic_slice_in_dim(shard, start, RADIUS, 1)
        return taken.reshape(2, RADIUS * shard.shape[2], channels)

    corner = swap(jnp.concatenate([edge(side_a, core_first), edge(side_b, core_first)], axis=1), 1)
    cross = swap(
        jnp.concatenate(
            [edge(key_values, cross_first), edge(side_a, cross_first), edge(side_b, cross_first)], axis=1
        ),
        3,
    )

    mask = call(
        functools.partial(mask_kernel, rows, cols, nbits),
        jax.ShapeDtypeStruct((sum(s[0] for s in segments(rows, cols)), AUG), BF16),
        (place, pole_mask, sea_mask),
        [SMEM, SMEM, SMEM],
    )

    stages = [tuple(range(b, min(b + 2, nbits))) for b in range(1, nbits, 2)]
    for stage in stages:
        gathered = [payload]
        for chosen in range(1, 1 << len(stage)):
            flips = [b for k, b in enumerate(stage) if chosen >> k & 1]
            gathered.append(swap(payload, sum(1 << b for b in flips) + len(flips) % 2))
        last = stage is stages[-1]
        payload = call(
            functools.partial(merge_kernel, stage, last),
            jax.ShapeDtypeStruct((PAIR if last else PAIR + STATS, NREG), BF16),
            (place, *gathered),
            [SMEM] + [VMEM] * len(gathered),
        )

    square = jax.ShapeDtypeStruct((cells, channels), F32)
    acc, scale, reg_weights = call(
        functools.partial(near_kernel, rows, cols, nbits),
        (square, square, jax.ShapeDtypeStruct((HEADS, cells, NREG), BF16)),
        (
            place,
            queries.reshape(cells, channels),
            own,
            core,
            side_a.reshape(2, rows * SIDE, channels),
            side_b.reshape(2, rows * SIDE, channels),
            corner,
            cross,
            mask,
            reg_keys,
        ),
        [SMEM] + [VMEM] * 9,
        scratch=[
            pltpu.VMEM((2, mask.shape[0] + NREG, PAIR + AUG), BF16),
            pltpu.VMEM((mask.shape[0], channels), BF16),
        ],
        flops=2 * 2 * cells * mask.shape[0] * channels * 2,
        limit=32,
    )
    other = swap(payload, 1)
    attended, reg_out = call(
        final_kernel,
        (
            jax.ShapeDtypeStruct((cells, channels), BF16),
            jax.ShapeDtypeStruct((NREG, channels), BF16),
        ),
        (place, acc, scale, reg_weights, payload, other),
        [SMEM] + [VMEM] * 5,
        flops=2 * cells * NREG * channels * 2,
    )
    return attended.reshape(rows, cols, channels), reg_out


def solution(mesh):
    return jax.shard_map(
        shards,
        mesh=mesh,
        in_specs=(P("lat", "lon", None), P(None, "lat", "lon", None), P(), P(), P(), P()),
        out_specs=(P("lat", "lon", None), P()),
        check_vma=False,
    )
```

time: 200 us -> 41 us (0.20)
  blocking collectives: 79.5 us -> 0 us
  waiting for transfers between devices: 80.2 us -> 15.2 us
  between operations: 14.3 us -> 0.85 us
  Pallas kernels: 0 us -> 8.46 us
  starting transfers between devices: 7.96 us -> 15.2 us
  local copies, waits for them, and re-layouts: 8.11 us -> 1.18 us
  matrix products: 5.79 us -> 0 us
  other arithmetic: 3.24 us -> 0.02 us
    psum x1 -> x0, waiting for transfers between devices: 80.2 us -> none  [register_values(): lax.psum((weight_sums, weighted), ('lon', 'lat'))]
    psum x1 -> x0, blocking collectives: 41.5 us -> none  [register_values(): lax.psum((weight_sums, weighted), ('lon', 'lat'))]
    pmax x1 -> x0, blocking collectives: 38 us -> none  [register_values(): highest = lax.pmax(jnp.max(scores, axis=2), ('lon', 'lat'))]
    ppermute x4 -> x12, waiting for transfers between devices: 0.01 us -> 15.2 us  [the longest x11 11.8 us: swap(): return lax.ppermute(x, everyone, [(i, i ^ mask) for i in range(devices)])]
    pallas_call x0 -> x6, Pallas kernels: none -> 8.46 us  [call(): pl.pallas_call(kernel, out_shape=out, in_specs=specs, out_specs=jax.tree....]
    ppermute x4 -> x12, starting transfers between devices: 7.93 us -> 15.2 us  [the longest x11 9.08 us: swap(): return lax.ppermute(x, everyone, [(i, i ^ mask) for i in range(devices)])]
    dot_general x7 -> x0, matrix products: 5.79 us -> none  [the longest x1 2.9 us: one_block(): jnp.einsum('hqk,khd->qhd', near_weights.astype(jnp.bfloat16), block_value...]
    unnamed x17 -> x12, local copies, waits for them, and re-layouts: 3.54 us -> 0.03 us
  transfers between devices with their start and end apart: 5 -> 12, of which waited for: 1 -> 7; matrix products, arithmetic and copies ran while one was open for 4% -> 0% of each run, Pallas kernels for 0% -> 17%
where the time goes in v1:
time: 41 us; the launch traced here: 40.9 us
  starting transfers between devices  15.2 us (37%)
  waiting for transfers between devices  15.2 us (37%)
  Pallas kernels  8.46 us (21%)
  local copies, waits for them, and re-layouts  1.18 us (3%)
  between operations  0.85 us (2%)
    ppermute x11, waiting for transfers between devices, swap(): return lax.ppermute(x, everyone, [(i, i ^ mask) for i in range(devices)])  11.8 us
    ppermute x11, starting transfers between devices, swap(): return lax.ppermute(x, everyone, [(i, i ^ mask) for i in range(devices)])  9.08 us
    pallas_call x6, Pallas kernels, call(): pl.pallas_call(kernel, out_shape=out, in_specs=specs, out_specs=jax.tree....  8.46 us
    ppermute x1, starting transfers between devices, shards(): lax.ppermute(far_cols, 'lon', [(i, (i + 1 if i % 2 else i - 1) % lons) fo...  6.07 us
    ppermute x1, waiting for transfers between devices, shards(): lax.ppermute(far_cols, 'lon', [(i, (i + 1 if i % 2 else i - 1) % lons) fo...  3.37 us
    dynamic_slice x1, local copies, waits for them, and re-layouts, shards(): lax.dynamic_slice_in_dim(key_values, lon % 2 * (cols - SIDE), SIDE, 2)  1.03 us
  transfers between devices with their start and end apart: 12, of which 7 were waited for; matrix products, arithmetic and copies ran while one was open for 0% of the time, Pallas kernels for 17%

profile of v1, /device:TPU:0, one launch (start us, length us, event | category | flops | bytes accessed | tf_op | source)
XLA Modules:
  0.0 40.9 jit_solution(14878022397405404013)
XLA Ops:
  0.7 1.0 %constant_dynamic-slice_fusion.1 = (bf16[2,16,8,256]{3,2,1,0:T(8,128)(2,1)S(1)}, bf16[2,16,8,256]{3,2,1,0:T(8,128)(2,1)S(1)}) fusion(bf16[2,16,16,256]{3,2,1,0:T(8,128)(2,1)} %param.7, s32[]{:T(128)S(6)} %select_n.32, s32[]{:T(128)S(6)} %select_n.31), kind=kLoop, calls=%fused_computation.7 | loop fusion | bytes 524296 | tf_op jit(solution)/shard_map/dynamic_slice | solution.py:241
  1.7 6.1 %collective-permute-start.2 = (bf16[2,16,8,256]{3,2,1,0:T(8,128)(2,1)S(1)}, bf16[2,16,8,256]{3,2,1,0:T(8,128)(2,1)S(1)}, u32[]{:S(2)}, u32[]{:S(2)}) collective-permute-start(bf16[2,16,8,256]{3,2,1,0:T(8,128)(2,1)S(1)} %get-tuple-element.12), channel_id=1, source_target_pairs={{0,28},{4,8},{8,4},{12,16},{16,12},{20,24},{24,20},{28,0},{1,29},{... | collective-permute-start | bytes 393224 | tf_op jit(solution)/shard_map/ppermute | solution.py:243
  7.8 0.1 stack.35.place
  7.9 3.4 %collective-permute-done.2 = bf16[2,16,8,256]{3,2,1,0:T(8,128)(2,1)S(1)} collective-permute-done((bf16[2,16,8,256]{3,2,1,0:T(8,128)(2,1)S(1)}, bf16[2,16,8,256]{3,2,1,0:T(8,128)(2,1)S(1)}, u32[]{:S(2)}, u32[]{:S(2)}) %collective-permute-start.2) | collective-permute-done | bytes 131104 | tf_op jit(solution)/shard_map/ppermute | solution.py:243
  11.3 2.8 %collective-permute-done.1 = bf16[2,16,8,256]{3,2,1,0:T(8,128)(2,1)S(1)} collective-permute-done((bf16[2,16,8,256]{3,2,1,0:T(8,128)(2,1)S(1)}, bf16[2,16,8,256]{3,2,1,0:T(8,128)(2,1)S(1)}, u32[]{:S(2)}, u32[]{:S(2)}) %collective-permute-start.1) | collective-permute-done | bytes 131104 | tf_op jit(solution)/shard_map/ppermute | solution.py:234
  14.1 1.2 %collective-permute-start.4 = (bf16[2,192,256]{2,1,0:T(8,128)(2,1)S(1)}, bf16[2,192,256]{2,1,0:T(8,128)(2,1)S(1)}, u32[]{:S(2)}, u32[]{:S(2)}) collective-permute-start(bf16[2,192,256]{2,1,0:T(8,128)(2,1)S(1)} %pad_maximum_fusion), channel_id=1, source_target_pairs={{0,3},{1,2},{2,1},{3,0},{4,7},{5,6},{6,5},{7,4},{8,11},{9,10},{10,... | collective-permute-start | bytes 589832 | tf_op jit(solution)/shard_map/ppermute | solution.py:234
  15.3 1.5 %shard_map.79.refs_0_ = bf16[144,256]{1,0:T(8,128)(2,1)S(1)} custom-call(s32[8]{0:T(128)S(1)} %stack.35.place, bf16[2,256,256]{2,1,0:T(8,128)(2,1)S(1)} %bitcast.23, bf16[2,256,256]{2,1,0:T(8,128)(2,1)S(1)} %collective-permute-done.core.other, bf16[256,256]{1,0:T(8,128)(2,1)S(1)} %copy-done.1), custom_call_target="tpu_custom_call" | custom-call | flops 134217728 | bytes 655392 | tf_op jit(solution)/shard_map/pallas_call | solution.py:40
  16.9 0.9 %collective-permute-start.5 = (bf16[144,256]{1,0:T(8,128)(2,1)S(1)}, bf16[144,256]{1,0:T(8,128)(2,1)S(1)}, u32[]{:S(2)}, u32[]{:S(2)}) collective-permute-start(bf16[144,256]{1,0:T(8,128)(2,1)S(1)} %shard_map.79.refs_0_), channel_id=1, source_target_pairs={{0,3},{1,2},{2,1},{3,0},{4,7},{5,6},{6,5},{7,4},{8,11},{9,10},{10,... | collective-permute-start | bytes 221192 | tf_op jit(solution)/shard_map/ppermute | solution.py:234
  17.7 2.4 %collective-permute-start.7 = (bf16[144,256]{1,0:T(8,128)(2,1)S(1)}, bf16[144,256]{1,0:T(8,128)(2,1)S(1)}, u32[]{:S(2)}, u32[]{:S(2)}) collective-permute-start(bf16[144,256]{1,0:T(8,128)(2,1)S(1)} %shard_map.79.refs_0_), channel_id=1, source_target_pairs={{0,6},{1,7},{2,4},{3,5},{4,2},{5,3},{6,0},{7,1},{8,14},{9,15},{10,... | collective-permute-start | bytes 221192 | tf_op jit(solution)/shard_map/ppermute | solution.py:234
  20.1 0.3 collective-permute-start.3
  20.4 2.4 %collective-permute-done.5.refs_1_ = bf16[144,256]{1,0:T(8,128)(2,1)S(1)} collective-permute-done((bf16[144,256]{1,0:T(8,128)(2,1)S(1)}, bf16[144,256]{1,0:T(8,128)(2,1)S(1)}, u32[]{:S(2)}, u32[]{:S(2)}) %collective-permute-start.5) | collective-permute-done | bytes 73760 | tf_op jit(solution)/shard_map/ppermute | solution.py:234
  22.7 1.1 %collective-permute-done.7.refs_3_ = bf16[144,256]{1,0:T(8,128)(2,1)S(1)} collective-permute-done((bf16[144,256]{1,0:T(8,128)(2,1)S(1)}, bf16[144,256]{1,0:T(8,128)(2,1)S(1)}, u32[]{:S(2)}, u32[]{:S(2)}) %collective-permute-start.7) | collective-permute-done | bytes 73760 | tf_op jit(solution)/shard_map/ppermute | solution.py:234
  23.9 0.7 %shard_map.80.refs_0_ = bf16[144,256]{1,0:T(8,128)(2,1)S(1)} custom-call(s32[8]{0:T(128)S(1)} %stack.35.place, bf16[144,256]{1,0:T(8,128)(2,1)S(1)} %shard_map.79.refs_0_, bf16[144,256]{1,0:T(8,128)(2,1)S(1)} %collective-permute-done.5.refs_1_, bf16[144,256]{1,0:T(8,128)(2,1)S(1)} %collective-permute-done.6.refs_2_, ...), custom_call_target="tpu_custom_call" | custom-call | bytes 294944 | tf_op jit(solution)/shard_map/pallas_call | solution.py:40
  24.6 0.8 %collective-permute-start.8 = (bf16[144,256]{1,0:T(8,128)(2,1)S(1)}, bf16[144,256]{1,0:T(8,128)(2,1)S(1)}, u32[]{:S(2)}, u32[]{:S(2)}) collective-permute-start(bf16[144,256]{1,0:T(8,128)(2,1)S(1)} %shard_map.80.refs_0_), channel_id=1, source_target_pairs={{0,9},{1,8},{2,11},{3,10},{4,13},{5,12},{6,15},{7,14},{8,1},{9,0},... | collective-permute-start | bytes 221192 | tf_op jit(solution)/shard_map/ppermute | solution.py:234
  25.4 2.8 %collective-permute-start.9 = (bf16[144,256]{1,0:T(8,128)(2,1)S(1)}, bf16[144,256]{1,0:T(8,128)(2,1)S(1)}, u32[]{:S(2)}, u32[]{:S(2)}) collective-permute-start(bf16[144,256]{1,0:T(8,128)(2,1)S(1)} %shard_map.80.refs_0_), channel_id=1, source_target_pairs={{0,17},{1,16},{2,19},{3,18},{4,21},{5,20},{6,23},{7,22},{8,25},{9,... | collective-permute-start | bytes 221192 | tf_op jit(solution)/shard_map/ppermute | solution.py:234
  28.2 0.6 %collective-permute-start.10 = (bf16[144,256]{1,0:T(8,128)(2,1)S(1)}, bf16[144,256]{1,0:T(8,128)(2,1)S(1)}, u32[]{:S(2)}, u32[]{:S(2)}) collective-permute-start(bf16[144,256]{1,0:T(8,128)(2,1)S(1)} %shard_map.80.refs_0_), channel_id=1, source_target_pairs={{0,24},{1,25},{2,26},{3,27},{4,28},{5,29},{6,30},{7,31},{8,16},{9,... | collective-permute-start | bytes 221192 | tf_op jit(solution)/shard_map/ppermute | solution.py:234
  28.7 0.3 collective-permute-done.8.refs_1_
  29.0 1.8 %collective-permute-done.9.refs_2_ = bf16[144,256]{1,0:T(8,128)(2,1)S(1)} collective-permute-done((bf16[144,256]{1,0:T(8,128)(2,1)S(1)}, bf16[144,256]{1,0:T(8,128)(2,1)S(1)}, u32[]{:S(2)}, u32[]{:S(2)}) %collective-permute-start.9) | collective-permute-done | bytes 73760 | tf_op jit(solution)/shard_map/ppermute | solution.py:234
  30.8 3.5 %collective-permute-done.10.refs_3_ = bf16[144,256]{1,0:T(8,128)(2,1)S(1)} collective-permute-done((bf16[144,256]{1,0:T(8,128)(2,1)S(1)}, bf16[144,256]{1,0:T(8,128)(2,1)S(1)}, u32[]{:S(2)}, u32[]{:S(2)}) %collective-permute-start.10) | collective-permute-done | bytes 73760 | tf_op jit(solution)/shard_map/ppermute | solution.py:234
  34.3 0.7 %shard_map.81.mine = bf16[128,256]{1,0:T(8,128)(2,1)S(1)} custom-call(s32[8]{0:T(128)S(1)} %stack.35.place, bf16[144,256]{1,0:T(8,128)(2,1)S(1)} %shard_map.80.refs_0_, bf16[144,256]{1,0:T(8,128)(2,1)S(1)} %collective-permute-done.8.refs_1_, bf16[144,256]{1,0:T(8,128)(2,1)S(1)} %collective-permute-done.9.refs_2_, ...), custom_call_target="tpu_custom_call" | custom-call | bytes 294944 | tf_op jit(solution)/shard_map/pallas_call | solution.py:40
  35.0 0.2 collective-permute-start.11
  35.2 1.0 %shard_map.77.mask = bf16[896,128]{1,0:T(8,128)(2,1)S(1)} custom-call(s32[8]{0:T(128)S(1)} %stack.35.place, s32[8]{0:T(128)S(1)} %copy-done.3, s32[8,16]{1,0:T(8,128)S(1)} %copy-done.2), custom_call_target="tpu_custom_call" | custom-call | bytes 576 | tf_op jit(solution)/shard_map/pallas_call | solution.py:40
  36.3 3.1 %shard_map.78 = (f32[256,256]{1,0:T(8,128)S(1)}, f32[256,256]{1,0:T(8,128)S(1)}, bf16[4,256,256]{2,1,0:T(8,128)(2,1)S(1)}) custom-call(s32[8]{0:T(128)S(1)} %stack.35.place, bf16[256,256]{1,0:T(8,128)(2,1)S(1)} %bitcast.27, bf16[2,256,256]{2,1,0:T(8,128)(2,1)S(1)} %bitcast.24, bf16[2,256,256]{2,1,0:T(8,128)(2,1)S(1)} %collective-permute-done.core.other, ...), custom_call_target="tpu_custom_call" | custom-call | flops 469762048 | bytes 1572896 | tf_op jit(solution)/shard_map/pallas_call | solution.py:40
  39.4 1.5 %shard_map.82 = (bf16[256,256]{1,0:T(8,128)(2,1)}, bf16[256,256]{1,0:T(8,128)(2,1)}) custom-call(s32[8]{0:T(128)S(1)} %stack.35.place, f32[256,256]{1,0:T(8,128)S(1)} %get-tuple-element.7.acc, f32[256,256]{1,0:T(8,128)S(1)} %get-tuple-element.8.scale, bf16[4,256,256]{2,1,0:T(8,128)(2,1)S(1)} %get-tuple-element.9.reg_weights, ...), custom_call_target="tpu_custom_call" | custom-call | flops 67108864 | bytes 1179680 | tf_op jit(solution)/shard_map/pallas_call | solution.py:40
  (25 shorter events, 0.1 us)
Async XLA Ops:
  0.7 7.1 %copy-start = (bf16[2,16,16,256]{3,2,1,0:T(8,128)(2,1)S(1)}, bf16[2,16,16,256]{3,2,1,0:T(8,128)(2,1)}, u32[]{:S(2)}) copy-start(bf16[2,16,16,256]{3,2,1,0:T(8,128)(2,1)} %param.7) | copy-start | bytes 786436
  1.7 9.6 %collective-permute-start.2 = (bf16[2,16,8,256]{3,2,1,0:T(8,128)(2,1)S(1)}, bf16[2,16,8,256]{3,2,1,0:T(8,128)(2,1)S(1)}, u32[]{:S(2)}, u32[]{:S(2)}) collective-permute-start(bf16[2,16,8,256]{3,2,1,0:T(8,128)(2,1)S(1)} %get-tuple-element.12), channel_id=1, source_target_pairs={{0,28},{4,8},{8,4},{12,16},{16,12},{20,24},{24,20},{28,0},{1,29},{... | collective-permute-start | bytes 393224 | tf_op jit(solution)/shard_map/ppermute | solution.py:243
  7.8 7.6 %collective-permute-start = (bf16[2,256,256]{2,1,0:T(8,128)(2,1)S(1)}, bf16[2,256,256]{2,1,0:T(8,128)(2,1)S(1)}, u32[]{:S(2)}, u32[]{:S(2)}) collective-permute-start(bf16[2,256,256]{2,1,0:T(8,128)(2,1)S(1)} %bitcast.22), channel_id=1, source_target_pairs={{0,1},{1,0},{2,3},{3,2},{4,5},{5,4},{6,7},{7,6},{8,9},{9,8},{10,11... | collective-permute-start | bytes 786440 | tf_op jit(solution)/shard_map/ppermute | solution.py:234
  7.8 6.3 %collective-permute-start.1 = (bf16[2,16,8,256]{3,2,1,0:T(8,128)(2,1)S(1)}, bf16[2,16,8,256]{3,2,1,0:T(8,128)(2,1)S(1)}, u32[]{:S(2)}, u32[]{:S(2)}) collective-permute-start(bf16[2,16,8,256]{3,2,1,0:T(8,128)(2,1)S(1)} %get-tuple-element.13), channel_id=1, source_target_pairs={{0,4},{1,5},{2,6},{3,7},{4,0},{5,1},{6,2},{7,3},{8,12},{9,13},{10,... | collective-permute-start | bytes 393224 | tf_op jit(solution)/shard_map/ppermute | solution.py:234
  14.1 1.2 %copy-start.1 = (bf16[256,256]{1,0:T(8,128)(2,1)S(1)}, bf16[256,256]{1,0:T(8,128)(2,1)}, u32[]{:S(2)}) copy-start(bf16[256,256]{1,0:T(8,128)(2,1)} %queries.1) | copy-start | bytes 393220
  14.1 22.1 %collective-permute-start.4 = (bf16[2,192,256]{2,1,0:T(8,128)(2,1)S(1)}, bf16[2,192,256]{2,1,0:T(8,128)(2,1)S(1)}, u32[]{:S(2)}, u32[]{:S(2)}) collective-permute-start(bf16[2,192,256]{2,1,0:T(8,128)(2,1)S(1)} %pad_maximum_fusion), channel_id=1, source_target_pairs={{0,3},{1,2},{2,1},{3,0},{4,7},{5,6},{6,5},{7,4},{8,11},{9,10},{10,... | collective-permute-start | bytes 589832 | tf_op jit(solution)/shard_map/ppermute | solution.py:234
  16.9 5.9 %collective-permute-start.5 = (bf16[144,256]{1,0:T(8,128)(2,1)S(1)}, bf16[144,256]{1,0:T(8,128)(2,1)S(1)}, u32[]{:S(2)}, u32[]{:S(2)}) collective-permute-start(bf16[144,256]{1,0:T(8,128)(2,1)S(1)} %shard_map.79.refs_0_), channel_id=1, source_target_pairs={{0,3},{1,2},{2,1},{3,0},{4,7},{5,6},{6,5},{7,4},{8,11},{9,10},{10,... | collective-permute-start | bytes 221192 | tf_op jit(solution)/shard_map/ppermute | solution.py:234
  17.7 5.0 %collective-permute-start.6 = (bf16[144,256]{1,0:T(8,128)(2,1)S(1)}, bf16[144,256]{1,0:T(8,128)(2,1)S(1)}, u32[]{:S(2)}, u32[]{:S(2)}) collective-permute-start(bf16[144,256]{1,0:T(8,128)(2,1)S(1)} %shard_map.79.refs_0_), channel_id=1, source_target_pairs={{0,5},{1,4},{2,7},{3,6},{4,1},{5,0},{6,3},{7,2},{8,13},{9,12},{10,... | collective-permute-start | bytes 221192 | tf_op jit(solution)/shard_map/ppermute | solution.py:234
  17.7 6.2 %collective-permute-start.7 = (bf16[144,256]{1,0:T(8,128)(2,1)S(1)}, bf16[144,256]{1,0:T(8,128)(2,1)S(1)}, u32[]{:S(2)}, u32[]{:S(2)}) collective-permute-start(bf16[144,256]{1,0:T(8,128)(2,1)S(1)} %shard_map.79.refs_0_), channel_id=1, source_target_pairs={{0,6},{1,7},{2,4},{3,5},{4,2},{5,3},{6,0},{7,1},{8,14},{9,15},{10,... | collective-permute-start | bytes 221192 | tf_op jit(solution)/shard_map/ppermute | solution.py:234
  20.1 16.1 %collective-permute-start.3 = (bf16[2,96,256]{2,1,0:T(8,128)(2,1)S(1)}, bf16[2,96,256]{2,1,0:T(8,128)(2,1)S(1)}, u32[]{:S(2)}, u32[]{:S(2)}) collective-permute-start(bf16[2,96,256]{2,1,0:T(8,128)(2,1)S(1)} %pad_maximum_fusion.1), channel_id=1, source_target_pairs={{0,1},{1,0},{2,3},{3,2},{4,5},{5,4},{6,7},{7,6},{8,9},{9,8},{10,11... | collective-permute-start | bytes 294920 | tf_op jit(solution)/shard_map/ppermute | solution.py:234
  24.5 10.6 %copy-start.2 = (s32[8,16]{1,0:T(8,128)S(1)}, s32[8,16]{1,0:T(8,128)}, u32[]{:S(2)}) copy-start(s32[8,16]{1,0:T(8,128)} %sea.1) | copy-start | bytes 1540
  24.5 10.6 %copy-start.3 = (s32[8]{0:T(128)S(1)}, s32[8]{0:T(128)}, u32[]{:S(2)}) copy-start(s32[8]{0:T(128)} %pole.1) | copy-start | bytes 100
  24.6 4.4 %collective-permute-start.8 = (bf16[144,256]{1,0:T(8,128)(2,1)S(1)}, bf16[144,256]{1,0:T(8,128)(2,1)S(1)}, u32[]{:S(2)}, u32[]{:S(2)}) collective-permute-start(bf16[144,256]{1,0:T(8,128)(2,1)S(1)} %shard_map.80.refs_0_), channel_id=1, source_target_pairs={{0,9},{1,8},{2,11},{3,10},{4,13},{5,12},{6,15},{7,14},{8,1},{9,0},... | collective-permute-start | bytes 221192 | tf_op jit(solution)/shard_map/ppermute | solution.py:234
  25.4 5.4 %collective-permute-start.9 = (bf16[144,256]{1,0:T(8,128)(2,1)S(1)}, bf16[144,256]{1,0:T(8,128)(2,1)S(1)}, u32[]{:S(2)}, u32[]{:S(2)}) collective-permute-start(bf16[144,256]{1,0:T(8,128)(2,1)S(1)} %shard_map.80.refs_0_), channel_id=1, source_target_pairs={{0,17},{1,16},{2,19},{3,18},{4,21},{5,20},{6,23},{7,22},{8,25},{9,... | collective-permute-start | bytes 221192 | tf_op jit(solution)/shard_map/ppermute | solution.py:234
  28.2 6.2 %collective-permute-start.10 = (bf16[144,256]{1,0:T(8,128)(2,1)S(1)}, bf16[144,256]{1,0:T(8,128)(2,1)S(1)}, u32[]{:S(2)}, u32[]{:S(2)}) collective-permute-start(bf16[144,256]{1,0:T(8,128)(2,1)S(1)} %shard_map.80.refs_0_), channel_id=1, source_target_pairs={{0,24},{1,25},{2,26},{3,27},{4,28},{5,29},{6,30},{7,31},{8,16},{9,... | collective-permute-start | bytes 221192 | tf_op jit(solution)/shard_map/ppermute | solution.py:234
  34.3 1.9 %copy-start.5 = (bf16[256,256]{1,0:T(8,128)(2,1)S(1)}, bf16[256,256]{1,0:T(8,128)(2,1)}, u32[]{:S(2)}) copy-start(bf16[256,256]{1,0:T(8,128)(2,1)} %reg_keys.1) | copy-start | bytes 393220
  35.0 1.3 %copy-start.4 = (bf16[16,16,256]{2,1,0:T(8,128)(2,1)S(1)}, bf16[16,16,256]{2,1,0:T(8,128)(2,1)}, u32[]{:S(2)}) copy-start(bf16[16,16,256]{2,1,0:T(8,128)(2,1)} %param.6) | copy-start | bytes 393220
  35.0 4.4 %collective-permute-start.11 = (bf16[128,256]{1,0:T(8,128)(2,1)S(1)}, bf16[128,256]{1,0:T(8,128)(2,1)S(1)}, u32[]{:S(2)}, u32[]{:S(2)}) collective-permute-start(bf16[128,256]{1,0:T(8,128)(2,1)S(1)} %shard_map.81.mine), channel_id=1, source_target_pairs={{0,1},{1,0},{2,3},{3,2},{4,5},{5,4},{6,7},{7,6},{8,9},{9,8},{10,11... | collective-permute-start | bytes 196616 | tf_op jit(solution)/shard_map/ppermute | solution.py:234

commit v2 on v1

--- a/solution.py
+++ b/solution.py
@@ -252,6 +252,7 @@
         flops=4 * 2 * cells * NREG * 2 * PAIR,
     )
 
+    side_a, side_b, _ = lax.optimization_barrier((side_a, side_b, payload))
     core_first = (1 - lat % 2) * (rows - RADIUS)
     cross_first = (lat % 2) * (rows - RADIUS)
 
@@ -273,20 +274,6 @@
         (place, pole_mask, sea_mask),
         [SMEM, SMEM, SMEM],
     )
-
-    stages = [tuple(range(b, min(b + 2, nbits))) for b in range(1, nbits, 2)]
-    for stage in stages:
-        gathered = [payload]
-        for chosen in range(1, 1 << len(stage)):
-            flips = [b for k, b in enumerate(stage) if chosen >> k & 1]
-            gathered.append(swap(payload, sum(1 << b for b in flips) + len(flips) % 2))
-        last = stage is stages[-1]
-        payload = call(
-            functools.partial(merge_kernel, stage, last),
-            jax.ShapeDtypeStruct((PAIR if last else PAIR + STATS, NREG), BF16),
-            (place, *gathered),
-            [SMEM] + [VMEM] * len(gathered),
-        )
 
     square = jax.ShapeDtypeStruct((cells, channels), F32)
     acc, scale, reg_weights = call(
@@ -312,6 +299,26 @@
         flops=2 * 2 * cells * mask.shape[0] * channels * 2,
         limit=32,
     )
+    stages = [tuple(range(b, min(b + 2, nbits))) for b in range(1, nbits, 2)]
+    for stage in stages:
+        gathered = [payload]
+        for chosen in range(1, 1 << len(stage)):
+            flips = [b for k, b in enumerate(stage) if chosen >> k & 1]
+            gathered.append(swap(payload, sum(1 << b for b in flips) + len(flips) % 2))
+        last = stage is stages[-1]
+        if stage is stages[0]:
+            gathered[0], mask = lax.optimization_barrier((gathered[0], mask))
+        if last:
+            gathered[0], acc, scale, reg_weights = lax.optimization_barrier(
+                (gathered[0], acc, scale, reg_weights)
+            )
+        payload = call(
+            functools.partial(merge_kernel, stage, last),
+            jax.ShapeDtypeStruct((PAIR if last else PAIR + STATS, NREG), BF16),
+            (place, *gathered),
+            [SMEM] + [VMEM] * len(gathered),
+        )
+
     other = swap(payload, 1)
     attended, reg_out = call(
         final_kernel,

time: 41 us -> 31.5 us (0.77)
  waiting for transfers between devices: 15.2 us -> 2.92 us
  starting transfers between devices: 15.2 us -> 17.2 us
  local copies, waits for them, and re-layouts: 1.18 us -> 1.95 us
    ppermute x11, waiting for transfers between devices: 11.8 us -> 2.92 us  [swap(): return lax.ppermute(x, everyone, [(i, i ^ mask) for i in range(devices)])]
    ppermute x11, starting transfers between devices: 9.08 us -> 13.7 us  [swap(): return lax.ppermute(x, everyone, [(i, i ^ mask) for i in range(devices)])]
    ppermute x1, waiting for transfers between devices: 3.37 us -> 0.01 us  [shards(): lax.ppermute(far_cols, 'lon', [(i, (i + 1 if i % 2 else i - 1) % lons) fo...]
    ppermute x1, starting transfers between devices: 6.07 us -> 3.54 us  [shards(): lax.ppermute(far_cols, 'lon', [(i, (i + 1 if i % 2 else i - 1) % lons) fo...]
    unnamed x12, local copies, waits for them, and re-layouts: 0.03 us -> 0.81 us
  transfers between devices with their start and end apart: 12 -> 12, of which waited for: 7 -> 4; matrix products, arithmetic and copies ran while one was open for 0% -> 4% of each run, Pallas kernels for 17% -> 20%
where the time goes in v2:
time: 31.5 us; the launch traced here: 31.3 us
  starting transfers between devices  17.2 us (55%)
  Pallas kernels  8.44 us (27%)
  waiting for transfers between devices  2.92 us (9%)
  local copies, waits for them, and re-layouts  1.95 us (6%)
  between operations  0.76 us (2%)
    ppermute x11, starting transfers between devices, swap(): return lax.ppermute(x, everyone, [(i, i ^ mask) for i in range(devices)])  13.7 us
    pallas_call x6, Pallas kernels, call(): pl.pallas_call(kernel, out_shape=out, in_specs=specs, out_specs=jax.tree....  8.44 us
    ppermute x1, starting transfers between devices, shards(): lax.ppermute(far_cols, 'lon', [(i, (i + 1 if i % 2 else i - 1) % lons) fo...  3.54 us
    ppermute x11, waiting for transfers between devices, swap(): return lax.ppermute(x, everyone, [(i, i ^ mask) for i in range(devices)])  2.92 us
    dynamic_slice x1, local copies, waits for them, and re-layouts, shards(): lax.dynamic_slice_in_dim(key_values, lon % 2 * (cols - SIDE), SIDE, 2)  1.03 us
    unnamed x12, local copies, waits for them, and re-layouts  0.81 us
  transfers between devices with their start and end apart: 12, of which 4 were waited for; matrix products, arithmetic and copies ran while one was open for 4% of the time, Pallas kernels for 20%

profile of v2, /device:TPU:0, one launch (start us, length us, event | category | flops | bytes accessed | tf_op | source)
XLA Modules:
  0.0 31.3 jit_solution(1161572998406933236)
XLA Ops:
  0.6 0.5 %collective-permute-start = (bf16[2,256,256]{2,1,0:T(8,128)(2,1)}, bf16[2,256,256]{2,1,0:T(8,128)(2,1)S(1)}, u32[]{:S(2)}, u32[]{:S(2)}) collective-permute-start(bf16[2,256,256]{2,1,0:T(8,128)(2,1)} %bitcast.22), channel_id=1, source_target_pairs={{0,1},{1,0},{2,3},{3,2},{4,5},{5,4},{6,7},{7,6},{8,9},{9,8},{10,11... | collective-permute-start | bytes 786440 | tf_op jit(solution)/shard_map/ppermute | solution.py:234
  1.1 1.0 %constant_dynamic-slice_fusion.1 = (bf16[2,16,8,256]{3,2,1,0:T(8,128)(2,1)S(1)}, bf16[2,16,8,256]{3,2,1,0:T(8,128)(2,1)S(1)}) fusion(bf16[2,16,16,256]{3,2,1,0:T(8,128)(2,1)} %param.7, s32[]{:T(128)S(6)} %select_n.32, s32[]{:T(128)S(6)} %select_n.31), kind=kLoop, calls=%fused_computation.7 | loop fusion | bytes 524296 | tf_op jit(solution)/shard_map/dynamic_slice | solution.py:241
  2.2 2.6 %collective-permute-start.4 = (bf16[2,16,8,256]{3,2,1,0:T(8,128)(2,1)S(1)}, bf16[2,16,8,256]{3,2,1,0:T(8,128)(2,1)S(1)}, u32[]{:S(2)}, u32[]{:S(2)}) collective-permute-start(bf16[2,16,8,256]{3,2,1,0:T(8,128)(2,1)S(1)} %get-tuple-element.27), channel_id=1, source_target_pairs={{0,4},{1,5},{2,6},{3,7},{4,0},{5,1},{6,2},{7,3},{8,12},{9,13},{10,... | collective-permute-start | bytes 393224 | tf_op jit(solution)/shard_map/ppermute | solution.py:234
  4.8 3.5 %collective-permute-start.5 = (bf16[2,16,8,256]{3,2,1,0:T(8,128)(2,1)S(1)}, bf16[2,16,8,256]{3,2,1,0:T(8,128)(2,1)S(1)}, u32[]{:S(2)}, u32[]{:S(2)}) collective-permute-start(bf16[2,16,8,256]{3,2,1,0:T(8,128)(2,1)S(1)} %get-tuple-element.26), channel_id=1, source_target_pairs={{0,28},{4,8},{8,4},{12,16},{16,12},{20,24},{24,20},{28,0},{1,29},{... | collective-permute-start | bytes 393224 | tf_op jit(solution)/shard_map/ppermute | solution.py:243
  8.4 0.1 stack.35.place
  8.5 0.8 %copy-done.1 = bf16[256,256]{1,0:T(8,128)(2,1)S(1)} copy-done((bf16[256,256]{1,0:T(8,128)(2,1)S(1)}, bf16[256,256]{1,0:T(8,128)(2,1)}, u32[]{:S(2)}) %copy-start.1) | copy-done | bytes 131096
  9.3 1.5 %shard_map.77.refs_0_ = bf16[144,256]{1,0:T(8,128)(2,1)S(1)} custom-call(s32[8]{0:T(128)S(1)} %stack.35.place, bf16[2,256,256]{2,1,0:T(8,128)(2,1)S(1)} %bitcast.23, bf16[2,256,256]{2,1,0:T(8,128)(2,1)S(1)} %collective-permute-done.other.core, bf16[256,256]{1,0:T(8,128)(2,1)S(1)} %copy-done.1), custom_call_target="tpu_custom_call" | custom-call | flops 134217728 | bytes 655392 | tf_op jit(solution)/shard_map/pallas_call | solution.py:40
  10.8 1.1 %collective-permute-start.1 = (bf16[144,256]{1,0:T(8,128)(2,1)S(1)}, bf16[144,256]{1,0:T(8,128)(2,1)S(1)}, u32[]{:S(2)}, u32[]{:S(2)}) collective-permute-start(bf16[144,256]{1,0:T(8,128)(2,1)S(1)} %shard_map.77.refs_0_), channel_id=1, source_target_pairs={{0,3},{1,2},{2,1},{3,0},{4,7},{5,6},{6,5},{7,4},{8,11},{9,10},{10,... | collective-permute-start | bytes 221192 | tf_op jit(solution)/shard_map/ppermute | solution.py:234
  11.9 2.2 %collective-permute-start.3 = (bf16[144,256]{1,0:T(8,128)(2,1)S(1)}, bf16[144,256]{1,0:T(8,128)(2,1)S(1)}, u32[]{:S(2)}, u32[]{:S(2)}) collective-permute-start(bf16[144,256]{1,0:T(8,128)(2,1)S(1)} %shard_map.77.refs_0_), channel_id=1, source_target_pairs={{0,6},{1,7},{2,4},{3,5},{4,2},{5,3},{6,0},{7,1},{8,14},{9,15},{10,... | collective-permute-start | bytes 221192 | tf_op jit(solution)/shard_map/ppermute | solution.py:234
  14.1 0.8 %collective-permute-start.7 = (bf16[2,192,256]{2,1,0:T(8,128)(2,1)S(1)}, bf16[2,192,256]{2,1,0:T(8,128)(2,1)S(1)}, u32[]{:S(2)}, u32[]{:S(2)}) collective-permute-start(bf16[2,192,256]{2,1,0:T(8,128)(2,1)S(1)} %pad_maximum_fusion), channel_id=1, source_target_pairs={{0,3},{1,2},{2,1},{3,0},{4,7},{5,6},{6,5},{7,4},{8,11},{9,10},{10,... | collective-permute-start | bytes 589832 | tf_op jit(solution)/shard_map/ppermute | solution.py:234
  14.9 1.0 %collective-permute-start.6 = (bf16[2,96,256]{2,1,0:T(8,128)(2,1)S(1)}, bf16[2,96,256]{2,1,0:T(8,128)(2,1)S(1)}, u32[]{:S(2)}, u32[]{:S(2)}) collective-permute-start(bf16[2,96,256]{2,1,0:T(8,128)(2,1)S(1)} %pad_maximum_fusion.1), channel_id=1, source_target_pairs={{0,1},{1,0},{2,3},{3,2},{4,5},{5,4},{6,7},{7,6},{8,9},{9,8},{10,11... | collective-permute-start | bytes 294920 | tf_op jit(solution)/shard_map/ppermute | solution.py:234
  15.9 1.0 %shard_map.78.mask = bf16[896,128]{1,0:T(8,128)(2,1)S(1)} custom-call(s32[8]{0:T(128)S(1)} %stack.35.place, s32[8]{0:T(128)S(1)} %copy-done.3, s32[8,16]{1,0:T(8,128)S(1)} %copy-done.2), custom_call_target="tpu_custom_call" | custom-call | bytes 576 | tf_op jit(solution)/shard_map/pallas_call | solution.py:40
  16.9 0.0 copy-start.4
  17.0 0.9 %collective-permute-done.3.refs_3_ = bf16[144,256]{1,0:T(8,128)(2,1)S(1)} collective-permute-done((bf16[144,256]{1,0:T(8,128)(2,1)S(1)}, bf16[144,256]{1,0:T(8,128)(2,1)S(1)}, u32[]{:S(2)}, u32[]{:S(2)}) %collective-permute-start.3) | collective-permute-done | bytes 73760 | tf_op jit(solution)/shard_map/ppermute | solution.py:234
  17.9 0.7 %shard_map.79.refs_0_ = bf16[144,256]{1,0:T(8,128)(2,1)S(1)} custom-call(s32[8]{0:T(128)S(1)} %stack.35.place, bf16[144,256]{1,0:T(8,128)(2,1)S(1)} %shard_map.77.refs_0_, bf16[144,256]{1,0:T(8,128)(2,1)S(1)} %collective-permute-done.1.refs_1_, bf16[144,256]{1,0:T(8,128)(2,1)S(1)} %collective-permute-done.2.refs_2_, ...), custom_call_target="tpu_custom_call" | custom-call | bytes 294944 | tf_op jit(solution)/shard_map/pallas_call | solution.py:40
  18.5 1.3 %collective-permute-start.10 = (bf16[144,256]{1,0:T(8,128)(2,1)S(1)}, bf16[144,256]{1,0:T(8,128)(2,1)S(1)}, u32[]{:S(2)}, u32[]{:S(2)}) collective-permute-start(bf16[144,256]{1,0:T(8,128)(2,1)S(1)} %shard_map.79.refs_0_), channel_id=1, source_target_pairs={{0,24},{1,25},{2,26},{3,27},{4,28},{5,29},{6,30},{7,31},{8,16},{9,... | collective-permute-start | bytes 221192 | tf_op jit(solution)/shard_map/ppermute | solution.py:234
  19.8 2.9 %collective-permute-start.9 = (bf16[144,256]{1,0:T(8,128)(2,1)S(1)}, bf16[144,256]{1,0:T(8,128)(2,1)S(1)}, u32[]{:S(2)}, u32[]{:S(2)}) collective-permute-start(bf16[144,256]{1,0:T(8,128)(2,1)S(1)} %shard_map.79.refs_0_), channel_id=1, source_target_pairs={{0,17},{1,16},{2,19},{3,18},{4,21},{5,20},{6,23},{7,22},{8,25},{9,... | collective-permute-start | bytes 221192 | tf_op jit(solution)/shard_map/ppermute | solution.py:234
  22.7 3.1 %shard_map.80 = (f32[256,256]{1,0:T(8,128)S(1)}, f32[256,256]{1,0:T(8,128)S(1)}, bf16[4,256,256]{2,1,0:T(8,128)(2,1)S(1)}) custom-call(s32[8]{0:T(128)S(1)} %stack.35.place, bf16[256,256]{1,0:T(8,128)(2,1)S(1)} %bitcast.27, bf16[2,256,256]{2,1,0:T(8,128)(2,1)S(1)} %bitcast.24, bf16[2,256,256]{2,1,0:T(8,128)(2,1)S(1)} %collective-permute-done.other.core, ...), custom_call_target="tpu_custom_call" | custom-call | flops 469762048 | bytes 1572896 | tf_op jit(solution)/shard_map/pallas_call | solution.py:40
  25.8 0.9 %collective-permute-done.8.refs_1_ = bf16[144,256]{1,0:T(8,128)(2,1)S(1)} collective-permute-done((bf16[144,256]{1,0:T(8,128)(2,1)S(1)}, bf16[144,256]{1,0:T(8,128)(2,1)S(1)}, u32[]{:S(2)}, u32[]{:S(2)}) %collective-permute-start.8) | collective-permute-done | bytes 73760 | tf_op jit(solution)/shard_map/ppermute | solution.py:234
  26.7 0.2 collective-permute-done.9.refs_2_
  26.9 0.7 %shard_map.81.mine = bf16[128,256]{1,0:T(8,128)(2,1)S(1)} custom-call(s32[8]{0:T(128)S(1)} %stack.35.place, bf16[144,256]{1,0:T(8,128)(2,1)S(1)} %shard_map.79.refs_0_, bf16[144,256]{1,0:T(8,128)(2,1)S(1)} %collective-permute-done.8.refs_1_, bf16[144,256]{1,0:T(8,128)(2,1)S(1)} %collective-permute-done.9.refs_2_, ...), custom_call_target="tpu_custom_call" | custom-call | bytes 294944 | tf_op jit(solution)/shard_map/pallas_call | solution.py:40
  27.6 1.3 %collective-permute-start.11 = (bf16[128,256]{1,0:T(8,128)(2,1)S(1)}, bf16[128,256]{1,0:T(8,128)(2,1)S(1)}, u32[]{:S(2)}, u32[]{:S(2)}) collective-permute-start(bf16[128,256]{1,0:T(8,128)(2,1)S(1)} %shard_map.81.mine), channel_id=1, source_target_pairs={{0,1},{1,0},{2,3},{3,2},{4,5},{5,4},{6,7},{7,6},{8,9},{9,8},{10,11... | collective-permute-start | bytes 196616 | tf_op jit(solution)/shard_map/ppermute | solution.py:234
  28.9 0.9 %collective-permute-done.11.other = bf16[128,256]{1,0:T(8,128)(2,1)S(1)} collective-permute-done((bf16[128,256]{1,0:T(8,128)(2,1)S(1)}, bf16[128,256]{1,0:T(8,128)(2,1)S(1)}, u32[]{:S(2)}, u32[]{:S(2)}) %collective-permute-start.11) | collective-permute-done | bytes 65568 | tf_op jit(solution)/shard_map/ppermute | solution.py:234
  29.8 1.5 %shard_map.82 = (bf16[256,256]{1,0:T(8,128)(2,1)}, bf16[256,256]{1,0:T(8,128)(2,1)}) custom-call(s32[8]{0:T(128)S(1)} %stack.35.place, f32[256,256]{1,0:T(8,128)S(1)} %get-tuple-element.20.acc, f32[256,256]{1,0:T(8,128)S(1)} %get-tuple-element.21.scale, bf16[4,256,256]{2,1,0:T(8,128)(2,1)S(1)} %get-tuple-element.22.reg_weights, ...), custom_call_target="tpu_custom_call" | custom-call | flops 67108864 | bytes 1179680 | tf_op jit(solution)/shard_map/pallas_call | solution.py:40
  (24 shorter events, 0.1 us)
Async XLA Ops:
  0.6 7.8 %collective-permute-start = (bf16[2,256,256]{2,1,0:T(8,128)(2,1)}, bf16[2,256,256]{2,1,0:T(8,128)(2,1)S(1)}, u32[]{:S(2)}, u32[]{:S(2)}) collective-permute-start(bf16[2,256,256]{2,1,0:T(8,128)(2,1)} %bitcast.22), channel_id=1, source_target_pairs={{0,1},{1,0},{2,3},{3,2},{4,5},{5,4},{6,7},{7,6},{8,9},{9,8},{10,11... | collective-permute-start | bytes 786440 | tf_op jit(solution)/shard_map/ppermute | solution.py:234
  1.1 7.3 %copy-start = (bf16[2,16,16,256]{3,2,1,0:T(8,128)(2,1)S(1)}, bf16[2,16,16,256]{3,2,1,0:T(8,128)(2,1)}, u32[]{:S(2)}) copy-start(bf16[2,16,16,256]{3,2,1,0:T(8,128)(2,1)} %param.7) | copy-start | bytes 786436
  2.2 11.9 %collective-permute-start.4 = (bf16[2,16,8,256]{3,2,1,0:T(8,128)(2,1)S(1)}, bf16[2,16,8,256]{3,2,1,0:T(8,128)(2,1)S(1)}, u32[]{:S(2)}, u32[]{:S(2)}) collective-permute-start(bf16[2,16,8,256]{3,2,1,0:T(8,128)(2,1)S(1)} %get-tuple-element.27), channel_id=1, source_target_pairs={{0,4},{1,5},{2,6},{3,7},{4,0},{5,1},{6,2},{7,3},{8,12},{9,13},{10,... | collective-permute-start | bytes 393224 | tf_op jit(solution)/shard_map/ppermute | solution.py:234
  4.8 9.3 %collective-permute-start.5 = (bf16[2,16,8,256]{3,2,1,0:T(8,128)(2,1)S(1)}, bf16[2,16,8,256]{3,2,1,0:T(8,128)(2,1)S(1)}, u32[]{:S(2)}, u32[]{:S(2)}) collective-permute-start(bf16[2,16,8,256]{3,2,1,0:T(8,128)(2,1)S(1)} %get-tuple-element.26), channel_id=1, source_target_pairs={{0,28},{4,8},{8,4},{12,16},{16,12},{20,24},{24,20},{28,0},{1,29},{... | collective-permute-start | bytes 393224 | tf_op jit(solution)/shard_map/ppermute | solution.py:243
  8.4 0.9 %copy-start.1 = (bf16[256,256]{1,0:T(8,128)(2,1)S(1)}, bf16[256,256]{1,0:T(8,128)(2,1)}, u32[]{:S(2)}) copy-start(bf16[256,256]{1,0:T(8,128)(2,1)} %queries.1) | copy-start | bytes 393220
  10.8 6.2 %collective-permute-start.1 = (bf16[144,256]{1,0:T(8,128)(2,1)S(1)}, bf16[144,256]{1,0:T(8,128)(2,1)S(1)}, u32[]{:S(2)}, u32[]{:S(2)}) collective-permute-start(bf16[144,256]{1,0:T(8,128)(2,1)S(1)} %shard_map.77.refs_0_), channel_id=1, source_target_pairs={{0,3},{1,2},{2,1},{3,0},{4,7},{5,6},{6,5},{7,4},{8,11},{9,10},{10,... | collective-permute-start | bytes 221192 | tf_op jit(solution)/shard_map/ppermute | solution.py:234
  11.9 5.1 %collective-permute-start.2 = (bf16[144,256]{1,0:T(8,128)(2,1)S(1)}, bf16[144,256]{1,0:T(8,128)(2,1)S(1)}, u32[]{:S(2)}, u32[]{:S(2)}) collective-permute-start(bf16[144,256]{1,0:T(8,128)(2,1)S(1)} %shard_map.77.refs_0_), channel_id=1, source_target_pairs={{0,5},{1,4},{2,7},{3,6},{4,1},{5,0},{6,3},{7,2},{8,13},{9,12},{10,... | collective-permute-start | bytes 221192 | tf_op jit(solution)/shard_map/ppermute | solution.py:234
  11.9 6.0 %collective-permute-start.3 = (bf16[144,256]{1,0:T(8,128)(2,1)S(1)}, bf16[144,256]{1,0:T(8,128)(2,1)S(1)}, u32[]{:S(2)}, u32[]{:S(2)}) collective-permute-start(bf16[144,256]{1,0:T(8,128)(2,1)S(1)} %shard_map.77.refs_0_), channel_id=1, source_target_pairs={{0,6},{1,7},{2,4},{3,5},{4,2},{5,3},{6,0},{7,1},{8,14},{9,15},{10,... | collective-permute-start | bytes 221192 | tf_op jit(solution)/shard_map/ppermute | solution.py:234
  14.1 8.6 %collective-permute-start.7 = (bf16[2,192,256]{2,1,0:T(8,128)(2,1)S(1)}, bf16[2,192,256]{2,1,0:T(8,128)(2,1)S(1)}, u32[]{:S(2)}, u32[]{:S(2)}) collective-permute-start(bf16[2,192,256]{2,1,0:T(8,128)(2,1)S(1)} %pad_maximum_fusion), channel_id=1, source_target_pairs={{0,3},{1,2},{2,1},{3,0},{4,7},{5,6},{6,5},{7,4},{8,11},{9,10},{10,... | collective-permute-start | bytes 589832 | tf_op jit(solution)/shard_map/ppermute | solution.py:234
  14.9 1.0 %copy-start.2 = (s32[8,16]{1,0:T(8,128)S(1)}, s32[8,16]{1,0:T(8,128)}, u32[]{:S(2)}) copy-start(s32[8,16]{1,0:T(8,128)} %sea.1) | copy-start | bytes 1540
  14.9 1.0 %copy-start.3 = (s32[8]{0:T(128)S(1)}, s32[8]{0:T(128)}, u32[]{:S(2)}) copy-start(s32[8]{0:T(128)} %pole.1) | copy-start | bytes 100
  14.9 7.8 %collective-permute-start.6 = (bf16[2,96,256]{2,1,0:T(8,128)(2,1)S(1)}, bf16[2,96,256]{2,1,0:T(8,128)(2,1)S(1)}, u32[]{:S(2)}, u32[]{:S(2)}) collective-permute-start(bf16[2,96,256]{2,1,0:T(8,128)(2,1)S(1)} %pad_maximum_fusion.1), channel_id=1, source_target_pairs={{0,1},{1,0},{2,3},{3,2},{4,5},{5,4},{6,7},{7,6},{8,9},{9,8},{10,11... | collective-permute-start | bytes 294920 | tf_op jit(solution)/shard_map/ppermute | solution.py:234
  16.9 5.8 %copy-start.4 = (bf16[16,16,256]{2,1,0:T(8,128)(2,1)S(1)}, bf16[16,16,256]{2,1,0:T(8,128)(2,1)}, u32[]{:S(2)}) copy-start(bf16[16,16,256]{2,1,0:T(8,128)(2,1)} %param.6) | copy-start | bytes 393220
  16.9 5.8 %copy-start.5 = (bf16[256,256]{1,0:T(8,128)(2,1)S(1)}, bf16[256,256]{1,0:T(8,128)(2,1)}, u32[]{:S(2)}) copy-start(bf16[256,256]{1,0:T(8,128)(2,1)} %reg_keys.1) | copy-start | bytes 393220
  18.5 7.3 %collective-permute-start.10 = (bf16[144,256]{1,0:T(8,128)(2,1)S(1)}, bf16[144,256]{1,0:T(8,128)(2,1)S(1)}, u32[]{:S(2)}, u32[]{:S(2)}) collective-permute-start(bf16[144,256]{1,0:T(8,128)(2,1)S(1)} %shard_map.79.refs_0_), channel_id=1, source_target_pairs={{0,24},{1,25},{2,26},{3,27},{4,28},{5,29},{6,30},{7,31},{8,16},{9,... | collective-permute-start | bytes 221192 | tf_op jit(solution)/shard_map/ppermute | solution.py:234
  19.8 6.9 %collective-permute-start.8 = (bf16[144,256]{1,0:T(8,128)(2,1)S(1)}, bf16[144,256]{1,0:T(8,128)(2,1)S(1)}, u32[]{:S(2)}, u32[]{:S(2)}) collective-permute-start(bf16[144,256]{1,0:T(8,128)(2,1)S(1)} %shard_map.79.refs_0_), channel_id=1, source_target_pairs={{0,9},{1,8},{2,11},{3,10},{4,13},{5,12},{6,15},{7,14},{8,1},{9,0},... | collective-permute-start | bytes 221192 | tf_op jit(solution)/shard_map/ppermute | solution.py:234
  19.8 7.1 %collective-permute-start.9 = (bf16[144,256]{1,0:T(8,128)(2,1)S(1)}, bf16[144,256]{1,0:T(8,128)(2,1)S(1)}, u32[]{:S(2)}, u32[]{:S(2)}) collective-permute-start(bf16[144,256]{1,0:T(8,128)(2,1)S(1)} %shard_map.79.refs_0_), channel_id=1, source_target_pairs={{0,17},{1,16},{2,19},{3,18},{4,21},{5,20},{6,23},{7,22},{8,25},{9,... | collective-permute-start | bytes 221192 | tf_op jit(solution)/shard_map/ppermute | solution.py:234
  27.6 2.3 %collective-permute-start.11 = (bf16[128,256]{1,0:T(8,128)(2,1)S(1)}, bf16[128,256]{1,0:T(8,128)(2,1)S(1)}, u32[]{:S(2)}, u32[]{:S(2)}) collective-permute-start(bf16[128,256]{1,0:T(8,128)(2,1)S(1)} %shard_map.81.mine), channel_id=1, source_target_pairs={{0,1},{1,0},{2,3},{3,2},{4,5},{5,4},{6,7},{7,6},{8,9},{9,8},{10,11... | collective-permute-start | bytes 196616 | tf_op jit(solution)/shard_map/ppermute | solution.py:234

commit v3 on v2

v3 whole, which is shorter than its diff:
```python
import functools

import jax
import jax.numpy as jnp
from jax import lax
from jax.experimental import pallas as pl
from jax.experimental.pallas import tpu as pltpu
from jax.sharding import PartitionSpec as P

HEADS = 4
HEAD_DIM = 64
NREG = 256
RADIUS = 6
TILE = 8
PAIR = 2 * HEAD_DIM
DEEP = 8
STATS = 16
AUG = 128
MASKED = -8192.0
SCALE = HEAD_DIM ** (-0.5)

BF16 = jnp.bfloat16
F32 = jnp.float32
NT = (((1,), (1,)), ((), ()))
TN = (((0,), (0,)), ((), ()))
VMEM = pl.BlockSpec(memory_space=pltpu.VMEM)
HBM = pl.BlockSpec(memory_space=pltpu.HBM)


def dot(a, b, dims):
    return lax.dot_general(a, b, dims, preferred_element_type=F32)


def place():
    count = lax.axis_size("lon") * lax.axis_size("lat")
    flat = lax.axis_index("lon") * lax.axis_size("lat") + lax.axis_index("lat")
    return [(flat >> b) & 1 for b in range(count.bit_length() - 1)]


def half():
    return functools.reduce(jnp.bitwise_xor, place())


def iota(shape, axis):
    return lax.broadcasted_iota(jnp.int32, shape, axis)


def call(kernel, out, args, specs, scratch=(), flops=0, limit=16):
    size = sum(a.size * a.dtype.itemsize for a in args)
    return pl.pallas_call(
        kernel,
        out_shape=out,
        in_specs=specs,
        out_specs=jax.tree.map(lambda _: VMEM, out),
        scratch_shapes=scratch,
        compiler_params=pltpu.CompilerParams(vmem_limit_bytes=limit * 2**20),
        cost_estimate=pl.CostEstimate(flops=flops, bytes_accessed=size, transcendentals=0),
    )(*args)


def pack(values, tops, sums, out_ref):
    rows = iota((STATS, values.shape[1]), 0)
    stats = jnp.zeros((STATS, values.shape[1]), F32)
    for j in range(2):
        high = sums[j].astype(BF16).astype(F32)
        for row, value in ((j, tops[j]), (2 + 2 * j, high), (3 + 2 * j, sums[j] - high)):
            stats = jnp.where(rows == row, value, stats)
    out_ref[:PAIR] = values.astype(BF16)
    out_ref[PAIR:] = stats.astype(BF16)


def sides_kernel(rows, cols, kv_ref, queries_ref, own, queries, near_ref, far_ref, wide, sem):
    copies = [
        pltpu.make_async_copy(kv_ref, own, sem.at[0]),
        pltpu.make_async_copy(queries_ref, queries, sem.at[1]),
    ]
    for copy in copies:
        copy.start()
    copies[0].wait()
    odd = lax.axis_index("lon") % 2 == 1
    for k in range(2):
        for lane in range(0, own.shape[2], 128):
            lanes = slice(lane, lane + 128)
            wide[...] = own[k, :, lanes].astype(F32)
            for c in range(RADIUS):
                low = wide[pl.ds(c, rows, stride=cols)]
                high = wide[pl.ds(cols - RADIUS + c, rows, stride=cols)]
                near_ref[k, c * rows : (c + 1) * rows, lanes] = jnp.where(odd, low, high).astype(BF16)
                far_ref[k, c * rows : (c + 1) * rows, lanes] = jnp.where(odd, high, low).astype(BF16)
    copies[1].wait()


def register_kernel(own, other, queries, out_ref):
    lanes = pl.ds(pl.multiple_of(half() * PAIR, PAIR), PAIR)
    keys = jnp.concatenate([own[0, :, lanes], other[0, :, lanes]], axis=0)
    vals = jnp.concatenate([own[1, :, lanes], other[1, :, lanes]], axis=0)
    scaled = queries[:, lanes] * jnp.asarray(SCALE, BF16)
    first = iota(scaled.shape, 1) < HEAD_DIM
    parts, tops, sums = [], [], []
    for j in range(2):
        mine = jnp.where(first == (j == 0), scaled, jnp.zeros_like(scaled))
        scores = dot(keys, mine, NT)
        top = jnp.max(scores, axis=0, keepdims=True).astype(BF16).astype(F32)
        weights = jnp.exp(scores - top)
        sums.append(jnp.sum(weights, axis=0, keepdims=True))
        tops.append(top)
        parts.append(dot(vals, weights.astype(BF16), TN))
    upper = iota(parts[0].shape, 0) < HEAD_DIM
    pack(jnp.where(upper, parts[0], parts[1]), tops, sums, out_ref)


def merge_kernel(bits, last, *refs):
    payloads, out_ref = refs[:-1], refs[-1]
    here = place()
    found = [(r[:PAIR].astype(F32), r[PAIR:].astype(F32)) for r in payloads]
    for level, bit in enumerate(bits):
        swap = here[bit] == 1
        step = 1 << level
        for low in range(len(found)):
            if not low & step:
                a, b = found[low], found[low + step]
                found[low] = tuple(jnp.where(swap, v, u) for u, v in zip(a, b))
                found[low + step] = tuple(jnp.where(swap, u, v) for u, v in zip(a, b))
    upper = iota((PAIR, found[0][0].shape[1]), 0) < HEAD_DIM
    tops, sums, factors = [], [], []
    for j in range(2):
        each = [stats[j : j + 1] for _, stats in found]
        top = functools.reduce(jnp.maximum, each)
        factor = [jnp.exp(e - top) for e in each]
        totals = [
            f * (stats[2 + 2 * j : 3 + 2 * j] + stats[3 + 2 * j : 4 + 2 * j])
            for f, (_, stats) in zip(factor, found)
        ]
        tops.append(top)
        sums.append(functools.reduce(jnp.add, totals))
        factors.append(factor)
    merged = functools.reduce(
        jnp.add,
        [values * jnp.where(upper, f, g) for f, g, (values, _) in zip(*factors, found)],
    )
    if last:
        out_ref[...] = (merged / jnp.where(upper, sums[0], sums[1])).astype(BF16)
    else:
        pack(merged, tops, sums, out_ref)


def segments(rows, cols):
    return (
        (rows, cols, False, 0, 0),
        (RADIUS, cols, False, "core", 0),
        (RADIUS, rows, True, 0, "a"),
        (RADIUS, rows, True, 0, "b"),
        (RADIUS, DEEP, True, "core deep", "a"),
        (RADIUS, DEEP, True, "core deep", "b"),
        (RADIUS, cols, False, "cross", 0),
        (RADIUS, DEEP, True, "cross deep", "a"),
        (RADIUS, DEEP, True, "cross deep", "b"),
    )


def closed_tiles(rows, cols, pole, sea):
    lat, lon = lax.axis_index("lat"), lax.axis_index("lon")
    bands, tiles = sea.shape
    down, across = rows // TILE, cols // TILE
    lane = iota((1, AUG), 1)
    closed = jnp.zeros((1, AUG), F32)
    for i in range(down + 2):
        band = lat * down - 1 + i
        inside = (band >= 0) & (band < bands)
        band = jnp.clip(band, 0, bands - 1)
        for j in range(across + 2):
            tile = (lon * across - 1 + j + tiles) % tiles
            kept = inside & (pole[band] * sea[band, tile] > 0)
            at = rows + cols + i * (across + 2) + j
            closed = jnp.where(lane == at, jnp.where(kept, 0.0, MASKED), closed)
    return closed


def masks(rows, cols, closed):
    lat, lon = lax.axis_index("lat"), lax.axis_index("lon")
    across = cols // TILE
    lat_odd, lon_odd = lat % 2 == 1, lon % 2 == 1
    starts = {
        0: 0,
        "core": jnp.where(lat_odd, -RADIUS, rows),
        "core deep": jnp.where(lat_odd, -DEEP, rows),
        "cross": jnp.where(lat_odd, rows, -RADIUS),
        "cross deep": jnp.where(lat_odd, rows, -DEEP),
        "a": jnp.where(lon_odd, -RADIUS, cols),
        "b": jnp.where(lon_odd, cols, -RADIUS),
    }
    lane = iota((1, AUG), 1)
    for slow, fast, fast_rows, row, col in segments(rows, cols):
        index = iota((slow * fast, AUG), 0)
        outer, inner = index >> (fast.bit_length() - 1), index & (fast - 1)
        row = starts[row] + (inner if fast_rows else outer)
        col = starts[col] + (outer if fast_rows else inner)
        apart = jnp.where(lane < rows, lane - row, lane - rows - col)
        far = (lane < rows + cols) & (jnp.abs(apart) > RADIUS)
        cell = ((row + TILE) >> 3) * (across + 2) + ((col + TILE) >> 3)
        value = jnp.where(lane - (rows + cols) == cell, closed, 0.0)
        yield jnp.where(far, MASKED, value).astype(BF16)


def near_kernel(rows, cols, q_ref, own, core, a, b, corner, cross, reg_keys, pole_ref, sea_ref,
                acc_ref, scale_ref, reg_ref, kbuf, vbuf, pole, sea, sem):
    copies = [
        pltpu.make_async_copy(pole_ref, pole, sem.at[0]),
        pltpu.make_async_copy(sea_ref, sea, sem.at[1]),
    ]
    for copy in copies:
        copy.start()
    cells = vbuf.shape[0]
    lat = lax.axis_index("lat")
    taken = pl.ds(pl.multiple_of(jnp.where(lat % 2 == 0, 0, (rows - RADIUS) * cols), 16), RADIUS * cols)
    offset = 0
    for ref, index in ((own, slice(None)), (core, taken), (a, slice(None)), (b, slice(None)),
                       (corner, slice(None)), (cross, slice(None))):
        keys, vals = ref[0, index], ref[1, index]
        end = offset + keys.shape[0]
        for p in range(2):
            kbuf[p, offset:end, :PAIR] = keys[:, p * PAIR : (p + 1) * PAIR]
        vbuf[offset:end] = vals
        offset = end
    for p in range(2):
        kbuf[p, cells:, :PAIR] = reg_keys[:, p * PAIR : (p + 1) * PAIR]
        kbuf[p, cells:, PAIR:] = jnp.zeros((NREG, AUG), BF16)
    for copy in copies:
        copy.wait()
    offset = 0
    for mask in masks(rows, cols, closed_tiles(rows, cols, pole, sea)):
        for p in range(2):
            kbuf[p, offset : offset + mask.shape[0], PAIR:] = mask
        offset += mask.shape[0]
    count = rows * cols
    query = iota((count, AUG), 0)
    lane = iota((count, AUG), 1)
    tiles = (rows // TILE + 2) * (cols // TILE + 2)
    hot = (lane == query >> (cols.bit_length() - 1)) | (lane - rows == query & (cols - 1))
    hot = hot | ((lane >= rows + cols) & (lane < rows + cols + tiles))
    hot = jnp.where(hot, 1.0, 0.0).astype(BF16)
    first = iota((count, PAIR), 1) < HEAD_DIM
    for p in range(2):
        scaled = q_ref[:, p * PAIR : (p + 1) * PAIR] * jnp.asarray(SCALE, BF16)
        mixed, totals = [], []
        for j in range(2):
            mine = jnp.where(first == (j == 0), scaled, jnp.zeros_like(scaled))
            scores = dot(jnp.concatenate([mine, hot], axis=1), kbuf[p], NT)
            weights = jnp.exp(scores - jnp.max(scores, axis=1, keepdims=True))
            totals.append(jnp.sum(weights, axis=1, keepdims=True))
            rounded = weights.astype(BF16)
            reg_ref[2 * p + j] = rounded[:, cells:]
            mixed.append(
                jnp.dot(rounded[:, :cells], vbuf[:, p * PAIR : (p + 1) * PAIR], preferred_element_type=F32)
            )
        acc_ref[:, p * PAIR : (p + 1) * PAIR] = jnp.where(first, *mixed)
        scale_ref[:, p * PAIR : (p + 1) * PAIR] = 1.0 / jnp.where(first, *totals)


def final_kernel(acc, scale, reg_weights, mine, other, out_ref, reg_out_ref):
    here = half() == 0
    first = iota((acc.shape[0], PAIR), 1) < HEAD_DIM
    for p in range(2):
        lanes = slice(p * PAIR, (p + 1) * PAIR)
        vals = jnp.where(here == (p == 0), mine[...], other[...])
        added = jnp.where(first, dot(reg_weights[2 * p], vals, NT), dot(reg_weights[2 * p + 1], vals, NT))
        out_ref[:, lanes] = ((acc[:, lanes] + added) * scale[:, lanes]).astype(BF16)
        reg_out_ref[:, lanes] = vals.astype(F32).T.astype(BF16)


def shards(queries, key_values, pole_mask, sea_mask, reg_queries, reg_keys):
    rows, cols, channels = queries.shape
    lats, lons = lax.axis_size("lat"), lax.axis_size("lon")
    devices = lats * lons
    assert lats == 4 and lons & (lons - 1) == 0 and lons > 1
    assert rows & (rows - 1) == 0 and cols & (cols - 1) == 0 and rows % TILE == 0 and cols % TILE == 0 and TILE == DEEP == 8
    nbits = devices.bit_length() - 1
    lat = lax.axis_index("lat")
    everyone = ("lon", "lat")

    def swap(x, mask):
        return lax.ppermute(x, everyone, [(i, i ^ mask) for i in range(devices)])

    cells = rows * cols
    key_values = key_values.reshape(2, cells, channels)
    core = swap(key_values, 1)

    side = jax.ShapeDtypeStruct((2, RADIUS * rows, channels), BF16)
    own, reg_queries, near_cols, far_cols = call(
        functools.partial(sides_kernel, rows, cols),
        (jax.ShapeDtypeStruct(key_values.shape, BF16), jax.ShapeDtypeStruct(reg_queries.shape, BF16), side, side),
        tuple(pltpu.with_memory_space_constraint(x, pltpu.HBM) for x in (key_values, reg_queries)),
        [HBM] * 2,
        scratch=[pltpu.VMEM((cells, 128), F32), pltpu.SemaphoreType.DMA((2,))],
    )
    side_a = swap(near_cols, lats)
    side_b = lax.ppermute(
        far_cols, "lon", [(i, (i + 1 if i % 2 else i - 1) % lons) for i in range(lons)]
    )

    payload = call(
        register_kernel,
        jax.ShapeDtypeStruct((PAIR + STATS, NREG), BF16),
        (own, core, reg_queries),
        [VMEM] * 3,
        flops=4 * 2 * cells * NREG * 2 * PAIR,
    )

    side_a, side_b, _ = lax.optimization_barrier((side_a, side_b, payload))
    def take(shard, size, start, count):
        taken = lax.dynamic_slice_in_dim(shard.reshape(2, -1, size, channels), start, count, 2)
        return taken.reshape(2, -1, channels)

    core_deep, cross_deep = (1 - lat % 2) * (rows - DEEP), (lat % 2) * (rows - DEEP)
    corner = swap(
        jnp.concatenate([take(s, rows, core_deep, DEEP) for s in (side_a, side_b)], axis=1), 1
    )
    cross = swap(
        jnp.concatenate(
            [
                take(own, cells, (lat % 2) * (rows - RADIUS) * cols, RADIUS * cols),
                *[take(s, rows, cross_deep, DEEP) for s in (side_a, side_b)],
            ],
            axis=1,
        ),
        3,
    )
    keys = sum(segment[0] * segment[1] for segment in segments(rows, cols))
    square = jax.ShapeDtypeStruct((cells, channels), F32)
    acc, scale, reg_weights = call(
        functools.partial(near_kernel, rows, cols),
        (square, square, jax.ShapeDtypeStruct((HEADS, cells, NREG), BF16)),
        (
            queries.reshape(cells, channels),
            own,
            core,
            side_a,
            side_b,
            corner,
            cross,
            reg_keys,
            pole_mask,
            sea_mask,
        ),
        [VMEM] * 8 + [HBM] * 2,
        scratch=[
            pltpu.VMEM((2, keys + NREG, PAIR + AUG), BF16),
            pltpu.VMEM((keys, channels), BF16),
            pltpu.SMEM(pole_mask.shape, jnp.int32),
            pltpu.SMEM(sea_mask.shape, jnp.int32),
            pltpu.SemaphoreType.DMA((2,)),
        ],
        flops=2 * 2 * cells * keys * channels * 2,
        limit=32,
    )
    stages = [tuple(range(b, min(b + 2, nbits))) for b in range(1, nbits, 2)]
    for stage in stages:
        gathered = [payload]
        for chosen in range(1, 1 << len(stage)):
            flips = [b for k, b in enumerate(stage) if chosen >> k & 1]
            gathered.append(swap(payload, sum(1 << b for b in flips) + len(flips) % 2))
        last = stage is stages[-1]
        if last:
            gathered[0], acc, scale, reg_weights = lax.optimization_barrier(
                (gathered[0], acc, scale, reg_weights)
            )
        payload = call(
            functools.partial(merge_kernel, stage, last),
            jax.ShapeDtypeStruct((PAIR if last else PAIR + STATS, NREG), BF16),
            tuple(gathered),
            [VMEM] * len(gathered),
        )

    other = swap(payload, 1)
    attended, reg_out = call(
        final_kernel,
        (
            jax.ShapeDtypeStruct((cells, channels), BF16),
            jax.ShapeDtypeStruct((NREG, channels), BF16),
        ),
        (acc, scale, reg_weights, payload, other),
        [VMEM] * 5,
        flops=2 * cells * NREG * channels * 2,
    )
    return attended.reshape(rows, cols, channels), reg_out


def solution(mesh):
    return jax.shard_map(
        shards,
        mesh=mesh,
        in_specs=(P("lat", "lon", None), P(None, "lat", "lon", None), P(), P(), P(), P()),
        out_specs=(P("lat", "lon", None), P()),
        check_vma=False,
    )
```

time: 31.5 us -> 28.6 us (0.908)
  local copies, waits for them, and re-layouts: 1.95 us -> 0.04 us
  Pallas kernels: 8.44 us -> 7.03 us
  waiting for transfers between devices: 2.92 us -> 3.36 us
    pallas_call x6, Pallas kernels: 8.44 us -> 7.03 us  [call(): pl.pallas_call(kernel, out_shape=out, in_specs=specs, out_specs=jax.tree....]
    dynamic_slice x2 -> x0, local copies, waits for them, and re-layouts: 1.04 us -> none  [the longest x1 1.03 us: shards(): lax.dynamic_slice_in_dim(key_values, lon % 2 * (cols - SIDE), SIDE, 2)]
    unnamed x12 -> x8, local copies, waits for them, and re-layouts: 0.81 us -> 0.02 us
    ppermute x11, waiting for transfers between devices: 2.92 us -> 3.36 us  [swap(): return lax.ppermute(x, everyone, [(i, i ^ mask) for i in range(devices)])]
  transfers between devices with their start and end apart: 12 -> 12, of which waited for: 4 -> 3; matrix products, arithmetic and copies ran while one was open for 4% -> 0% of each run, Pallas kernels for 20% -> 21%
where the time goes in v3:
time: 28.6 us; the launch traced here: 28.4 us
  starting transfers between devices  17.2 us (60%)
  Pallas kernels  7.03 us (25%)
  waiting for transfers between devices  3.36 us (12%)
  between operations  0.75 us (3%)
    ppermute x11, starting transfers between devices, swap(): return lax.ppermute(x, everyone, [(i, i ^ mask) for i in range(devices)])  13.6 us
    pallas_call x6, Pallas kernels, call(): pl.pallas_call(kernel, out_shape=out, in_specs=specs, out_specs=jax.tree....  7.03 us
    ppermute x1, starting transfers between devices, shards(): lax.ppermute(far_cols, 'lon', [(i, (i + 1 if i % 2 else i - 1) % lons) fo...  3.54 us
    ppermute x11, waiting for transfers between devices, swap(): return lax.ppermute(x, everyone, [(i, i ^ mask) for i in range(devices)])  3.36 us
  transfers between devices with their start and end apart: 12, of which 3 were waited for; matrix products, arithmetic and copies ran while one was open for 0% of the time, Pallas kernels for 21%

profile of v3, /device:TPU:0, one launch (start us, length us, event | category | flops | bytes accessed | tf_op | source)
XLA Modules:
  0.0 28.4 jit_solution(6429618326920168222)
XLA Ops:
  0.6 0.5 %collective-permute-start = (bf16[2,256,256]{2,1,0:T(8,128)(2,1)}, bf16[2,256,256]{2,1,0:T(8,128)(2,1)S(1)}, u32[]{:S(2)}, u32[]{:S(2)}) collective-permute-start(bf16[2,256,256]{2,1,0:T(8,128)(2,1)} %bitcast.16), channel_id=1, source_target_pairs={{0,1},{1,0},{2,3},{3,2},{4,5},{5,4},{6,7},{7,6},{8,9},{9,8},{10,11... | collective-permute-start | bytes 786440 | tf_op jit(solution)/shard_map/ppermute | solution.py:282
  1.1 1.1 %shard_map.77 = (bf16[2,256,256]{2,1,0:T(8,128)(2,1)S(1)}, bf16[256,256]{1,0:T(8,128)(2,1)S(1)}, bf16[2,96,256]{2,1,0:T(8,128)(2,1)S(1)}, bf16[2,96,256]{2,1,0:T(8,128)(2,1)S(1)}) custom-call(bf16[2,256,256]{2,1,0:T(8,128)(2,1)} %bitcast.17, bf16[256,256]{1,0:T(8,128)(2,1)} %queries_ref.1), custom_call_target="tpu_custom_call" | custom-call | bytes 393216 | tf_op jit(solution)/shard_map/pallas_call | solution.py:50
  2.3 2.6 %collective-permute-start.4 = (bf16[2,96,256]{2,1,0:T(8,128)(2,1)S(1)}, bf16[2,96,256]{2,1,0:T(8,128)(2,1)S(1)}, u32[]{:S(2)}, u32[]{:S(2)}) collective-permute-start(bf16[2,96,256]{2,1,0:T(8,128)(2,1)S(1)} %get-tuple-element.19), channel_id=1, source_target_pairs={{0,4},{1,5},{2,6},{3,7},{4,0},{5,1},{6,2},{7,3},{8,12},{9,13},{10,... | collective-permute-start | bytes 294920 | tf_op jit(solution)/shard_map/ppermute | solution.py:282
  4.9 3.5 %collective-permute-start.5 = (bf16[2,96,256]{2,1,0:T(8,128)(2,1)S(1)}, bf16[2,96,256]{2,1,0:T(8,128)(2,1)S(1)}, u32[]{:S(2)}, u32[]{:S(2)}) collective-permute-start(bf16[2,96,256]{2,1,0:T(8,128)(2,1)S(1)} %get-tuple-element.20), channel_id=1, source_target_pairs={{0,28},{4,8},{8,4},{12,16},{16,12},{20,24},{24,20},{28,0},{1,29},{... | collective-permute-start | bytes 294920 | tf_op jit(solution)/shard_map/ppermute | solution.py:297
  8.4 0.0 collective-permute-done.other.core
  8.4 1.0 %shard_map.78.refs_0_ = bf16[144,256]{1,0:T(8,128)(2,1)S(1)} custom-call(bf16[2,256,256]{2,1,0:T(8,128)(2,1)S(1)} %get-tuple-element.17.own, bf16[2,256,256]{2,1,0:T(8,128)(2,1)S(1)} %collective-permute-done.other.core, bf16[256,256]{1,0:T(8,128)(2,1)S(1)} %get-tuple-element.18.queries), custom_call_target="tpu_custom_call" | custom-call | flops 134217728 | bytes 655360 | tf_op jit(solution)/shard_map/pallas_call | solution.py:50
  9.5 1.1 %collective-permute-start.1 = (bf16[144,256]{1,0:T(8,128)(2,1)S(1)}, bf16[144,256]{1,0:T(8,128)(2,1)S(1)}, u32[]{:S(2)}, u32[]{:S(2)}) collective-permute-start(bf16[144,256]{1,0:T(8,128)(2,1)S(1)} %shard_map.78.refs_0_), channel_id=1, source_target_pairs={{0,3},{1,2},{2,1},{3,0},{4,7},{5,6},{6,5},{7,4},{8,11},{9,10},{10,... | collective-permute-start | bytes 221192 | tf_op jit(solution)/shard_map/ppermute | solution.py:282
  10.5 0.0 collective-permute-start.2
  10.5 2.2 %collective-permute-start.3 = (bf16[144,256]{1,0:T(8,128)(2,1)S(1)}, bf16[144,256]{1,0:T(8,128)(2,1)S(1)}, u32[]{:S(2)}, u32[]{:S(2)}) collective-permute-start(bf16[144,256]{1,0:T(8,128)(2,1)S(1)} %shard_map.78.refs_0_), channel_id=1, source_target_pairs={{0,6},{1,7},{2,4},{3,5},{4,2},{5,3},{6,0},{7,1},{8,14},{9,15},{10,... | collective-permute-start | bytes 221192 | tf_op jit(solution)/shard_map/ppermute | solution.py:282
  12.8 0.8 %collective-permute-start.7 = (bf16[2,192,256]{2,1,0:T(8,128)(2,1)S(1)}, bf16[2,192,256]{2,1,0:T(8,128)(2,1)S(1)}, u32[]{:S(2)}, u32[]{:S(2)}) collective-permute-start(bf16[2,192,256]{2,1,0:T(8,128)(2,1)S(1)} %pad_maximum_fusion), channel_id=1, source_target_pairs={{0,3},{1,2},{2,1},{3,0},{4,7},{5,6},{6,5},{7,4},{8,11},{9,10},{10,... | collective-permute-start | bytes 589832 | tf_op jit(solution)/shard_map/ppermute | solution.py:282
  13.6 0.0 copy-start.1
  13.6 0.0 copy-start.2
  13.6 0.9 %collective-permute-start.6 = (bf16[2,96,256]{2,1,0:T(8,128)(2,1)S(1)}, bf16[2,96,256]{2,1,0:T(8,128)(2,1)S(1)}, u32[]{:S(2)}, u32[]{:S(2)}) collective-permute-start(bf16[2,96,256]{2,1,0:T(8,128)(2,1)S(1)} %pad_maximum_fusion.1), channel_id=1, source_target_pairs={{0,1},{1,0},{2,3},{3,2},{4,5},{5,4},{6,7},{7,6},{8,9},{9,8},{10,11... | collective-permute-start | bytes 294920 | tf_op jit(solution)/shard_map/ppermute | solution.py:282
  14.6 2.0 %collective-permute-done.3.refs_3_ = bf16[144,256]{1,0:T(8,128)(2,1)S(1)} collective-permute-done((bf16[144,256]{1,0:T(8,128)(2,1)S(1)}, bf16[144,256]{1,0:T(8,128)(2,1)S(1)}, u32[]{:S(2)}, u32[]{:S(2)}) %collective-permute-start.3) | collective-permute-done | bytes 73760 | tf_op jit(solution)/shard_map/ppermute | solution.py:282
  16.5 0.1 shard_map.79.refs_0_
  16.7 0.0 copy-start.3
  16.7 1.2 %collective-permute-start.10 = (bf16[144,256]{1,0:T(8,128)(2,1)S(1)}, bf16[144,256]{1,0:T(8,128)(2,1)S(1)}, u32[]{:S(2)}, u32[]{:S(2)}) collective-permute-start(bf16[144,256]{1,0:T(8,128)(2,1)S(1)} %shard_map.79.refs_0_), channel_id=1, source_target_pairs={{0,24},{1,25},{2,26},{3,27},{4,28},{5,29},{6,30},{7,31},{8,16},{9,... | collective-permute-start | bytes 221192 | tf_op jit(solution)/shard_map/ppermute | solution.py:282
  17.9 2.9 %collective-permute-start.9 = (bf16[144,256]{1,0:T(8,128)(2,1)S(1)}, bf16[144,256]{1,0:T(8,128)(2,1)S(1)}, u32[]{:S(2)}, u32[]{:S(2)}) collective-permute-start(bf16[144,256]{1,0:T(8,128)(2,1)S(1)} %shard_map.79.refs_0_), channel_id=1, source_target_pairs={{0,17},{1,16},{2,19},{3,18},{4,21},{5,20},{6,23},{7,22},{8,25},{9,... | collective-permute-start | bytes 221192 | tf_op jit(solution)/shard_map/ppermute | solution.py:282
  20.9 3.7 %shard_map.80 = (f32[256,256]{1,0:T(8,128)S(1)}, f32[256,256]{1,0:T(8,128)S(1)}, bf16[4,256,256]{2,1,0:T(8,128)(2,1)S(1)}) custom-call(bf16[256,256]{1,0:T(8,128)(2,1)S(1)} %bitcast.15, bf16[2,256,256]{2,1,0:T(8,128)(2,1)S(1)} %get-tuple-element.17.own, bf16[2,256,256]{2,1,0:T(8,128)(2,1)S(1)} %collective-permute-done.other.core, ...), custom_call_target="tpu_custom_call" | custom-call | flops 436207616 | bytes 1278496 | tf_op jit(solution)/shard_map/pallas_call | solution.py:50
  24.6 0.4 %collective-permute-done.8.refs_1_ = bf16[144,256]{1,0:T(8,128)(2,1)S(1)} collective-permute-done((bf16[144,256]{1,0:T(8,128)(2,1)S(1)}, bf16[144,256]{1,0:T(8,128)(2,1)S(1)}, u32[]{:S(2)}, u32[]{:S(2)}) %collective-permute-start.8) | collective-permute-done | bytes 73760 | tf_op jit(solution)/shard_map/ppermute | solution.py:282
  25.0 0.1 shard_map.81.mine
  25.2 1.4 %collective-permute-start.11 = (bf16[128,256]{1,0:T(8,128)(2,1)S(1)}, bf16[128,256]{1,0:T(8,128)(2,1)S(1)}, u32[]{:S(2)}, u32[]{:S(2)}) collective-permute-start(bf16[128,256]{1,0:T(8,128)(2,1)S(1)} %shard_map.81.mine), channel_id=1, source_target_pairs={{0,1},{1,0},{2,3},{3,2},{4,5},{5,4},{6,7},{7,6},{8,9},{9,8},{10,11... | collective-permute-start | bytes 196616 | tf_op jit(solution)/shard_map/ppermute | solution.py:282
  26.5 0.9 %collective-permute-done.11.other = bf16[128,256]{1,0:T(8,128)(2,1)S(1)} collective-permute-done((bf16[128,256]{1,0:T(8,128)(2,1)S(1)}, bf16[128,256]{1,0:T(8,128)(2,1)S(1)}, u32[]{:S(2)}, u32[]{:S(2)}) %collective-permute-start.11) | collective-permute-done | bytes 65568 | tf_op jit(solution)/shard_map/ppermute | solution.py:282
  27.4 1.0 %shard_map.82 = (bf16[256,256]{1,0:T(8,128)(2,1)}, bf16[256,256]{1,0:T(8,128)(2,1)}) custom-call(f32[256,256]{1,0:T(8,128)S(1)} %get-tuple-element.26.acc, f32[256,256]{1,0:T(8,128)S(1)} %get-tuple-element.27.scale, bf16[4,256,256]{2,1,0:T(8,128)(2,1)S(1)} %get-tuple-element.28.reg_weights, bf16[128,256]{1,0:T(8,128)(2,1)S(1)} %shard_map.81.mine, ...), custom_call_target="tpu_custom_call" | custom-call | flops 67108864 | bytes 1179648 | tf_op jit(solution)/shard_map/pallas_call | solution.py:50
  (18 shorter events, 0.1 us)
Async XLA Ops:
  0.6 7.8 %collective-permute-start = (bf16[2,256,256]{2,1,0:T(8,128)(2,1)}, bf16[2,256,256]{2,1,0:T(8,128)(2,1)S(1)}, u32[]{:S(2)}, u32[]{:S(2)}) collective-permute-start(bf16[2,256,256]{2,1,0:T(8,128)(2,1)} %bitcast.16), channel_id=1, source_target_pairs={{0,1},{1,0},{2,3},{3,2},{4,5},{5,4},{6,7},{7,6},{8,9},{9,8},{10,11... | collective-permute-start | bytes 786440 | tf_op jit(solution)/shard_map/ppermute | solution.py:282
  2.3 10.4 %collective-permute-start.4 = (bf16[2,96,256]{2,1,0:T(8,128)(2,1)S(1)}, bf16[2,96,256]{2,1,0:T(8,128)(2,1)S(1)}, u32[]{:S(2)}, u32[]{:S(2)}) collective-permute-start(bf16[2,96,256]{2,1,0:T(8,128)(2,1)S(1)} %get-tuple-element.19), channel_id=1, source_target_pairs={{0,4},{1,5},{2,6},{3,7},{4,0},{5,1},{6,2},{7,3},{8,12},{9,13},{10,... | collective-permute-start | bytes 294920 | tf_op jit(solution)/shard_map/ppermute | solution.py:282
  4.9 7.8 %collective-permute-start.5 = (bf16[2,96,256]{2,1,0:T(8,128)(2,1)S(1)}, bf16[2,96,256]{2,1,0:T(8,128)(2,1)S(1)}, u32[]{:S(2)}, u32[]{:S(2)}) collective-permute-start(bf16[2,96,256]{2,1,0:T(8,128)(2,1)S(1)} %get-tuple-element.20), channel_id=1, source_target_pairs={{0,28},{4,8},{8,4},{12,16},{16,12},{20,24},{24,20},{28,0},{1,29},{... | collective-permute-start | bytes 294920 | tf_op jit(solution)/shard_map/ppermute | solution.py:297
  9.5 5.1 %collective-permute-start.1 = (bf16[144,256]{1,0:T(8,128)(2,1)S(1)}, bf16[144,256]{1,0:T(8,128)(2,1)S(1)}, u32[]{:S(2)}, u32[]{:S(2)}) collective-permute-start(bf16[144,256]{1,0:T(8,128)(2,1)S(1)} %shard_map.78.refs_0_), channel_id=1, source_target_pairs={{0,3},{1,2},{2,1},{3,0},{4,7},{5,6},{6,5},{7,4},{8,11},{9,10},{10,... | collective-permute-start | bytes 221192 | tf_op jit(solution)/shard_map/ppermute | solution.py:282
  10.5 4.0 %collective-permute-start.2 = (bf16[144,256]{1,0:T(8,128)(2,1)S(1)}, bf16[144,256]{1,0:T(8,128)(2,1)S(1)}, u32[]{:S(2)}, u32[]{:S(2)}) collective-permute-start(bf16[144,256]{1,0:T(8,128)(2,1)S(1)} %shard_map.78.refs_0_), channel_id=1, source_target_pairs={{0,5},{1,4},{2,7},{3,6},{4,1},{5,0},{6,3},{7,2},{8,13},{9,12},{10,... | collective-permute-start | bytes 221192 | tf_op jit(solution)/shard_map/ppermute | solution.py:282
  10.5 6.0 %collective-permute-start.3 = (bf16[144,256]{1,0:T(8,128)(2,1)S(1)}, bf16[144,256]{1,0:T(8,128)(2,1)S(1)}, u32[]{:S(2)}, u32[]{:S(2)}) collective-permute-start(bf16[144,256]{1,0:T(8,128)(2,1)S(1)} %shard_map.78.refs_0_), channel_id=1, source_target_pairs={{0,6},{1,7},{2,4},{3,5},{4,2},{5,3},{6,0},{7,1},{8,14},{9,15},{10,... | collective-permute-start | bytes 221192 | tf_op jit(solution)/shard_map/ppermute | solution.py:282
  12.8 8.1 %collective-permute-start.7 = (bf16[2,192,256]{2,1,0:T(8,128)(2,1)S(1)}, bf16[2,192,256]{2,1,0:T(8,128)(2,1)S(1)}, u32[]{:S(2)}, u32[]{:S(2)}) collective-permute-start(bf16[2,192,256]{2,1,0:T(8,128)(2,1)S(1)} %pad_maximum_fusion), channel_id=1, source_target_pairs={{0,3},{1,2},{2,1},{3,0},{4,7},{5,6},{6,5},{7,4},{8,11},{9,10},{10,... | collective-permute-start | bytes 589832 | tf_op jit(solution)/shard_map/ppermute | solution.py:282
  13.6 7.3 %copy-start = (bf16[16,16,256]{2,1,0:T(8,128)(2,1)S(1)}, bf16[16,16,256]{2,1,0:T(8,128)(2,1)}, u32[]{:S(2)}) copy-start(bf16[16,16,256]{2,1,0:T(8,128)(2,1)} %param.6) | copy-start | bytes 393220
  13.6 7.3 %copy-start.1 = (bf16[256,256]{1,0:T(8,128)(2,1)S(1)}, bf16[256,256]{1,0:T(8,128)(2,1)}, u32[]{:S(2)}) copy-start(bf16[256,256]{1,0:T(8,128)(2,1)} %reg_keys.1) | copy-start | bytes 393220
  13.6 7.3 %copy-start.2 = (s32[8,16]{1,0:T(8,128)S(1)}, s32[8,16]{1,0:T(8,128)}, u32[]{:S(2)}) copy-start(s32[8,16]{1,0:T(8,128)} %sea_ref.1) | copy-start | bytes 1540
  13.6 7.2 %collective-permute-start.6 = (bf16[2,96,256]{2,1,0:T(8,128)(2,1)S(1)}, bf16[2,96,256]{2,1,0:T(8,128)(2,1)S(1)}, u32[]{:S(2)}, u32[]{:S(2)}) collective-permute-start(bf16[2,96,256]{2,1,0:T(8,128)(2,1)S(1)} %pad_maximum_fusion.1), channel_id=1, source_target_pairs={{0,1},{1,0},{2,3},{3,2},{4,5},{5,4},{6,7},{7,6},{8,9},{9,8},{10,11... | collective-permute-start | bytes 294920 | tf_op jit(solution)/shard_map/ppermute | solution.py:282
  16.7 4.2 %copy-start.3 = (s32[8]{0:T(128)S(1)}, s32[8]{0:T(128)}, u32[]{:S(2)}) copy-start(s32[8]{0:T(128)} %pole_ref.1) | copy-start | bytes 100
  16.7 7.9 %collective-permute-start.10 = (bf16[144,256]{1,0:T(8,128)(2,1)S(1)}, bf16[144,256]{1,0:T(8,128)(2,1)S(1)}, u32[]{:S(2)}, u32[]{:S(2)}) collective-permute-start(bf16[144,256]{1,0:T(8,128)(2,1)S(1)} %shard_map.79.refs_0_), channel_id=1, source_target_pairs={{0,24},{1,25},{2,26},{3,27},{4,28},{5,29},{6,30},{7,31},{8,16},{9,... | collective-permute-start | bytes 221192 | tf_op jit(solution)/shard_map/ppermute | solution.py:282
  17.9 7.1 %collective-permute-start.8 = (bf16[144,256]{1,0:T(8,128)(2,1)S(1)}, bf16[144,256]{1,0:T(8,128)(2,1)S(1)}, u32[]{:S(2)}, u32[]{:S(2)}) collective-permute-start(bf16[144,256]{1,0:T(8,128)(2,1)S(1)} %shard_map.79.refs_0_), channel_id=1, source_target_pairs={{0,9},{1,8},{2,11},{3,10},{4,13},{5,12},{6,15},{7,14},{8,1},{9,0},... | collective-permute-start | bytes 221192 | tf_op jit(solution)/shard_map/ppermute | solution.py:282
  17.9 7.1 %collective-permute-start.9 = (bf16[144,256]{1,0:T(8,128)(2,1)S(1)}, bf16[144,256]{1,0:T(8,128)(2,1)S(1)}, u32[]{:S(2)}, u32[]{:S(2)}) collective-permute-start(bf16[144,256]{1,0:T(8,128)(2,1)S(1)} %shard_map.79.refs_0_), channel_id=1, source_target_pairs={{0,17},{1,16},{2,19},{3,18},{4,21},{5,20},{6,23},{7,22},{8,25},{9,... | collective-permute-start | bytes 221192 | tf_op jit(solution)/shard_map/ppermute | solution.py:282
  25.2 2.3 %collective-permute-start.11 = (bf16[128,256]{1,0:T(8,128)(2,1)S(1)}, bf16[128,256]{1,0:T(8,128)(2,1)S(1)}, u32[]{:S(2)}, u32[]{:S(2)}) collective-permute-start(bf16[128,256]{1,0:T(8,128)(2,1)S(1)} %shard_map.81.mine), channel_id=1, source_target_pairs={{0,1},{1,0},{2,3},{3,2},{4,5},{5,4},{6,7},{7,6},{8,9},{9,8},{10,11... | collective-permute-start | bytes 196616 | tf_op jit(solution)/shard_map/ppermute | solution.py:282

commit v4 on v3

--- a/solution.py
+++ b/solution.py
@@ -58,25 +58,26 @@
     )(*args)
 
 
-def pack(values, tops, sums, out_ref):
+def pack(values, tops, sums):
     rows = iota((STATS, values.shape[1]), 0)
     stats = jnp.zeros((STATS, values.shape[1]), F32)
     for j in range(2):
         high = sums[j].astype(BF16).astype(F32)
         for row, value in ((j, tops[j]), (2 + 2 * j, high), (3 + 2 * j, sums[j] - high)):
             stats = jnp.where(rows == row, value, stats)
-    out_ref[:PAIR] = values.astype(BF16)
-    out_ref[PAIR:] = stats.astype(BF16)
-
-
-def sides_kernel(rows, cols, kv_ref, queries_ref, own, queries, near_ref, far_ref, wide, sem):
-    copies = [
-        pltpu.make_async_copy(kv_ref, own, sem.at[0]),
-        pltpu.make_async_copy(queries_ref, queries, sem.at[1]),
-    ]
+    return jnp.concatenate([values, stats], axis=0)
+
+
+def sides_kernel(rows, cols, kv_ref, queries_ref, pole_ref, sea_ref, own, queries, near_ref, far_ref, closed_ref,
+                 wide, pole, sea, sem):
+    pairs = ((pole_ref, pole), (sea_ref, sea), (kv_ref, own), (queries_ref, queries))
+    copies = [pltpu.make_async_copy(*pair, sem.at[k]) for k, pair in enumerate(pairs)]
     for copy in copies:
         copy.start()
     copies[0].wait()
+    copies[1].wait()
+    closed_ref[...] = jnp.broadcast_to(closed_tiles(rows, cols, pole, sea), closed_ref.shape)
+    copies[2].wait()
     odd = lax.axis_index("lon") % 2 == 1
     for k in range(2):
         for lane in range(0, own.shape[2], 128):
@@ -87,7 +88,7 @@
                 high = wide[pl.ds(cols - RADIUS + c, rows, stride=cols)]
                 near_ref[k, c * rows : (c + 1) * rows, lanes] = jnp.where(odd, low, high).astype(BF16)
                 far_ref[k, c * rows : (c + 1) * rows, lanes] = jnp.where(odd, high, low).astype(BF16)
-    copies[1].wait()
+    copies[3].wait()
 
 
 def register_kernel(own, other, queries, out_ref):
@@ -106,7 +107,7 @@
         tops.append(top)
         parts.append(dot(vals, weights.astype(BF16), TN))
     upper = iota(parts[0].shape, 0) < HEAD_DIM
-    pack(jnp.where(upper, parts[0], parts[1]), tops, sums, out_ref)
+    out_ref[...] = pack(jnp.where(upper, parts[0], parts[1]), tops, sums).astype(BF16)
 
 
 def merge_kernel(bits, last, *refs):
@@ -141,13 +142,15 @@
     if last:
         out_ref[...] = (merged / jnp.where(upper, sums[0], sums[1])).astype(BF16)
     else:
-        pack(merged, tops, sums, out_ref)
+        out_ref[...] = pack(merged, tops, sums).astype(BF16)
 
 
 def segments(rows, cols):
-    return (
+    inner = (
         (rows, cols, False, 0, 0),
         (RADIUS, cols, False, "core", 0),
+    )
+    outer = (
         (RADIUS, rows, True, 0, "a"),
         (RADIUS, rows, True, 0, "b"),
         (RADIUS, DEEP, True, "core deep", "a"),
@@ -156,6 +159,11 @@
         (RADIUS, DEEP, True, "cross deep", "a"),
         (RADIUS, DEEP, True, "cross deep", "b"),
     )
+    return inner, outer
+
+
+def count(parts):
+    return sum(part[0] * part[1] for part in parts)
 
 
 def closed_tiles(rows, cols, pole, sea):
@@ -176,7 +184,7 @@
     return closed
 
 
-def masks(rows, cols, closed):
+def masks(rows, cols, closed, parts):
     lat, lon = lax.axis_index("lat"), lax.axis_index("lon")
     across = cols // TILE
     lat_odd, lon_odd = lat % 2 == 1, lon % 2 == 1
@@ -190,7 +198,7 @@
         "b": jnp.where(lon_odd, cols, -RADIUS),
     }
     lane = iota((1, AUG), 1)
-    for slow, fast, fast_rows, row, col in segments(rows, cols):
+    for slow, fast, fast_rows, row, col in parts:
         index = iota((slow * fast, AUG), 0)
         outer, inner = index >> (fast.bit_length() - 1), index & (fast - 1)
         row = starts[row] + (inner if fast_rows else outer)
@@ -202,69 +210,81 @@
         yield jnp.where(far, MASKED, value).astype(BF16)
 
 
-def near_kernel(rows, cols, q_ref, own, core, a, b, corner, cross, reg_keys, pole_ref, sea_ref,
-                acc_ref, scale_ref, reg_ref, kbuf, vbuf, pole, sea, sem):
-    copies = [
-        pltpu.make_async_copy(pole_ref, pole, sem.at[0]),
-        pltpu.make_async_copy(sea_ref, sea, sem.at[1]),
-    ]
-    for copy in copies:
-        copy.start()
-    cells = vbuf.shape[0]
-    lat = lax.axis_index("lat")
-    taken = pl.ds(pl.multiple_of(jnp.where(lat % 2 == 0, 0, (rows - RADIUS) * cols), 16), RADIUS * cols)
+def fill(kbuf, vbuf, blocks, mask_blocks):
+    ahead = kbuf.shape[1] - vbuf.shape[0]
     offset = 0
-    for ref, index in ((own, slice(None)), (core, taken), (a, slice(None)), (b, slice(None)),
-                       (corner, slice(None)), (cross, slice(None))):
-        keys, vals = ref[0, index], ref[1, index]
+    for keys, vals in blocks:
         end = offset + keys.shape[0]
         for p in range(2):
-            kbuf[p, offset:end, :PAIR] = keys[:, p * PAIR : (p + 1) * PAIR]
+            kbuf[p, ahead + offset : ahead + end, :PAIR] = keys[:, p * PAIR : (p + 1) * PAIR]
         vbuf[offset:end] = vals
         offset = end
-    for p in range(2):
-        kbuf[p, cells:, :PAIR] = reg_keys[:, p * PAIR : (p + 1) * PAIR]
-        kbuf[p, cells:, PAIR:] = jnp.zeros((NREG, AUG), BF16)
-    for copy in copies:
-        copy.wait()
-    offset = 0
-    for mask in masks(rows, cols, closed_tiles(rows, cols, pole, sea)):
+    offset = ahead
+    for mask in mask_blocks:
         for p in range(2):
             kbuf[p, offset : offset + mask.shape[0], PAIR:] = mask
         offset += mask.shape[0]
-    count = rows * cols
-    query = iota((count, AUG), 0)
-    lane = iota((count, AUG), 1)
+
+
+def attend(rows, cols, q_ref, kbuf, vbuf):
+    size, ahead = rows * cols, kbuf.shape[1] - vbuf.shape[0]
+    query = iota((size, AUG), 0)
+    lane = iota((size, AUG), 1)
     tiles = (rows // TILE + 2) * (cols // TILE + 2)
     hot = (lane == query >> (cols.bit_length() - 1)) | (lane - rows == query & (cols - 1))
     hot = hot | ((lane >= rows + cols) & (lane < rows + cols + tiles))
     hot = jnp.where(hot, 1.0, 0.0).astype(BF16)
-    first = iota((count, PAIR), 1) < HEAD_DIM
+    first = iota((size, PAIR), 1) < HEAD_DIM
     for p in range(2):
-        scaled = q_ref[:, p * PAIR : (p + 1) * PAIR] * jnp.asarray(SCALE, BF16)
-        mixed, totals = [], []
+        lanes = slice(p * PAIR, (p + 1) * PAIR)
+        scaled = q_ref[:, lanes] * jnp.asarray(SCALE, BF16)
+        tops, totals, mixed, weights = [], [], [], []
         for j in range(2):
             mine = jnp.where(first == (j == 0), scaled, jnp.zeros_like(scaled))
             scores = dot(jnp.concatenate([mine, hot], axis=1), kbuf[p], NT)
-            weights = jnp.exp(scores - jnp.max(scores, axis=1, keepdims=True))
-            totals.append(jnp.sum(weights, axis=1, keepdims=True))
-            rounded = weights.astype(BF16)
-            reg_ref[2 * p + j] = rounded[:, cells:]
-            mixed.append(
-                jnp.dot(rounded[:, :cells], vbuf[:, p * PAIR : (p + 1) * PAIR], preferred_element_type=F32)
-            )
-        acc_ref[:, p * PAIR : (p + 1) * PAIR] = jnp.where(first, *mixed)
-        scale_ref[:, p * PAIR : (p + 1) * PAIR] = 1.0 / jnp.where(first, *totals)
-
-
-def final_kernel(acc, scale, reg_weights, mine, other, out_ref, reg_out_ref):
+            tops.append(jnp.max(scores, axis=1, keepdims=True))
+            each = jnp.exp(scores - tops[j])
+            totals.append(jnp.sum(each, axis=1, keepdims=True))
+            weights.append(each.astype(BF16))
+            mixed.append(jnp.dot(weights[j][:, ahead:], vbuf[:, lanes], preferred_element_type=F32))
+        yield p, lanes, *(jnp.where(first, *x) for x in (tops, totals, mixed)), weights
+
+
+def inner_kernel(rows, cols, q_ref, own, core, reg_keys, closed_ref,
+                 mixed_ref, top_ref, total_ref, reg_ref, kbuf, vbuf):
+    first = jnp.where(lax.axis_index("lat") % 2 == 0, 0, (rows - RADIUS) * cols)
+    taken = pl.ds(pl.multiple_of(first, 16), RADIUS * cols)
+    blocks = [(own[0], own[1]), (core[0, taken], core[1, taken])]
+    fill(kbuf, vbuf, blocks, masks(rows, cols, closed_ref[:1], segments(rows, cols)[0]))
+    for p in range(2):
+        kbuf[p, :NREG, :PAIR] = reg_keys[:, p * PAIR : (p + 1) * PAIR]
+        kbuf[p, :NREG, PAIR:] = jnp.zeros((NREG, AUG), BF16)
+    for p, lanes, top, total, mixed, weights in attend(rows, cols, q_ref, kbuf, vbuf):
+        top_ref[:, lanes], total_ref[:, lanes], mixed_ref[:, lanes] = top, total, mixed
+        for j in range(2):
+            reg_ref[2 * p + j] = weights[j][:, :NREG]
+
+
+def outer_kernel(rows, cols, q_ref, a, b, corner, cross, inner_top, inner_total, closed_ref,
+                 rest_ref, factor_ref, kbuf, vbuf):
+    blocks = [(ref[0], ref[1]) for ref in (a, b, corner, cross)]
+    fill(kbuf, vbuf, blocks, masks(rows, cols, closed_ref[:1], segments(rows, cols)[1]))
+    for _, lanes, top, total, mixed, _ in attend(rows, cols, q_ref, kbuf, vbuf):
+        highest = jnp.maximum(top, inner_top[:, lanes])
+        inner, outer = jnp.exp(inner_top[:, lanes] - highest), jnp.exp(top - highest)
+        scale = 1.0 / (inner * inner_total[:, lanes] + outer * total)
+        factor_ref[:, lanes] = inner * scale
+        rest_ref[:, lanes] = mixed * (outer * scale)
+
+
+def final_kernel(inner, factor, rest, reg_weights, mine, other, out_ref, reg_out_ref):
     here = half() == 0
-    first = iota((acc.shape[0], PAIR), 1) < HEAD_DIM
+    first = iota((inner.shape[0], PAIR), 1) < HEAD_DIM
     for p in range(2):
         lanes = slice(p * PAIR, (p + 1) * PAIR)
         vals = jnp.where(here == (p == 0), mine[...], other[...])
         added = jnp.where(first, dot(reg_weights[2 * p], vals, NT), dot(reg_weights[2 * p + 1], vals, NT))
-        out_ref[:, lanes] = ((acc[:, lanes] + added) * scale[:, lanes]).astype(BF16)
+        out_ref[:, lanes] = ((inner[:, lanes] + added) * factor[:, lanes] + rest[:, lanes]).astype(BF16)
         reg_out_ref[:, lanes] = vals.astype(F32).T.astype(BF16)
 
 
@@ -286,12 +306,24 @@
     core = swap(key_values, 1)
 
     side = jax.ShapeDtypeStruct((2, RADIUS * rows, channels), BF16)
-    own, reg_queries, near_cols, far_cols = call(
+    inputs = (key_values, reg_queries, pole_mask, sea_mask)
+    own, reg_queries, near_cols, far_cols, closed = call(
         functools.partial(sides_kernel, rows, cols),
-        (jax.ShapeDtypeStruct(key_values.shape, BF16), jax.ShapeDtypeStruct(reg_queries.shape, BF16), side, side),
-        tuple(pltpu.with_memory_space_constraint(x, pltpu.HBM) for x in (key_values, reg_queries)),
-        [HBM] * 2,
-        scratch=[pltpu.VMEM((cells, 128), F32), pltpu.SemaphoreType.DMA((2,))],
+        (
+            jax.ShapeDtypeStruct(key_values.shape, BF16),
+            jax.ShapeDtypeStruct(reg_queries.shape, BF16),
+            side,
+            side,
+            jax.ShapeDtypeStruct((8, AUG), F32),
+        ),
+        tuple(pltpu.with_memory_space_constraint(x, pltpu.HBM) for x in inputs),
+        [HBM] * 4,
+        scratch=[
+            pltpu.VMEM((cells, 128), F32),
+            pltpu.SMEM(pole_mask.shape, jnp.int32),
+            pltpu.SMEM(sea_mask.shape, jnp.int32),
+            pltpu.SemaphoreType.DMA((4,)),
+        ],
     )
     side_a = swap(near_cols, lats)
     side_b = lax.ppermute(
@@ -306,7 +338,23 @@
         flops=4 * 2 * cells * NREG * 2 * PAIR,
     )
 
+    queries = queries.reshape(cells, channels)
+    square = jax.ShapeDtypeStruct((cells, channels), F32)
+    inner, outer = (count(parts) for parts in segments(rows, cols))
+    mixed, top, total, reg_weights = call(
+        functools.partial(inner_kernel, rows, cols),
+        (square, square, square, jax.ShapeDtypeStruct((HEADS, cells, NREG), BF16)),
+        (queries, own, core, reg_keys, closed),
+        [VMEM] * 5,
+        scratch=[
+            pltpu.VMEM((2, inner + NREG, PAIR + AUG), BF16),
+            pltpu.VMEM((inner, channels), BF16),
+        ],
+        flops=2 * 2 * cells * inner * channels * 2,
+    )
+
     side_a, side_b, _ = lax.optimization_barrier((side_a, side_b, payload))
+
     def take(shard, size, start, count):
         taken = lax.dynamic_slice_in_dim(shard.reshape(2, -1, size, channels), start, count, 2)
         return taken.reshape(2, -1, channels)
@@ -325,45 +373,26 @@
         ),
         3,
     )
-    keys = sum(segment[0] * segment[1] for segment in segments(rows, cols))
-    square = jax.ShapeDtypeStruct((cells, channels), F32)
-    acc, scale, reg_weights = call(
-        functools.partial(near_kernel, rows, cols),
-        (square, square, jax.ShapeDtypeStruct((HEADS, cells, NREG), BF16)),
-        (
-            queries.reshape(cells, channels),
-            own,
-            core,
-            side_a,
-            side_b,
-            corner,
-            cross,
-            reg_keys,
-            pole_mask,
-            sea_mask,
-        ),
-        [VMEM] * 8 + [HBM] * 2,
-        scratch=[
-            pltpu.VMEM((2, keys + NREG, PAIR + AUG), BF16),
-            pltpu.VMEM((keys, channels), BF16),
-            pltpu.SMEM(pole_mask.shape, jnp.int32),
-            pltpu.SMEM(sea_mask.shape, jnp.int32),
-            pltpu.SemaphoreType.DMA((2,)),
-        ],
-        flops=2 * 2 * cells * keys * channels * 2,
-        limit=32,
-    )
-    stages = [tuple(range(b, min(b + 2, nbits))) for b in range(1, nbits, 2)]
+    rest, factor = call(
+        functools.partial(outer_kernel, rows, cols),
+        (square, square),
+        (queries, side_a, side_b, corner, cross, top, total, closed),
+        [VMEM] * 8,
+        scratch=[pltpu.VMEM((2, outer, PAIR + AUG), BF16), pltpu.VMEM((outer, channels), BF16)],
+        flops=2 * 2 * cells * outer * channels * 2,
+    )
+
+    stages = [tuple(range(b, min(b + 2, nbits))) for b in range(3, nbits, 2)] + [(1, 2)]
     for stage in stages:
+        first, last = stage is stages[0], stage is stages[-1]
         gathered = [payload]
         for chosen in range(1, 1 << len(stage)):
             flips = [b for k, b in enumerate(stage) if chosen >> k & 1]
             gathered.append(swap(payload, sum(1 << b for b in flips) + len(flips) % 2))
-        last = stage is stages[-1]
+        if first:
+            gathered[0], _ = lax.optimization_barrier((gathered[0], mixed))
         if last:
-            gathered[0], acc, scale, reg_weights = lax.optimization_barrier(
-                (gathered[0], acc, scale, reg_weights)
-            )
+            gathered[0], rest, factor = lax.optimization_barrier((gathered[0], rest, factor))
         payload = call(
             functools.partial(merge_kernel, stage, last),
             jax.ShapeDtypeStruct((PAIR if last else PAIR + STATS, NREG), BF16),
@@ -371,15 +400,14 @@
             [VMEM] * len(gathered),
         )
 
-    other = swap(payload, 1)
     attended, reg_out = call(
         final_kernel,
         (
             jax.ShapeDtypeStruct((cells, channels), BF16),
             jax.ShapeDtypeStruct((NREG, channels), BF16),
         ),
-        (acc, scale, reg_weights, payload, other),
-        [VMEM] * 5,
+        (mixed, factor, rest, reg_weights, payload, swap(payload, 1)),
+        [VMEM] * 6,
         flops=2 * cells * NREG * channels * 2,
     )
     return attended.reshape(rows, cols, channels), reg_out

time: 28.6 us -> 27.5 us (0.962)
  starting transfers between devices: 17.2 us -> 16 us
  waiting for transfers between devices: 3.36 us -> 3.74 us
    ppermute x11, starting transfers between devices: 13.6 us -> 12.5 us  [swap(): return lax.ppermute(x, everyone, [(i, i ^ mask) for i in range(devices)])]
    ppermute x11, waiting for transfers between devices: 3.36 us -> 3.74 us  [swap(): return lax.ppermute(x, everyone, [(i, i ^ mask) for i in range(devices)])]
    pallas_call x6 -> x7, Pallas kernels: 7.03 us -> 6.8 us  [call(): pl.pallas_call(kernel, out_shape=out, in_specs=specs, out_specs=jax.tree....]
  transfers between devices with their start and end apart: 12 -> 12, of which waited for: 3 -> 5; matrix products, arithmetic and copies ran while one was open for 0% -> 0% of each run, Pallas kernels for 21% -> 21%
where the time goes in v4:
time: 27.5 us; the launch traced here: 27.3 us
  starting transfers between devices  16 us (58%)
  Pallas kernels  6.8 us (25%)
  waiting for transfers between devices  3.74 us (14%)
  between operations  0.73 us (3%)
    ppermute x11, starting transfers between devices, swap(): return lax.ppermute(x, everyone, [(i, i ^ mask) for i in range(devices)])  12.5 us
    pallas_call x7, Pallas kernels, call(): pl.pallas_call(kernel, out_shape=out, in_specs=specs, out_specs=jax.tree....  6.8 us
    ppermute x11, waiting for transfers between devices, swap(): return lax.ppermute(x, everyone, [(i, i ^ mask) for i in range(devices)])  3.74 us
    ppermute x1, starting transfers between devices, shards(): lax.ppermute(far_cols, 'lon', [(i, (i + 1 if i % 2 else i - 1) % lons) fo...  3.54 us
  transfers between devices with their start and end apart: 12, of which 5 were waited for; matrix products, arithmetic and copies ran while one was open for 0% of the time, Pallas kernels for 21%

profile of v4, /device:TPU:0, one launch (start us, length us, event | category | flops | bytes accessed | tf_op | source)
XLA Modules:
  0.0 27.3 jit_solution(17775583026909031461)
XLA Ops:
  0.6 0.5 %collective-permute-start = (bf16[2,256,256]{2,1,0:T(8,128)(2,1)}, bf16[2,256,256]{2,1,0:T(8,128)(2,1)S(1)}, u32[]{:S(2)}, u32[]{:S(2)}) collective-permute-start(bf16[2,256,256]{2,1,0:T(8,128)(2,1)} %bitcast.17), channel_id=1, source_target_pairs={{0,1},{1,0},{2,3},{3,2},{4,5},{5,4},{6,7},{7,6},{8,9},{9,8},{10,11... | collective-permute-start | bytes 786440 | tf_op jit(solution)/shard_map/ppermute | solution.py:302
  1.1 1.2 %shard_map.77 = (bf16[2,256,256]{2,1,0:T(8,128)(2,1)S(1)}, bf16[256,256]{1,0:T(8,128)(2,1)S(1)}, bf16[2,96,256]{2,1,0:T(8,128)(2,1)S(1)}, bf16[2,96,256]{2,1,0:T(8,128)(2,1)S(1)}, f32[8,128]{1,0:T(8,128)S(1)}) custom-call(bf16[2,256,256]{2,1,0:T(8,128)(2,1)} %bitcast.18, bf16[256,256]{1,0:T(8,128)(2,1)} %queries_ref.1, s32[8]{0:T(128)} %pole_ref.1, ...), custom_call_target="tpu_custom_call" | custom-call | bytes 393760 | tf_op jit(solution)/shard_map/pallas_call | solution.py:50
  2.3 2.6 %collective-permute-start.4 = (bf16[2,96,256]{2,1,0:T(8,128)(2,1)S(1)}, bf16[2,96,256]{2,1,0:T(8,128)(2,1)S(1)}, u32[]{:S(2)}, u32[]{:S(2)}) collective-permute-start(bf16[2,96,256]{2,1,0:T(8,128)(2,1)S(1)} %get-tuple-element.26), channel_id=1, source_target_pairs={{0,4},{1,5},{2,6},{3,7},{4,0},{5,1},{6,2},{7,3},{8,12},{9,13},{10,... | collective-permute-start | bytes 294920 | tf_op jit(solution)/shard_map/ppermute | solution.py:302
  4.9 3.5 %collective-permute-start.5 = (bf16[2,96,256]{2,1,0:T(8,128)(2,1)S(1)}, bf16[2,96,256]{2,1,0:T(8,128)(2,1)S(1)}, u32[]{:S(2)}, u32[]{:S(2)}) collective-permute-start(bf16[2,96,256]{2,1,0:T(8,128)(2,1)S(1)} %get-tuple-element.27), channel_id=1, source_target_pairs={{0,28},{4,8},{8,4},{12,16},{16,12},{20,24},{24,20},{28,0},{1,29},{... | collective-permute-start | bytes 294920 | tf_op jit(solution)/shard_map/ppermute | solution.py:329
  8.5 1.0 %shard_map.79.refs_0_ = bf16[144,256]{1,0:T(8,128)(2,1)S(1)} custom-call(bf16[2,256,256]{2,1,0:T(8,128)(2,1)S(1)} %get-tuple-element.21.own, bf16[2,256,256]{2,1,0:T(8,128)(2,1)S(1)} %collective-permute-done.core.other, bf16[256,256]{1,0:T(8,128)(2,1)S(1)} %get-tuple-element.24.queries), custom_call_target="tpu_custom_call" | custom-call | flops 134217728 | bytes 655360 | tf_op jit(solution)/shard_map/pallas_call | solution.py:50
  9.5 0.1 collective-permute-start.1
  9.5 0.7 %collective-permute-start.2 = (bf16[144,256]{1,0:T(8,128)(2,1)S(1)}, bf16[144,256]{1,0:T(8,128)(2,1)S(1)}, u32[]{:S(2)}, u32[]{:S(2)}) collective-permute-start(bf16[144,256]{1,0:T(8,128)(2,1)S(1)} %shard_map.79.refs_0_), channel_id=1, source_target_pairs={{0,17},{1,16},{2,19},{3,18},{4,21},{5,20},{6,23},{7,22},{8,25},{9,... | collective-permute-start | bytes 221192 | tf_op jit(solution)/shard_map/ppermute | solution.py:302
  10.3 3.4 %collective-permute-start.3 = (bf16[144,256]{1,0:T(8,128)(2,1)S(1)}, bf16[144,256]{1,0:T(8,128)(2,1)S(1)}, u32[]{:S(2)}, u32[]{:S(2)}) collective-permute-start(bf16[144,256]{1,0:T(8,128)(2,1)S(1)} %shard_map.79.refs_0_), channel_id=1, source_target_pairs={{0,24},{1,25},{2,26},{3,27},{4,28},{5,29},{6,30},{7,31},{8,16},{9,... | collective-permute-start | bytes 221192 | tf_op jit(solution)/shard_map/ppermute | solution.py:302
  13.7 0.8 %collective-permute-start.7 = (bf16[2,192,256]{2,1,0:T(8,128)(2,1)S(1)}, bf16[2,192,256]{2,1,0:T(8,128)(2,1)S(1)}, u32[]{:S(2)}, u32[]{:S(2)}) collective-permute-start(bf16[2,192,256]{2,1,0:T(8,128)(2,1)S(1)} %pad_maximum_fusion), channel_id=1, source_target_pairs={{0,3},{1,2},{2,1},{3,0},{4,7},{5,6},{6,5},{7,4},{8,11},{9,10},{10,... | collective-permute-start | bytes 589832 | tf_op jit(solution)/shard_map/ppermute | solution.py:302
  14.5 0.9 %collective-permute-start.6 = (bf16[2,96,256]{2,1,0:T(8,128)(2,1)S(1)}, bf16[2,96,256]{2,1,0:T(8,128)(2,1)S(1)}, u32[]{:S(2)}, u32[]{:S(2)}) collective-permute-start(bf16[2,96,256]{2,1,0:T(8,128)(2,1)S(1)} %pad_maximum_fusion.1), channel_id=1, source_target_pairs={{0,1},{1,0},{2,3},{3,2},{4,5},{5,4},{6,7},{7,6},{8,9},{9,8},{10,11... | collective-permute-start | bytes 294920 | tf_op jit(solution)/shard_map/ppermute | solution.py:302
  15.5 1.8 %shard_map.78 = (f32[256,256]{1,0:T(8,128)S(1)}, f32[256,256]{1,0:T(8,128)S(1)}, f32[256,256]{1,0:T(8,128)S(1)}, bf16[4,256,256]{2,1,0:T(8,128)(2,1)S(1)}) custom-call(bf16[256,256]{1,0:T(8,128)(2,1)S(1)} %bitcast.13, bf16[2,256,256]{2,1,0:T(8,128)(2,1)S(1)} %get-tuple-element.21.own, bf16[2,256,256]{2,1,0:T(8,128)(2,1)S(1)} %collective-permute-done.core.other, ...), custom_call_target="tpu_custom_call" | custom-call | flops 184549376 | bytes 790528 | tf_op jit(solution)/shard_map/pallas_call | solution.py:50
  17.3 0.8 %collective-permute-done.2.refs_2_ = bf16[144,256]{1,0:T(8,128)(2,1)S(1)} collective-permute-done((bf16[144,256]{1,0:T(8,128)(2,1)S(1)}, bf16[144,256]{1,0:T(8,128)(2,1)S(1)}, u32[]{:S(2)}, u32[]{:S(2)}) %collective-permute-start.2) | collective-permute-done | bytes 73760 | tf_op jit(solution)/shard_map/ppermute | solution.py:302
  18.1 0.1 shard_map.80.refs_0_
  18.3 1.7 %collective-permute-start.10 = (bf16[144,256]{1,0:T(8,128)(2,1)S(1)}, bf16[144,256]{1,0:T(8,128)(2,1)S(1)}, u32[]{:S(2)}, u32[]{:S(2)}) collective-permute-start(bf16[144,256]{1,0:T(8,128)(2,1)S(1)} %shard_map.80.refs_0_), channel_id=1, source_target_pairs={{0,6},{1,7},{2,4},{3,5},{4,2},{5,3},{6,0},{7,1},{8,14},{9,15},{10,... | collective-permute-start | bytes 221192 | tf_op jit(solution)/shard_map/ppermute | solution.py:302
  20.0 0.0 collective-permute-start.8
  20.0 1.5 %collective-permute-start.9 = (bf16[144,256]{1,0:T(8,128)(2,1)S(1)}, bf16[144,256]{1,0:T(8,128)(2,1)S(1)}, u32[]{:S(2)}, u32[]{:S(2)}) collective-permute-start(bf16[144,256]{1,0:T(8,128)(2,1)S(1)} %shard_map.80.refs_0_), channel_id=1, source_target_pairs={{0,5},{1,4},{2,7},{3,6},{4,1},{5,0},{6,3},{7,2},{8,13},{9,12},{10,... | collective-permute-start | bytes 221192 | tf_op jit(solution)/shard_map/ppermute | solution.py:302
  21.5 1.6 %shard_map.81 = (f32[256,256]{1,0:T(8,128)S(1)}, f32[256,256]{1,0:T(8,128)S(1)}) custom-call(bf16[256,256]{1,0:T(8,128)(2,1)S(1)} %bitcast.14, bf16[2,96,256]{2,1,0:T(8,128)(2,1)S(1)} %collective-permute-done.4.a, bf16[2,96,256]{2,1,0:T(8,128)(2,1)S(1)} %collective-permute-done.5.b, bf16[2,96,256]{2,1,0:T(8,128)(2,1)S(1)} %collective-permute-done.6.corner, ...), custom_call_target="tpu_custom_call" | custom-call | flops 251658240 | bytes 1150976 | tf_op jit(solution)/shard_map/pallas_call | solution.py:50
  23.2 0.5 %collective-permute-done.10.refs_3_ = bf16[144,256]{1,0:T(8,128)(2,1)S(1)} collective-permute-done((bf16[144,256]{1,0:T(8,128)(2,1)S(1)}, bf16[144,256]{1,0:T(8,128)(2,1)S(1)}, u32[]{:S(2)}, u32[]{:S(2)}) %collective-permute-start.10) | collective-permute-done | bytes 73760 | tf_op jit(solution)/shard_map/ppermute | solution.py:302
  23.6 0.9 %collective-permute-done.8.refs_1_ = bf16[144,256]{1,0:T(8,128)(2,1)S(1)} collective-permute-done((bf16[144,256]{1,0:T(8,128)(2,1)S(1)}, bf16[144,256]{1,0:T(8,128)(2,1)S(1)}, u32[]{:S(2)}, u32[]{:S(2)}) %collective-permute-start.8) | collective-permute-done | bytes 73760 | tf_op jit(solution)/shard_map/ppermute | solution.py:302
  24.5 0.4 %collective-permute-done.9.refs_2_ = bf16[144,256]{1,0:T(8,128)(2,1)S(1)} collective-permute-done((bf16[144,256]{1,0:T(8,128)(2,1)S(1)}, bf16[144,256]{1,0:T(8,128)(2,1)S(1)}, u32[]{:S(2)}, u32[]{:S(2)}) %collective-permute-start.9) | collective-permute-done | bytes 73760 | tf_op jit(solution)/shard_map/ppermute | solution.py:302
  24.9 0.1 shard_map.82.mine
  25.0 0.2 collective-permute-start.11
  25.2 1.1 %collective-permute-done.11.other = bf16[128,256]{1,0:T(8,128)(2,1)S(1)} collective-permute-done((bf16[128,256]{1,0:T(8,128)(2,1)S(1)}, bf16[128,256]{1,0:T(8,128)(2,1)S(1)}, u32[]{:S(2)}, u32[]{:S(2)}) %collective-permute-start.11) | collective-permute-done | bytes 65568 | tf_op jit(solution)/shard_map/ppermute | solution.py:302
  26.4 1.0 %shard_map.83 = (bf16[256,256]{1,0:T(8,128)(2,1)}, bf16[256,256]{1,0:T(8,128)(2,1)}) custom-call(f32[256,256]{1,0:T(8,128)S(1)} %get-tuple-element.23.inner, f32[256,256]{1,0:T(8,128)S(1)} %get-tuple-element.34.factor, f32[256,256]{1,0:T(8,128)S(1)} %get-tuple-element.35.rest, bf16[4,256,256]{2,1,0:T(8,128)(2,1)S(1)} %get-tuple-element.36.reg_weights, ...), custom_call_target="tpu_custom_call" | custom-call | flops 67108864 | bytes 1441792 | tf_op jit(solution)/shard_map/pallas_call | solution.py:50
  (15 shorter events, 0.1 us)
Async XLA Ops:
  0.6 7.8 %collective-permute-start = (bf16[2,256,256]{2,1,0:T(8,128)(2,1)}, bf16[2,256,256]{2,1,0:T(8,128)(2,1)S(1)}, u32[]{:S(2)}, u32[]{:S(2)}) collective-permute-start(bf16[2,256,256]{2,1,0:T(8,128)(2,1)} %bitcast.17), channel_id=1, source_target_pairs={{0,1},{1,0},{2,3},{3,2},{4,5},{5,4},{6,7},{7,6},{8,9},{9,8},{10,11... | collective-permute-start | bytes 786440 | tf_op jit(solution)/shard_map/ppermute | solution.py:302
  2.3 11.3 %collective-permute-start.4 = (bf16[2,96,256]{2,1,0:T(8,128)(2,1)S(1)}, bf16[2,96,256]{2,1,0:T(8,128)(2,1)S(1)}, u32[]{:S(2)}, u32[]{:S(2)}) collective-permute-start(bf16[2,96,256]{2,1,0:T(8,128)(2,1)S(1)} %get-tuple-element.26), channel_id=1, source_target_pairs={{0,4},{1,5},{2,6},{3,7},{4,0},{5,1},{6,2},{7,3},{8,12},{9,13},{10,... | collective-permute-start | bytes 294920 | tf_op jit(solution)/shard_map/ppermute | solution.py:302
  4.9 8.7 %collective-permute-start.5 = (bf16[2,96,256]{2,1,0:T(8,128)(2,1)S(1)}, bf16[2,96,256]{2,1,0:T(8,128)(2,1)S(1)}, u32[]{:S(2)}, u32[]{:S(2)}) collective-permute-start(bf16[2,96,256]{2,1,0:T(8,128)(2,1)S(1)} %get-tuple-element.27), channel_id=1, source_target_pairs={{0,28},{4,8},{8,4},{12,16},{16,12},{20,24},{24,20},{28,0},{1,29},{... | collective-permute-start | bytes 294920 | tf_op jit(solution)/shard_map/ppermute | solution.py:329
  9.5 7.8 %collective-permute-start.1 = (bf16[144,256]{1,0:T(8,128)(2,1)S(1)}, bf16[144,256]{1,0:T(8,128)(2,1)S(1)}, u32[]{:S(2)}, u32[]{:S(2)}) collective-permute-start(bf16[144,256]{1,0:T(8,128)(2,1)S(1)} %shard_map.79.refs_0_), channel_id=1, source_target_pairs={{0,9},{1,8},{2,11},{3,10},{4,13},{5,12},{6,15},{7,14},{8,1},{9,0},... | collective-permute-start | bytes 221192 | tf_op jit(solution)/shard_map/ppermute | solution.py:302
  9.5 8.6 %collective-permute-start.2 = (bf16[144,256]{1,0:T(8,128)(2,1)S(1)}, bf16[144,256]{1,0:T(8,128)(2,1)S(1)}, u32[]{:S(2)}, u32[]{:S(2)}) collective-permute-start(bf16[144,256]{1,0:T(8,128)(2,1)S(1)} %shard_map.79.refs_0_), channel_id=1, source_target_pairs={{0,17},{1,16},{2,19},{3,18},{4,21},{5,20},{6,23},{7,22},{8,25},{9,... | collective-permute-start | bytes 221192 | tf_op jit(solution)/shard_map/ppermute | solution.py:302
  10.3 7.9 %collective-permute-start.3 = (bf16[144,256]{1,0:T(8,128)(2,1)S(1)}, bf16[144,256]{1,0:T(8,128)(2,1)S(1)}, u32[]{:S(2)}, u32[]{:S(2)}) collective-permute-start(bf16[144,256]{1,0:T(8,128)(2,1)S(1)} %shard_map.79.refs_0_), channel_id=1, source_target_pairs={{0,24},{1,25},{2,26},{3,27},{4,28},{5,29},{6,30},{7,31},{8,16},{9,... | collective-permute-start | bytes 221192 | tf_op jit(solution)/shard_map/ppermute | solution.py:302
  13.7 1.8 %copy-start.1 = (bf16[256,256]{1,0:T(8,128)(2,1)S(1)}, bf16[256,256]{1,0:T(8,128)(2,1)}, u32[]{:S(2)}) copy-start(bf16[256,256]{1,0:T(8,128)(2,1)} %reg_keys.1) | copy-start | bytes 393220
  13.7 1.8 %copy-start = (bf16[16,16,256]{2,1,0:T(8,128)(2,1)S(1)}, bf16[16,16,256]{2,1,0:T(8,128)(2,1)}, u32[]{:S(2)}) copy-start(bf16[16,16,256]{2,1,0:T(8,128)(2,1)} %param.6) | copy-start | bytes 393220
  13.7 7.8 %collective-permute-start.7 = (bf16[2,192,256]{2,1,0:T(8,128)(2,1)S(1)}, bf16[2,192,256]{2,1,0:T(8,128)(2,1)S(1)}, u32[]{:S(2)}, u32[]{:S(2)}) collective-permute-start(bf16[2,192,256]{2,1,0:T(8,128)(2,1)S(1)} %pad_maximum_fusion), channel_id=1, source_target_pairs={{0,3},{1,2},{2,1},{3,0},{4,7},{5,6},{6,5},{7,4},{8,11},{9,10},{10,... | collective-permute-start | bytes 589832 | tf_op jit(solution)/shard_map/ppermute | solution.py:302
  14.5 7.0 %collective-permute-start.6 = (bf16[2,96,256]{2,1,0:T(8,128)(2,1)S(1)}, bf16[2,96,256]{2,1,0:T(8,128)(2,1)S(1)}, u32[]{:S(2)}, u32[]{:S(2)}) collective-permute-start(bf16[2,96,256]{2,1,0:T(8,128)(2,1)S(1)} %pad_maximum_fusion.1), channel_id=1, source_target_pairs={{0,1},{1,0},{2,3},{3,2},{4,5},{5,4},{6,7},{7,6},{8,9},{9,8},{10,11... | collective-permute-start | bytes 294920 | tf_op jit(solution)/shard_map/ppermute | solution.py:302
  18.3 5.4 %collective-permute-start.10 = (bf16[144,256]{1,0:T(8,128)(2,1)S(1)}, bf16[144,256]{1,0:T(8,128)(2,1)S(1)}, u32[]{:S(2)}, u32[]{:S(2)}) collective-permute-start(bf16[144,256]{1,0:T(8,128)(2,1)S(1)} %shard_map.80.refs_0_), channel_id=1, source_target_pairs={{0,6},{1,7},{2,4},{3,5},{4,2},{5,3},{6,0},{7,1},{8,14},{9,15},{10,... | collective-permute-start | bytes 221192 | tf_op jit(solution)/shard_map/ppermute | solution.py:302
  20.0 4.5 %collective-permute-start.8 = (bf16[144,256]{1,0:T(8,128)(2,1)S(1)}, bf16[144,256]{1,0:T(8,128)(2,1)S(1)}, u32[]{:S(2)}, u32[]{:S(2)}) collective-permute-start(bf16[144,256]{1,0:T(8,128)(2,1)S(1)} %shard_map.80.refs_0_), channel_id=1, source_target_pairs={{0,3},{1,2},{2,1},{3,0},{4,7},{5,6},{6,5},{7,4},{8,11},{9,10},{10,... | collective-permute-start | bytes 221192 | tf_op jit(solution)/shard_map/ppermute | solution.py:302
  20.0 4.9 %collective-permute-start.9 = (bf16[144,256]{1,0:T(8,128)(2,1)S(1)}, bf16[144,256]{1,0:T(8,128)(2,1)S(1)}, u32[]{:S(2)}, u32[]{:S(2)}) collective-permute-start(bf16[144,256]{1,0:T(8,128)(2,1)S(1)} %shard_map.80.refs_0_), channel_id=1, source_target_pairs={{0,5},{1,4},{2,7},{3,6},{4,1},{5,0},{6,3},{7,2},{8,13},{9,12},{10,... | collective-permute-start | bytes 221192 | tf_op jit(solution)/shard_map/ppermute | solution.py:302
  25.0 1.3 %collective-permute-start.11 = (bf16[128,256]{1,0:T(8,128)(2,1)S(1)}, bf16[128,256]{1,0:T(8,128)(2,1)S(1)}, u32[]{:S(2)}, u32[]{:S(2)}) collective-permute-start(bf16[128,256]{1,0:T(8,128)(2,1)S(1)} %shard_map.82.mine), channel_id=1, source_target_pairs={{0,1},{1,0},{2,3},{3,2},{4,5},{5,4},{6,7},{7,6},{8,9},{9,8},{10,11... | collective-permute-start | bytes 196616 | tf_op jit(solution)/shard_map/ppermute | solution.py:302

commit v5 on v4

--- a/solution.py
+++ b/solution.py
@@ -14,7 +14,7 @@
 TILE = 8
 PAIR = 2 * HEAD_DIM
 DEEP = 8
-STATS = 16
+STATS = 8
 AUG = 128
 MASKED = -8192.0
 SCALE = HEAD_DIM ** (-0.5)
@@ -97,17 +97,16 @@
     vals = jnp.concatenate([own[1, :, lanes], other[1, :, lanes]], axis=0)
     scaled = queries[:, lanes] * jnp.asarray(SCALE, BF16)
     first = iota(scaled.shape, 1) < HEAD_DIM
+    asked = [jnp.where(first == (j == 0), scaled, jnp.zeros_like(scaled)) for j in range(2)]
+    scores = [dot(keys, each, NT) for each in asked]
     parts, tops, sums = [], [], []
     for j in range(2):
-        mine = jnp.where(first == (j == 0), scaled, jnp.zeros_like(scaled))
-        scores = dot(keys, mine, NT)
-        top = jnp.max(scores, axis=0, keepdims=True).astype(BF16).astype(F32)
-        weights = jnp.exp(scores - top)
+        top = jnp.max(scores[j], axis=0, keepdims=True).astype(BF16).astype(F32)
+        weights = jnp.exp(scores[j] - top)
         sums.append(jnp.sum(weights, axis=0, keepdims=True))
         tops.append(top)
-        parts.append(dot(vals, weights.astype(BF16), TN))
-    upper = iota(parts[0].shape, 0) < HEAD_DIM
-    out_ref[...] = pack(jnp.where(upper, parts[0], parts[1]), tops, sums).astype(BF16)
+        parts.append(dot(vals[:, j * HEAD_DIM : (j + 1) * HEAD_DIM], weights.astype(BF16), TN))
+    out_ref[...] = pack(jnp.concatenate(parts, axis=0), tops, sums).astype(BF16)
 
 
 def merge_kernel(bits, last, *refs):

time: 27.5 us -> 26.7 us (0.971)
  waiting for transfers between devices: 3.74 us -> 3.27 us
  Pallas kernels: 6.8 us -> 6.48 us
    ppermute x11, waiting for transfers between devices: 3.74 us -> 3.27 us  [swap(): return lax.ppermute(x, everyone, [(i, i ^ mask) for i in range(devices)])]
    pallas_call x7, Pallas kernels: 6.8 us -> 6.48 us  [call(): pl.pallas_call(kernel, out_shape=out, in_specs=specs, out_specs=jax.tree....]
  transfers between devices with their start and end apart: 12 -> 12, of which waited for: 5 -> 5; matrix products, arithmetic and copies ran while one was open for 0% -> 0% of each run, Pallas kernels for 21% -> 20%
where the time goes in v5:
time: 26.7 us; the launch traced here: 26.6 us
  starting transfers between devices  16 us (60%)
  Pallas kernels  6.48 us (24%)
  waiting for transfers between devices  3.27 us (12%)
  between operations  0.72 us (3%)
    ppermute x11, starting transfers between devices, swap(): return lax.ppermute(x, everyone, [(i, i ^ mask) for i in range(devices)])  12.5 us
    pallas_call x7, Pallas kernels, call(): pl.pallas_call(kernel, out_shape=out, in_specs=specs, out_specs=jax.tree....  6.48 us
    ppermute x1, starting transfers between devices, shards(): lax.ppermute(far_cols, 'lon', [(i, (i + 1 if i % 2 else i - 1) % lons) fo...  3.54 us
    ppermute x11, waiting for transfers between devices, swap(): return lax.ppermute(x, everyone, [(i, i ^ mask) for i in range(devices)])  3.27 us
  transfers between devices with their start and end apart: 12, of which 5 were waited for; matrix products, arithmetic and copies ran while one was open for 0% of the time, Pallas kernels for 20%

profile of v5, /device:TPU:0, one launch (start us, length us, event | category | flops | bytes accessed | tf_op | source)
XLA Modules:
  0.0 26.6 jit_solution(5045104185267426580)
XLA Ops:
  0.6 0.5 %collective-permute-start = (bf16[2,256,256]{2,1,0:T(8,128)(2,1)}, bf16[2,256,256]{2,1,0:T(8,128)(2,1)S(1)}, u32[]{:S(2)}, u32[]{:S(2)}) collective-permute-start(bf16[2,256,256]{2,1,0:T(8,128)(2,1)} %bitcast.17), channel_id=1, source_target_pairs={{0,1},{1,0},{2,3},{3,2},{4,5},{5,4},{6,7},{7,6},{8,9},{9,8},{10,11... | collective-permute-start | bytes 786440 | tf_op jit(solution)/shard_map/ppermute | solution.py:301
  1.1 1.2 %shard_map.77 = (bf16[2,256,256]{2,1,0:T(8,128)(2,1)S(1)}, bf16[256,256]{1,0:T(8,128)(2,1)S(1)}, bf16[2,96,256]{2,1,0:T(8,128)(2,1)S(1)}, bf16[2,96,256]{2,1,0:T(8,128)(2,1)S(1)}, f32[8,128]{1,0:T(8,128)S(1)}) custom-call(bf16[2,256,256]{2,1,0:T(8,128)(2,1)} %bitcast.18, bf16[256,256]{1,0:T(8,128)(2,1)} %queries_ref.1, s32[8]{0:T(128)} %pole_ref.1, ...), custom_call_target="tpu_custom_call" | custom-call | bytes 393760 | tf_op jit(solution)/shard_map/pallas_call | solution.py:50
  2.3 2.6 %collective-permute-start.4 = (bf16[2,96,256]{2,1,0:T(8,128)(2,1)S(1)}, bf16[2,96,256]{2,1,0:T(8,128)(2,1)S(1)}, u32[]{:S(2)}, u32[]{:S(2)}) collective-permute-start(bf16[2,96,256]{2,1,0:T(8,128)(2,1)S(1)} %get-tuple-element.26), channel_id=1, source_target_pairs={{0,4},{1,5},{2,6},{3,7},{4,0},{5,1},{6,2},{7,3},{8,12},{9,13},{10,... | collective-permute-start | bytes 294920 | tf_op jit(solution)/shard_map/ppermute | solution.py:301
  4.9 3.5 %collective-permute-start.5 = (bf16[2,96,256]{2,1,0:T(8,128)(2,1)S(1)}, bf16[2,96,256]{2,1,0:T(8,128)(2,1)S(1)}, u32[]{:S(2)}, u32[]{:S(2)}) collective-permute-start(bf16[2,96,256]{2,1,0:T(8,128)(2,1)S(1)} %get-tuple-element.27), channel_id=1, source_target_pairs={{0,28},{4,8},{8,4},{12,16},{16,12},{20,24},{24,20},{28,0},{1,29},{... | collective-permute-start | bytes 294920 | tf_op jit(solution)/shard_map/ppermute | solution.py:328
  8.5 0.7 %shard_map.79.refs_0_ = bf16[136,256]{1,0:T(8,128)(2,1)S(1)} custom-call(bf16[2,256,256]{2,1,0:T(8,128)(2,1)S(1)} %get-tuple-element.21.own, bf16[2,256,256]{2,1,0:T(8,128)(2,1)S(1)} %collective-permute-done.core.other, bf16[256,256]{1,0:T(8,128)(2,1)S(1)} %get-tuple-element.24.queries), custom_call_target="tpu_custom_call" | custom-call | flops 134217728 | bytes 655360 | tf_op jit(solution)/shard_map/pallas_call | solution.py:50
  9.2 0.1 collective-permute-start.1
  9.2 0.7 %collective-permute-start.2 = (bf16[136,256]{1,0:T(8,128)(2,1)S(1)}, bf16[136,256]{1,0:T(8,128)(2,1)S(1)}, u32[]{:S(2)}, u32[]{:S(2)}) collective-permute-start(bf16[136,256]{1,0:T(8,128)(2,1)S(1)} %shard_map.79.refs_0_), channel_id=1, source_target_pairs={{0,17},{1,16},{2,19},{3,18},{4,21},{5,20},{6,23},{7,22},{8,25},{9,... | collective-permute-start | bytes 208904 | tf_op jit(solution)/shard_map/ppermute | solution.py:301
  10.0 3.4 %collective-permute-start.3 = (bf16[136,256]{1,0:T(8,128)(2,1)S(1)}, bf16[136,256]{1,0:T(8,128)(2,1)S(1)}, u32[]{:S(2)}, u32[]{:S(2)}) collective-permute-start(bf16[136,256]{1,0:T(8,128)(2,1)S(1)} %shard_map.79.refs_0_), channel_id=1, source_target_pairs={{0,24},{1,25},{2,26},{3,27},{4,28},{5,29},{6,30},{7,31},{8,16},{9,... | collective-permute-start | bytes 208904 | tf_op jit(solution)/shard_map/ppermute | solution.py:301
  13.4 0.0 copy-start.1
  13.4 0.8 %collective-permute-start.7 = (bf16[2,192,256]{2,1,0:T(8,128)(2,1)S(1)}, bf16[2,192,256]{2,1,0:T(8,128)(2,1)S(1)}, u32[]{:S(2)}, u32[]{:S(2)}) collective-permute-start(bf16[2,192,256]{2,1,0:T(8,128)(2,1)S(1)} %pad_maximum_fusion), channel_id=1, source_target_pairs={{0,3},{1,2},{2,1},{3,0},{4,7},{5,6},{6,5},{7,4},{8,11},{9,10},{10,... | collective-permute-start | bytes 589832 | tf_op jit(solution)/shard_map/ppermute | solution.py:301
  14.2 0.9 %collective-permute-start.6 = (bf16[2,96,256]{2,1,0:T(8,128)(2,1)S(1)}, bf16[2,96,256]{2,1,0:T(8,128)(2,1)S(1)}, u32[]{:S(2)}, u32[]{:S(2)}) collective-permute-start(bf16[2,96,256]{2,1,0:T(8,128)(2,1)S(1)} %pad_maximum_fusion.1), channel_id=1, source_target_pairs={{0,1},{1,0},{2,3},{3,2},{4,5},{5,4},{6,7},{7,6},{8,9},{9,8},{10,11... | collective-permute-start | bytes 294920 | tf_op jit(solution)/shard_map/ppermute | solution.py:301
  15.2 1.8 %shard_map.78 = (f32[256,256]{1,0:T(8,128)S(1)}, f32[256,256]{1,0:T(8,128)S(1)}, f32[256,256]{1,0:T(8,128)S(1)}, bf16[4,256,256]{2,1,0:T(8,128)(2,1)S(1)}) custom-call(bf16[256,256]{1,0:T(8,128)(2,1)S(1)} %bitcast.13, bf16[2,256,256]{2,1,0:T(8,128)(2,1)S(1)} %get-tuple-element.21.own, bf16[2,256,256]{2,1,0:T(8,128)(2,1)S(1)} %collective-permute-done.core.other, ...), custom_call_target="tpu_custom_call" | custom-call | flops 184549376 | bytes 790528 | tf_op jit(solution)/shard_map/pallas_call | solution.py:50
  17.0 0.6 %collective-permute-done.2.refs_2_ = bf16[136,256]{1,0:T(8,128)(2,1)S(1)} collective-permute-done((bf16[136,256]{1,0:T(8,128)(2,1)S(1)}, bf16[136,256]{1,0:T(8,128)(2,1)S(1)}, u32[]{:S(2)}, u32[]{:S(2)}) %collective-permute-start.2) | collective-permute-done | bytes 69664 | tf_op jit(solution)/shard_map/ppermute | solution.py:301
  17.5 0.1 shard_map.80.refs_0_
  17.7 1.8 %collective-permute-start.10 = (bf16[136,256]{1,0:T(8,128)(2,1)S(1)}, bf16[136,256]{1,0:T(8,128)(2,1)S(1)}, u32[]{:S(2)}, u32[]{:S(2)}) collective-permute-start(bf16[136,256]{1,0:T(8,128)(2,1)S(1)} %shard_map.80.refs_0_), channel_id=1, source_target_pairs={{0,6},{1,7},{2,4},{3,5},{4,2},{5,3},{6,0},{7,1},{8,14},{9,15},{10,... | collective-permute-start | bytes 208904 | tf_op jit(solution)/shard_map/ppermute | solution.py:301
  19.5 1.5 %collective-permute-start.9 = (bf16[136,256]{1,0:T(8,128)(2,1)S(1)}, bf16[136,256]{1,0:T(8,128)(2,1)S(1)}, u32[]{:S(2)}, u32[]{:S(2)}) collective-permute-start(bf16[136,256]{1,0:T(8,128)(2,1)S(1)} %shard_map.80.refs_0_), channel_id=1, source_target_pairs={{0,5},{1,4},{2,7},{3,6},{4,1},{5,0},{6,3},{7,2},{8,13},{9,12},{10,... | collective-permute-start | bytes 208904 | tf_op jit(solution)/shard_map/ppermute | solution.py:301
  21.0 1.6 %shard_map.81 = (f32[256,256]{1,0:T(8,128)S(1)}, f32[256,256]{1,0:T(8,128)S(1)}) custom-call(bf16[256,256]{1,0:T(8,128)(2,1)S(1)} %bitcast.14, bf16[2,96,256]{2,1,0:T(8,128)(2,1)S(1)} %collective-permute-done.4.a, bf16[2,96,256]{2,1,0:T(8,128)(2,1)S(1)} %collective-permute-done.5.b, bf16[2,96,256]{2,1,0:T(8,128)(2,1)S(1)} %collective-permute-done.6.corner, ...), custom_call_target="tpu_custom_call" | custom-call | flops 251658240 | bytes 1150976 | tf_op jit(solution)/shard_map/pallas_call | solution.py:50
  22.6 0.4 %collective-permute-done.10.refs_3_ = bf16[136,256]{1,0:T(8,128)(2,1)S(1)} collective-permute-done((bf16[136,256]{1,0:T(8,128)(2,1)S(1)}, bf16[136,256]{1,0:T(8,128)(2,1)S(1)}, u32[]{:S(2)}, u32[]{:S(2)}) %collective-permute-start.10) | collective-permute-done | bytes 69664 | tf_op jit(solution)/shard_map/ppermute | solution.py:301
  23.0 0.9 %collective-permute-done.8.refs_1_ = bf16[136,256]{1,0:T(8,128)(2,1)S(1)} collective-permute-done((bf16[136,256]{1,0:T(8,128)(2,1)S(1)}, bf16[136,256]{1,0:T(8,128)(2,1)S(1)}, u32[]{:S(2)}, u32[]{:S(2)}) %collective-permute-start.8) | collective-permute-done | bytes 69664 | tf_op jit(solution)/shard_map/ppermute | solution.py:301
  23.9 0.2 collective-permute-done.9.refs_2_
  24.1 0.1 shard_map.82.mine
  24.3 0.2 collective-permute-start.11
  24.5 1.1 %collective-permute-done.11.other = bf16[128,256]{1,0:T(8,128)(2,1)S(1)} collective-permute-done((bf16[128,256]{1,0:T(8,128)(2,1)S(1)}, bf16[128,256]{1,0:T(8,128)(2,1)S(1)}, u32[]{:S(2)}, u32[]{:S(2)}) %collective-permute-start.11) | collective-permute-done | bytes 65568 | tf_op jit(solution)/shard_map/ppermute | solution.py:301
  25.6 1.0 %shard_map.83 = (bf16[256,256]{1,0:T(8,128)(2,1)}, bf16[256,256]{1,0:T(8,128)(2,1)}) custom-call(f32[256,256]{1,0:T(8,128)S(1)} %get-tuple-element.23.inner, f32[256,256]{1,0:T(8,128)S(1)} %get-tuple-element.34.factor, f32[256,256]{1,0:T(8,128)S(1)} %get-tuple-element.35.rest, bf16[4,256,256]{2,1,0:T(8,128)(2,1)S(1)} %get-tuple-element.36.reg_weights, ...), custom_call_target="tpu_custom_call" | custom-call | flops 67108864 | bytes 1441792 | tf_op jit(solution)/shard_map/pallas_call | solution.py:50
  (15 shorter events, 0.1 us)
Async XLA Ops:
  0.6 7.8 %collective-permute-start = (bf16[2,256,256]{2,1,0:T(8,128)(2,1)}, bf16[2,256,256]{2,1,0:T(8,128)(2,1)S(1)}, u32[]{:S(2)}, u32[]{:S(2)}) collective-permute-start(bf16[2,256,256]{2,1,0:T(8,128)(2,1)} %bitcast.17), channel_id=1, source_target_pairs={{0,1},{1,0},{2,3},{3,2},{4,5},{5,4},{6,7},{7,6},{8,9},{9,8},{10,11... | collective-permute-start | bytes 786440 | tf_op jit(solution)/shard_map/ppermute | solution.py:301
  2.3 11.0 %collective-permute-start.4 = (bf16[2,96,256]{2,1,0:T(8,128)(2,1)S(1)}, bf16[2,96,256]{2,1,0:T(8,128)(2,1)S(1)}, u32[]{:S(2)}, u32[]{:S(2)}) collective-permute-start(bf16[2,96,256]{2,1,0:T(8,128)(2,1)S(1)} %get-tuple-element.26), channel_id=1, source_target_pairs={{0,4},{1,5},{2,6},{3,7},{4,0},{5,1},{6,2},{7,3},{8,12},{9,13},{10,... | collective-permute-start | bytes 294920 | tf_op jit(solution)/shard_map/ppermute | solution.py:301
  4.9 8.4 %collective-permute-start.5 = (bf16[2,96,256]{2,1,0:T(8,128)(2,1)S(1)}, bf16[2,96,256]{2,1,0:T(8,128)(2,1)S(1)}, u32[]{:S(2)}, u32[]{:S(2)}) collective-permute-start(bf16[2,96,256]{2,1,0:T(8,128)(2,1)S(1)} %get-tuple-element.27), channel_id=1, source_target_pairs={{0,28},{4,8},{8,4},{12,16},{16,12},{20,24},{24,20},{28,0},{1,29},{... | collective-permute-start | bytes 294920 | tf_op jit(solution)/shard_map/ppermute | solution.py:328
  9.2 7.8 %collective-permute-start.1 = (bf16[136,256]{1,0:T(8,128)(2,1)S(1)}, bf16[136,256]{1,0:T(8,128)(2,1)S(1)}, u32[]{:S(2)}, u32[]{:S(2)}) collective-permute-start(bf16[136,256]{1,0:T(8,128)(2,1)S(1)} %shard_map.79.refs_0_), channel_id=1, source_target_pairs={{0,9},{1,8},{2,11},{3,10},{4,13},{5,12},{6,15},{7,14},{8,1},{9,0},... | collective-permute-start | bytes 208904 | tf_op jit(solution)/shard_map/ppermute | solution.py:301
  9.2 8.3 %collective-permute-start.2 = (bf16[136,256]{1,0:T(8,128)(2,1)S(1)}, bf16[136,256]{1,0:T(8,128)(2,1)S(1)}, u32[]{:S(2)}, u32[]{:S(2)}) collective-permute-start(bf16[136,256]{1,0:T(8,128)(2,1)S(1)} %shard_map.79.refs_0_), channel_id=1, source_target_pairs={{0,17},{1,16},{2,19},{3,18},{4,21},{5,20},{6,23},{7,22},{8,25},{9,... | collective-permute-start | bytes 208904 | tf_op jit(solution)/shard_map/ppermute | solution.py:301
  10.0 7.6 %collective-permute-start.3 = (bf16[136,256]{1,0:T(8,128)(2,1)S(1)}, bf16[136,256]{1,0:T(8,128)(2,1)S(1)}, u32[]{:S(2)}, u32[]{:S(2)}) collective-permute-start(bf16[136,256]{1,0:T(8,128)(2,1)S(1)} %shard_map.79.refs_0_), channel_id=1, source_target_pairs={{0,24},{1,25},{2,26},{3,27},{4,28},{5,29},{6,30},{7,31},{8,16},{9,... | collective-permute-start | bytes 208904 | tf_op jit(solution)/shard_map/ppermute | solution.py:301
  13.4 1.8 %copy-start.1 = (bf16[256,256]{1,0:T(8,128)(2,1)S(1)}, bf16[256,256]{1,0:T(8,128)(2,1)}, u32[]{:S(2)}) copy-start(bf16[256,256]{1,0:T(8,128)(2,1)} %reg_keys.1) | copy-start | bytes 393220
  13.4 1.8 %copy-start = (bf16[16,16,256]{2,1,0:T(8,128)(2,1)S(1)}, bf16[16,16,256]{2,1,0:T(8,128)(2,1)}, u32[]{:S(2)}) copy-start(bf16[16,16,256]{2,1,0:T(8,128)(2,1)} %param.6) | copy-start | bytes 393220
  13.4 7.6 %collective-permute-start.7 = (bf16[2,192,256]{2,1,0:T(8,128)(2,1)S(1)}, bf16[2,192,256]{2,1,0:T(8,128)(2,1)S(1)}, u32[]{:S(2)}, u32[]{:S(2)}) collective-permute-start(bf16[2,192,256]{2,1,0:T(8,128)(2,1)S(1)} %pad_maximum_fusion), channel_id=1, source_target_pairs={{0,3},{1,2},{2,1},{3,0},{4,7},{5,6},{6,5},{7,4},{8,11},{9,10},{10,... | collective-permute-start | bytes 589832 | tf_op jit(solution)/shard_map/ppermute | solution.py:301
  14.2 6.7 %collective-permute-start.6 = (bf16[2,96,256]{2,1,0:T(8,128)(2,1)S(1)}, bf16[2,96,256]{2,1,0:T(8,128)(2,1)S(1)}, u32[]{:S(2)}, u32[]{:S(2)}) collective-permute-start(bf16[2,96,256]{2,1,0:T(8,128)(2,1)S(1)} %pad_maximum_fusion.1), channel_id=1, source_target_pairs={{0,1},{1,0},{2,3},{3,2},{4,5},{5,4},{6,7},{7,6},{8,9},{9,8},{10,11... | collective-permute-start | bytes 294920 | tf_op jit(solution)/shard_map/ppermute | solution.py:301
  17.7 5.3 %collective-permute-start.10 = (bf16[136,256]{1,0:T(8,128)(2,1)S(1)}, bf16[136,256]{1,0:T(8,128)(2,1)S(1)}, u32[]{:S(2)}, u32[]{:S(2)}) collective-permute-start(bf16[136,256]{1,0:T(8,128)(2,1)S(1)} %shard_map.80.refs_0_), channel_id=1, source_target_pairs={{0,6},{1,7},{2,4},{3,5},{4,2},{5,3},{6,0},{7,1},{8,14},{9,15},{10,... | collective-permute-start | bytes 208904 | tf_op jit(solution)/shard_map/ppermute | solution.py:301
  19.4 4.4 %collective-permute-start.8 = (bf16[136,256]{1,0:T(8,128)(2,1)S(1)}, bf16[136,256]{1,0:T(8,128)(2,1)S(1)}, u32[]{:S(2)}, u32[]{:S(2)}) collective-permute-start(bf16[136,256]{1,0:T(8,128)(2,1)S(1)} %shard_map.80.refs_0_), channel_id=1, source_target_pairs={{0,3},{1,2},{2,1},{3,0},{4,7},{5,6},{6,5},{7,4},{8,11},{9,10},{10,... | collective-permute-start | bytes 208904 | tf_op jit(solution)/shard_map/ppermute | solution.py:301
  19.5 4.7 %collective-permute-start.9 = (bf16[136,256]{1,0:T(8,128)(2,1)S(1)}, bf16[136,256]{1,0:T(8,128)(2,1)S(1)}, u32[]{:S(2)}, u32[]{:S(2)}) collective-permute-start(bf16[136,256]{1,0:T(8,128)(2,1)S(1)} %shard_map.80.refs_0_), channel_id=1, source_target_pairs={{0,5},{1,4},{2,7},{3,6},{4,1},{5,0},{6,3},{7,2},{8,13},{9,12},{10,... | collective-permute-start | bytes 208904 | tf_op jit(solution)/shard_map/ppermute | solution.py:301
  24.3 1.3 %collective-permute-start.11 = (bf16[128,256]{1,0:T(8,128)(2,1)S(1)}, bf16[128,256]{1,0:T(8,128)(2,1)S(1)}, u32[]{:S(2)}, u32[]{:S(2)}) collective-permute-start(bf16[128,256]{1,0:T(8,128)(2,1)S(1)} %shard_map.82.mine), channel_id=1, source_target_pairs={{0,1},{1,0},{2,3},{3,2},{4,5},{5,4},{6,7},{7,6},{8,9},{9,8},{10,11... | collective-permute-start | bytes 196616 | tf_op jit(solution)/shard_map/ppermute | solution.py:301

commit v6 on v5

--- a/solution.py
+++ b/solution.py
@@ -99,22 +99,24 @@
     first = iota(scaled.shape, 1) < HEAD_DIM
     asked = [jnp.where(first == (j == 0), scaled, jnp.zeros_like(scaled)) for j in range(2)]
     scores = [dot(keys, each, NT) for each in asked]
+    ones = jnp.ones((keys.shape[0], HEAD_DIM), BF16)
     parts, tops, sums = [], [], []
     for j in range(2):
         top = jnp.max(scores[j], axis=0, keepdims=True).astype(BF16).astype(F32)
-        weights = jnp.exp(scores[j] - top)
-        sums.append(jnp.sum(weights, axis=0, keepdims=True))
         tops.append(top)
-        parts.append(dot(vals[:, j * HEAD_DIM : (j + 1) * HEAD_DIM], weights.astype(BF16), TN))
+        weights = jnp.exp(scores[j] - top).astype(BF16)
+        both = dot(jnp.concatenate([vals[:, j * HEAD_DIM : (j + 1) * HEAD_DIM], ones], axis=1), weights, TN)
+        parts.append(both[:HEAD_DIM])
+        sums.append(both[HEAD_DIM : HEAD_DIM + 1])
     out_ref[...] = pack(jnp.concatenate(parts, axis=0), tops, sums).astype(BF16)
 
 
-def merge_kernel(bits, last, *refs):
+def merge_kernel(stages, last, *refs):
     payloads, out_ref = refs[:-1], refs[-1]
     here = place()
     found = [(r[:PAIR].astype(F32), r[PAIR:].astype(F32)) for r in payloads]
-    for level, bit in enumerate(bits):
-        swap = here[bit] == 1
+    for level, (first, second) in enumerate(zip(*stages)):
+        swap = jnp.where(half() == 0, here[first], here[second]) == 1
         step = 1 << level
         for low in range(len(found)):
             if not low & step:
@@ -294,6 +296,7 @@
     assert lats == 4 and lons & (lons - 1) == 0 and lons > 1
     assert rows & (rows - 1) == 0 and cols & (cols - 1) == 0 and rows % TILE == 0 and cols % TILE == 0 and TILE == DEEP == 8
     nbits = devices.bit_length() - 1
+    assert nbits % 2 == 1
     lat = lax.axis_index("lat")
     everyone = ("lon", "lat")
 
@@ -352,7 +355,7 @@
         flops=2 * 2 * cells * inner * channels * 2,
     )
 
-    side_a, side_b, _ = lax.optimization_barrier((side_a, side_b, payload))
+    side_a, side_b, _, _ = lax.optimization_barrier((side_a, side_b, payload, mixed))
 
     def take(shard, size, start, count):
         taken = lax.dynamic_slice_in_dim(shard.reshape(2, -1, size, channels), start, count, 2)
@@ -362,7 +365,7 @@
     corner = swap(
         jnp.concatenate([take(s, rows, core_deep, DEEP) for s in (side_a, side_b)], axis=1), 1
     )
-    cross = swap(
+    cross = lax.ppermute(
         jnp.concatenate(
             [
                 take(own, cells, (lat % 2) * (rows - RADIUS) * cols, RADIUS * cols),
@@ -370,7 +373,8 @@
             ],
             axis=1,
         ),
-        3,
+        everyone,
+        [(i, i ^ 3 if i % lats in (1, 2) else i ^ 2 * lats) for i in range(devices)],
     )
     rest, factor = call(
         functools.partial(outer_kernel, rows, cols),
@@ -381,19 +385,23 @@
         flops=2 * 2 * cells * outer * channels * 2,
     )
 
-    stages = [tuple(range(b, min(b + 2, nbits))) for b in range(3, nbits, 2)] + [(1, 2)]
-    for stage in stages:
-        first, last = stage is stages[0], stage is stages[-1]
+    near_bits, far_bits = (1, 2), [(b, b + 1) for b in range(3, nbits, 2)]
+    steps = list(zip([*far_bits, near_bits], [near_bits, *far_bits]))
+    for step in steps:
+        first, last = step is steps[0], step is steps[-1]
         gathered = [payload]
-        for chosen in range(1, 1 << len(stage)):
-            flips = [b for k, b in enumerate(stage) if chosen >> k & 1]
-            gathered.append(swap(payload, sum(1 << b for b in flips) + len(flips) % 2))
+        for chosen in range(1, 4):
+            pairs = []
+            for i in range(devices):
+                flips = [b for k, b in enumerate(step[bin(i).count("1") % 2]) if chosen >> k & 1]
+                pairs.append((i, i ^ (sum(1 << b for b in flips) + len(flips) % 2)))
+            gathered.append(lax.ppermute(payload, everyone, pairs))
         if first:
             gathered[0], _ = lax.optimization_barrier((gathered[0], mixed))
         if last:
             gathered[0], rest, factor = lax.optimization_barrier((gathered[0], rest, factor))
         payload = call(
-            functools.partial(merge_kernel, stage, last),
+            functools.partial(merge_kernel, step, last),
             jax.ShapeDtypeStruct((PAIR if last else PAIR + STATS, NREG), BF16),
             tuple(gathered),
             [VMEM] * len(gathered),

time: 26.7 us -> 26 us (0.974)
  starting transfers between devices: 16 us -> 15.2 us
    ppermute x11 -> x4, starting transfers between devices: 12.5 us -> 4.16 us  [swap(): return lax.ppermute(x, everyone, [(i, i ^ mask) for i in range(devices)])]
    ppermute x0 -> x7, starting transfers between devices: none -> 7.51 us  [the longest x6 7.44 us: shards(): gathered.append(lax.ppermute(payload, everyone, pairs))]
    ppermute x11 -> x4, waiting for transfers between devices: 3.27 us -> 1.03 us  [swap(): return lax.ppermute(x, everyone, [(i, i ^ mask) for i in range(devices)])]
    ppermute x0 -> x7, waiting for transfers between devices: none -> 2.22 us  [the longest x1 1.92 us: shards(): lax.ppermute(jnp.concatenate([take(own, cells, lat % 2 * (rows - RADIUS)...]
  transfers between devices with their start and end apart: 12 -> 12, of which waited for: 5 -> 3; matrix products, arithmetic and copies ran while one was open for 0% -> 0% of each run, Pallas kernels for 20% -> 21%
where the time goes in v6:
time: 26 us; the launch traced here: 25.8 us
  starting transfers between devices  15.2 us (58%)
  Pallas kernels  6.51 us (25%)
  waiting for transfers between devices  3.25 us (12%)
  between operations  0.78 us (3%)
    ppermute x6, starting transfers between devices, shards(): gathered.append(lax.ppermute(payload, everyone, pairs))  7.44 us
    pallas_call x7, Pallas kernels, call(): pl.pallas_call(kernel, out_shape=out, in_specs=specs, out_specs=jax.tree....  6.51 us
    ppermute x4, starting transfers between devices, swap(): return lax.ppermute(x, everyone, [(i, i ^ mask) for i in range(devices)])  4.16 us
    ppermute x1, starting transfers between devices, shards(): lax.ppermute(far_cols, 'lon', [(i, (i + 1 if i % 2 else i - 1) % lons) fo...  3.54 us
    ppermute x1, waiting for transfers between devices, shards(): lax.ppermute(jnp.concatenate([take(own, cells, lat % 2 * (rows - RADIUS)...  1.92 us
    ppermute x4, waiting for transfers between devices, swap(): return lax.ppermute(x, everyone, [(i, i ^ mask) for i in range(devices)])  1.03 us
  transfers between devices with their start and end apart: 12, of which 3 were waited for; matrix products, arithmetic and copies ran while one was open for 0% of the time, Pallas kernels for 21%

profile of v6, /device:TPU:0, one launch (start us, length us, event | category | flops | bytes accessed | tf_op | source)
XLA Modules:
  0.0 25.8 jit_solution(1713660156673965961)
XLA Ops:
  0.6 0.5 %collective-permute-start = (bf16[2,256,256]{2,1,0:T(8,128)(2,1)}, bf16[2,256,256]{2,1,0:T(8,128)(2,1)S(1)}, u32[]{:S(2)}, u32[]{:S(2)}) collective-permute-start(bf16[2,256,256]{2,1,0:T(8,128)(2,1)} %bitcast.17), channel_id=1, source_target_pairs={{0,1},{1,0},{2,3},{3,2},{4,5},{5,4},{6,7},{7,6},{8,9},{9,8},{10,11... | collective-permute-start | bytes 786440 | tf_op jit(solution)/shard_map/ppermute | solution.py:304
  1.1 1.2 %shard_map.77 = (bf16[2,256,256]{2,1,0:T(8,128)(2,1)S(1)}, bf16[256,256]{1,0:T(8,128)(2,1)S(1)}, bf16[2,96,256]{2,1,0:T(8,128)(2,1)S(1)}, bf16[2,96,256]{2,1,0:T(8,128)(2,1)S(1)}, f32[8,128]{1,0:T(8,128)S(1)}) custom-call(bf16[2,256,256]{2,1,0:T(8,128)(2,1)} %bitcast.18, bf16[256,256]{1,0:T(8,128)(2,1)} %queries_ref.1, s32[8]{0:T(128)} %pole_ref.1, ...), custom_call_target="tpu_custom_call" | custom-call | bytes 393760 | tf_op jit(solution)/shard_map/pallas_call | solution.py:50
  2.3 2.6 %collective-permute-start.4 = (bf16[2,96,256]{2,1,0:T(8,128)(2,1)S(1)}, bf16[2,96,256]{2,1,0:T(8,128)(2,1)S(1)}, u32[]{:S(2)}, u32[]{:S(2)}) collective-permute-start(bf16[2,96,256]{2,1,0:T(8,128)(2,1)S(1)} %get-tuple-element.26), channel_id=1, source_target_pairs={{0,4},{1,5},{2,6},{3,7},{4,0},{5,1},{6,2},{7,3},{8,12},{9,13},{10,... | collective-permute-start | bytes 294920 | tf_op jit(solution)/shard_map/ppermute | solution.py:304
  4.9 3.5 %collective-permute-start.5 = (bf16[2,96,256]{2,1,0:T(8,128)(2,1)S(1)}, bf16[2,96,256]{2,1,0:T(8,128)(2,1)S(1)}, u32[]{:S(2)}, u32[]{:S(2)}) collective-permute-start(bf16[2,96,256]{2,1,0:T(8,128)(2,1)S(1)} %get-tuple-element.27), channel_id=1, source_target_pairs={{0,28},{4,8},{8,4},{12,16},{16,12},{20,24},{24,20},{28,0},{1,29},{... | collective-permute-start | bytes 294920 | tf_op jit(solution)/shard_map/ppermute | solution.py:331
  8.5 0.0 collective-permute-done.core.other
  8.5 0.0 copy-start
  8.5 0.0 copy-start.1
  8.5 0.7 %shard_map.79.refs_0_ = bf16[136,256]{1,0:T(8,128)(2,1)S(1)} custom-call(bf16[2,256,256]{2,1,0:T(8,128)(2,1)S(1)} %get-tuple-element.21.own, bf16[2,256,256]{2,1,0:T(8,128)(2,1)S(1)} %collective-permute-done.core.other, bf16[256,256]{1,0:T(8,128)(2,1)S(1)} %get-tuple-element.24.queries), custom_call_target="tpu_custom_call" | custom-call | flops 134217728 | bytes 655360 | tf_op jit(solution)/shard_map/pallas_call | solution.py:50
  9.2 0.1 collective-permute-start.1
  9.2 0.7 %collective-permute-start.2 = (bf16[136,256]{1,0:T(8,128)(2,1)S(1)}, bf16[136,256]{1,0:T(8,128)(2,1)S(1)}, u32[]{:S(2)}, u32[]{:S(2)}) collective-permute-start(bf16[136,256]{1,0:T(8,128)(2,1)S(1)} %shard_map.79.refs_0_), channel_id=1, source_target_pairs={{0,17},{1,4},{2,7},{3,18},{4,1},{5,20},{6,23},{7,2},{8,13},{9,24},... | collective-permute-start | bytes 208904 | tf_op jit(solution)/shard_map/ppermute | solution.py:398
  10.0 3.4 %collective-permute-start.3 = (bf16[136,256]{1,0:T(8,128)(2,1)S(1)}, bf16[136,256]{1,0:T(8,128)(2,1)S(1)}, u32[]{:S(2)}, u32[]{:S(2)}) collective-permute-start(bf16[136,256]{1,0:T(8,128)(2,1)S(1)} %shard_map.79.refs_0_), channel_id=1, source_target_pairs={{0,24},{1,7},{2,4},{3,27},{4,2},{5,29},{6,30},{7,1},{8,14},{9,17},... | collective-permute-start | bytes 208904 | tf_op jit(solution)/shard_map/ppermute | solution.py:398
  13.3 1.8 %shard_map.78 = (f32[256,256]{1,0:T(8,128)S(1)}, f32[256,256]{1,0:T(8,128)S(1)}, f32[256,256]{1,0:T(8,128)S(1)}, bf16[4,256,256]{2,1,0:T(8,128)(2,1)S(1)}) custom-call(bf16[256,256]{1,0:T(8,128)(2,1)S(1)} %bitcast.13, bf16[2,256,256]{2,1,0:T(8,128)(2,1)S(1)} %get-tuple-element.21.own, bf16[2,256,256]{2,1,0:T(8,128)(2,1)S(1)} %collective-permute-done.core.other, ...), custom_call_target="tpu_custom_call" | custom-call | flops 184549376 | bytes 790528 | tf_op jit(solution)/shard_map/pallas_call | solution.py:50
  15.2 0.1 collective-permute-start.7
  15.3 0.7 %collective-permute-start.6 = (bf16[2,96,256]{2,1,0:T(8,128)(2,1)S(1)}, bf16[2,96,256]{2,1,0:T(8,128)(2,1)S(1)}, u32[]{:S(2)}, u32[]{:S(2)}) collective-permute-start(bf16[2,96,256]{2,1,0:T(8,128)(2,1)S(1)} %pad_maximum_fusion.1), channel_id=1, source_target_pairs={{0,1},{1,0},{2,3},{3,2},{4,5},{5,4},{6,7},{7,6},{8,9},{9,8},{10,11... | collective-permute-start | bytes 294920 | tf_op jit(solution)/shard_map/ppermute | solution.py:304
  16.1 0.3 %collective-permute-done.3.refs_3_ = bf16[136,256]{1,0:T(8,128)(2,1)S(1)} collective-permute-done((bf16[136,256]{1,0:T(8,128)(2,1)S(1)}, bf16[136,256]{1,0:T(8,128)(2,1)S(1)}, u32[]{:S(2)}, u32[]{:S(2)}) %collective-permute-start.3) | collective-permute-done | bytes 69664 | tf_op jit(solution)/shard_map/ppermute | solution.py:398
  16.4 0.1 shard_map.80.refs_0_
  16.5 2.0 %collective-permute-start.10 = (bf16[136,256]{1,0:T(8,128)(2,1)S(1)}, bf16[136,256]{1,0:T(8,128)(2,1)S(1)}, u32[]{:S(2)}, u32[]{:S(2)}) collective-permute-start(bf16[136,256]{1,0:T(8,128)(2,1)S(1)} %shard_map.80.refs_0_), channel_id=1, source_target_pairs={{0,6},{1,25},{2,26},{3,5},{4,28},{5,3},{6,0},{7,31},{8,16},{9,15},... | collective-permute-start | bytes 208904 | tf_op jit(solution)/shard_map/ppermute | solution.py:398
  18.5 1.2 %collective-permute-start.9 = (bf16[136,256]{1,0:T(8,128)(2,1)S(1)}, bf16[136,256]{1,0:T(8,128)(2,1)S(1)}, u32[]{:S(2)}, u32[]{:S(2)}) collective-permute-start(bf16[136,256]{1,0:T(8,128)(2,1)S(1)} %shard_map.80.refs_0_), channel_id=1, source_target_pairs={{0,5},{1,16},{2,19},{3,6},{4,21},{5,0},{6,3},{7,22},{8,25},{9,12},... | collective-permute-start | bytes 208904 | tf_op jit(solution)/shard_map/ppermute | solution.py:398
  19.8 1.9 %collective-permute-done.7.cross = bf16[2,192,256]{2,1,0:T(8,128)(2,1)S(1)} collective-permute-done((bf16[2,192,256]{2,1,0:T(8,128)(2,1)S(1)}, bf16[2,192,256]{2,1,0:T(8,128)(2,1)S(1)}, u32[]{:S(2)}, u32[]{:S(2)}) %collective-permute-start.7) | collective-permute-done | bytes 196640 | tf_op jit(solution)/shard_map/ppermute | solution.py:368
  21.7 1.6 %shard_map.81 = (f32[256,256]{1,0:T(8,128)S(1)}, f32[256,256]{1,0:T(8,128)S(1)}) custom-call(bf16[256,256]{1,0:T(8,128)(2,1)S(1)} %bitcast.14, bf16[2,96,256]{2,1,0:T(8,128)(2,1)S(1)} %collective-permute-done.4.a, bf16[2,96,256]{2,1,0:T(8,128)(2,1)S(1)} %collective-permute-done.5.b, bf16[2,96,256]{2,1,0:T(8,128)(2,1)S(1)} %collective-permute-done.6.corner, ...), custom_call_target="tpu_custom_call" | custom-call | flops 251658240 | bytes 1150976 | tf_op jit(solution)/shard_map/pallas_call | solution.py:50
  23.4 0.1 shard_map.82.mine
  23.5 0.3 %collective-permute-start.11 = (bf16[128,256]{1,0:T(8,128)(2,1)S(1)}, bf16[128,256]{1,0:T(8,128)(2,1)S(1)}, u32[]{:S(2)}, u32[]{:S(2)}) collective-permute-start(bf16[128,256]{1,0:T(8,128)(2,1)S(1)} %shard_map.82.mine), channel_id=1, source_target_pairs={{0,1},{1,0},{2,3},{3,2},{4,5},{5,4},{6,7},{7,6},{8,9},{9,8},{10,11... | collective-permute-start | bytes 196616 | tf_op jit(solution)/shard_map/ppermute | solution.py:304
  23.8 1.0 %collective-permute-done.11.other = bf16[128,256]{1,0:T(8,128)(2,1)S(1)} collective-permute-done((bf16[128,256]{1,0:T(8,128)(2,1)S(1)}, bf16[128,256]{1,0:T(8,128)(2,1)S(1)}, u32[]{:S(2)}, u32[]{:S(2)}) %collective-permute-start.11) | collective-permute-done | bytes 65568 | tf_op jit(solution)/shard_map/ppermute | solution.py:304
  24.8 1.0 %shard_map.83 = (bf16[256,256]{1,0:T(8,128)(2,1)}, bf16[256,256]{1,0:T(8,128)(2,1)}) custom-call(f32[256,256]{1,0:T(8,128)S(1)} %get-tuple-element.23.inner, f32[256,256]{1,0:T(8,128)S(1)} %get-tuple-element.34.factor, f32[256,256]{1,0:T(8,128)S(1)} %get-tuple-element.35.rest, bf16[4,256,256]{2,1,0:T(8,128)(2,1)S(1)} %get-tuple-element.36.reg_weights, ...), custom_call_target="tpu_custom_call" | custom-call | flops 67108864 | bytes 1441792 | tf_op jit(solution)/shard_map/pallas_call | solution.py:50
  (15 shorter events, 0.1 us)
Async XLA Ops:
  0.6 7.8 %collective-permute-start = (bf16[2,256,256]{2,1,0:T(8,128)(2,1)}, bf16[2,256,256]{2,1,0:T(8,128)(2,1)S(1)}, u32[]{:S(2)}, u32[]{:S(2)}) collective-permute-start(bf16[2,256,256]{2,1,0:T(8,128)(2,1)} %bitcast.17), channel_id=1, source_target_pairs={{0,1},{1,0},{2,3},{3,2},{4,5},{5,4},{6,7},{7,6},{8,9},{9,8},{10,11... | collective-permute-start | bytes 786440 | tf_op jit(solution)/shard_map/ppermute | solution.py:304
  2.3 12.8 %collective-permute-start.4 = (bf16[2,96,256]{2,1,0:T(8,128)(2,1)S(1)}, bf16[2,96,256]{2,1,0:T(8,128)(2,1)S(1)}, u32[]{:S(2)}, u32[]{:S(2)}) collective-permute-start(bf16[2,96,256]{2,1,0:T(8,128)(2,1)S(1)} %get-tuple-element.26), channel_id=1, source_target_pairs={{0,4},{1,5},{2,6},{3,7},{4,0},{5,1},{6,2},{7,3},{8,12},{9,13},{10,... | collective-permute-start | bytes 294920 | tf_op jit(solution)/shard_map/ppermute | solution.py:304
  4.9 10.3 %collective-permute-start.5 = (bf16[2,96,256]{2,1,0:T(8,128)(2,1)S(1)}, bf16[2,96,256]{2,1,0:T(8,128)(2,1)S(1)}, u32[]{:S(2)}, u32[]{:S(2)}) collective-permute-start(bf16[2,96,256]{2,1,0:T(8,128)(2,1)S(1)} %get-tuple-element.27), channel_id=1, source_target_pairs={{0,28},{4,8},{8,4},{12,16},{16,12},{20,24},{24,20},{28,0},{1,29},{... | collective-permute-start | bytes 294920 | tf_op jit(solution)/shard_map/ppermute | solution.py:331
  8.5 4.9 %copy-start = (bf16[16,16,256]{2,1,0:T(8,128)(2,1)S(1)}, bf16[16,16,256]{2,1,0:T(8,128)(2,1)}, u32[]{:S(2)}) copy-start(bf16[16,16,256]{2,1,0:T(8,128)(2,1)} %param.6) | copy-start | bytes 393220
  8.5 4.9 %copy-start.1 = (bf16[256,256]{1,0:T(8,128)(2,1)S(1)}, bf16[256,256]{1,0:T(8,128)(2,1)}, u32[]{:S(2)}) copy-start(bf16[256,256]{1,0:T(8,128)(2,1)} %reg_keys.1) | copy-start | bytes 393220
  9.2 6.9 %collective-permute-start.1 = (bf16[136,256]{1,0:T(8,128)(2,1)S(1)}, bf16[136,256]{1,0:T(8,128)(2,1)S(1)}, u32[]{:S(2)}, u32[]{:S(2)}) collective-permute-start(bf16[136,256]{1,0:T(8,128)(2,1)S(1)} %shard_map.79.refs_0_), channel_id=1, source_target_pairs={{0,9},{1,2},{2,1},{3,10},{4,7},{5,12},{6,15},{7,4},{8,11},{9,0},{1... | collective-permute-start | bytes 208904 | tf_op jit(solution)/shard_map/ppermute | solution.py:398
  9.2 6.8 %collective-permute-start.2 = (bf16[136,256]{1,0:T(8,128)(2,1)S(1)}, bf16[136,256]{1,0:T(8,128)(2,1)S(1)}, u32[]{:S(2)}, u32[]{:S(2)}) collective-permute-start(bf16[136,256]{1,0:T(8,128)(2,1)S(1)} %shard_map.79.refs_0_), channel_id=1, source_target_pairs={{0,17},{1,4},{2,7},{3,18},{4,1},{5,20},{6,23},{7,2},{8,13},{9,24},... | collective-permute-start | bytes 208904 | tf_op jit(solution)/shard_map/ppermute | solution.py:398
  10.0 6.4 %collective-permute-start.3 = (bf16[136,256]{1,0:T(8,128)(2,1)S(1)}, bf16[136,256]{1,0:T(8,128)(2,1)S(1)}, u32[]{:S(2)}, u32[]{:S(2)}) collective-permute-start(bf16[136,256]{1,0:T(8,128)(2,1)S(1)} %shard_map.79.refs_0_), channel_id=1, source_target_pairs={{0,24},{1,7},{2,4},{3,27},{4,2},{5,29},{6,30},{7,1},{8,14},{9,17},... | collective-permute-start | bytes 208904 | tf_op jit(solution)/shard_map/ppermute | solution.py:398
  15.2 6.5 %collective-permute-start.7 = (bf16[2,192,256]{2,1,0:T(8,128)(2,1)S(1)}, bf16[2,192,256]{2,1,0:T(8,128)(2,1)S(1)}, u32[]{:S(2)}, u32[]{:S(2)}) collective-permute-start(bf16[2,192,256]{2,1,0:T(8,128)(2,1)S(1)} %pad_maximum_fusion), channel_id=1, source_target_pairs={{0,8},{1,2},{2,1},{3,11},{4,12},{5,6},{6,5},{7,15},{8,0},{9,10},{1... | collective-permute-start | bytes 589832 | tf_op jit(solution)/shard_map/ppermute | solution.py:368
  15.3 4.5 %collective-permute-start.6 = (bf16[2,96,256]{2,1,0:T(8,128)(2,1)S(1)}, bf16[2,96,256]{2,1,0:T(8,128)(2,1)S(1)}, u32[]{:S(2)}, u32[]{:S(2)}) collective-permute-start(bf16[2,96,256]{2,1,0:T(8,128)(2,1)S(1)} %pad_maximum_fusion.1), channel_id=1, source_target_pairs={{0,1},{1,0},{2,3},{3,2},{4,5},{5,4},{6,7},{7,6},{8,9},{9,8},{10,11... | collective-permute-start | bytes 294920 | tf_op jit(solution)/shard_map/ppermute | solution.py:304
  16.5 6.8 %collective-permute-start.10 = (bf16[136,256]{1,0:T(8,128)(2,1)S(1)}, bf16[136,256]{1,0:T(8,128)(2,1)S(1)}, u32[]{:S(2)}, u32[]{:S(2)}) collective-permute-start(bf16[136,256]{1,0:T(8,128)(2,1)S(1)} %shard_map.80.refs_0_), channel_id=1, source_target_pairs={{0,6},{1,25},{2,26},{3,5},{4,28},{5,3},{6,0},{7,31},{8,16},{9,15},... | collective-permute-start | bytes 208904 | tf_op jit(solution)/shard_map/ppermute | solution.py:398
  18.5 4.8 %collective-permute-start.8 = (bf16[136,256]{1,0:T(8,128)(2,1)S(1)}, bf16[136,256]{1,0:T(8,128)(2,1)S(1)}, u32[]{:S(2)}, u32[]{:S(2)}) collective-permute-start(bf16[136,256]{1,0:T(8,128)(2,1)S(1)} %shard_map.80.refs_0_), channel_id=1, source_target_pairs={{0,3},{1,8},{2,11},{3,0},{4,13},{5,6},{6,5},{7,14},{8,1},{9,10},{1... | collective-permute-start | bytes 208904 | tf_op jit(solution)/shard_map/ppermute | solution.py:398
  18.5 4.8 %collective-permute-start.9 = (bf16[136,256]{1,0:T(8,128)(2,1)S(1)}, bf16[136,256]{1,0:T(8,128)(2,1)S(1)}, u32[]{:S(2)}, u32[]{:S(2)}) collective-permute-start(bf16[136,256]{1,0:T(8,128)(2,1)S(1)} %shard_map.80.refs_0_), channel_id=1, source_target_pairs={{0,5},{1,16},{2,19},{3,6},{4,21},{5,0},{6,3},{7,22},{8,25},{9,12},... | collective-permute-start | bytes 208904 | tf_op jit(solution)/shard_map/ppermute | solution.py:398
  23.5 1.3 %collective-permute-start.11 = (bf16[128,256]{1,0:T(8,128)(2,1)S(1)}, bf16[128,256]{1,0:T(8,128)(2,1)S(1)}, u32[]{:S(2)}, u32[]{:S(2)}) collective-permute-start(bf16[128,256]{1,0:T(8,128)(2,1)S(1)} %shard_map.82.mine), channel_id=1, source_target_pairs={{0,1},{1,0},{2,3},{3,2},{4,5},{5,4},{6,7},{7,6},{8,9},{9,8},{10,11... | collective-permute-start | bytes 196616 | tf_op jit(solution)/shard_map/ppermute | solution.py:304

commit v7 on v6

--- a/solution.py
+++ b/solution.py
@@ -236,18 +236,22 @@
     hot = hot | ((lane >= rows + cols) & (lane < rows + cols + tiles))
     hot = jnp.where(hot, 1.0, 0.0).astype(BF16)
     first = iota((size, PAIR), 1) < HEAD_DIM
+    scores = []
+    for p in range(2):
+        scaled = q_ref[:, p * PAIR : (p + 1) * PAIR] * jnp.asarray(SCALE, BF16)
+        for j in range(2):
+            mine = jnp.where(first == (j == 0), scaled, jnp.zeros_like(scaled))
+            scores.append(dot(jnp.concatenate([mine, hot], axis=1), kbuf[p], NT))
     for p in range(2):
         lanes = slice(p * PAIR, (p + 1) * PAIR)
-        scaled = q_ref[:, lanes] * jnp.asarray(SCALE, BF16)
         tops, totals, mixed, weights = [], [], [], []
-        for j in range(2):
-            mine = jnp.where(first == (j == 0), scaled, jnp.zeros_like(scaled))
-            scores = dot(jnp.concatenate([mine, hot], axis=1), kbuf[p], NT)
-            tops.append(jnp.max(scores, axis=1, keepdims=True))
-            each = jnp.exp(scores - tops[j])
+        for each in scores[2 * p : 2 * p + 2]:
+            top = jnp.max(each, axis=1, keepdims=True)
+            each = jnp.exp(each - top)
+            tops.append(top)
             totals.append(jnp.sum(each, axis=1, keepdims=True))
             weights.append(each.astype(BF16))
-            mixed.append(jnp.dot(weights[j][:, ahead:], vbuf[:, lanes], preferred_element_type=F32))
+            mixed.append(jnp.dot(weights[-1][:, ahead:], vbuf[:, lanes], preferred_element_type=F32))
         yield p, lanes, *(jnp.where(first, *x) for x in (tops, totals, mixed)), weights
 
 
@@ -327,10 +331,12 @@
             pltpu.SemaphoreType.DMA((4,)),
         ],
     )
-    side_a = swap(near_cols, lats)
     side_b = lax.ppermute(
         far_cols, "lon", [(i, (i + 1 if i % 2 else i - 1) % lons) for i in range(lons)]
     )
+
+    near_cols, _ = lax.optimization_barrier((near_cols, core))
+    side_a = swap(near_cols, lats)
 
     payload = call(
         register_kernel,
@@ -355,6 +361,7 @@
         flops=2 * 2 * cells * inner * channels * 2,
     )
 
+    corner_a, corner_b, _ = lax.optimization_barrier((side_a, side_b, payload))
     side_a, side_b, _, _ = lax.optimization_barrier((side_a, side_b, payload, mixed))
 
     def take(shard, size, start, count):
@@ -363,7 +370,7 @@
 
     core_deep, cross_deep = (1 - lat % 2) * (rows - DEEP), (lat % 2) * (rows - DEEP)
     corner = swap(
-        jnp.concatenate([take(s, rows, core_deep, DEEP) for s in (side_a, side_b)], axis=1), 1
+        jnp.concatenate([take(s, rows, core_deep, DEEP) for s in (corner_a, corner_b)], axis=1), 1
     )
     cross = lax.ppermute(
         jnp.concatenate(

time: 26 us -> 25.4 us (0.977)
  Pallas kernels: 6.51 us -> 5.43 us
  waiting for transfers between devices: 3.25 us -> 3.8 us
    ppermute x6, waiting for transfers between devices: 0.3 us -> 2.53 us  [shards(): gathered.append(lax.ppermute(payload, everyone, pairs))]
    ppermute x4, starting transfers between devices: 4.16 us -> 2 us  [swap(): return lax.ppermute(x, everyone, [(i, i ^ mask) for i in range(devices)])]
    ppermute x1, starting transfers between devices: 3.54 us -> 5.63 us  [shards(): lax.ppermute(far_cols, 'lon', [(i, (i + 1 if i % 2 else i - 1) % lons) fo...]
    ppermute x1, waiting for transfers between devices: 1.92 us -> 0.24 us  [shards(): lax.ppermute(jnp.concatenate([take(own, cells, lat % 2 * (rows - RADIUS)...]
    pallas_call x7, Pallas kernels: 6.51 us -> 5.43 us  [call(): pl.pallas_call(kernel, out_shape=out, in_specs=specs, out_specs=jax.tree....]
  transfers between devices with their start and end apart: 12 -> 12, of which waited for: 3 -> 5; matrix products, arithmetic and copies ran while one was open for 0% -> 0% of each run, Pallas kernels for 21% -> 17%
where the time goes in v7:
time: 25.4 us; the launch traced here: 25.2 us
  starting transfers between devices  15.1 us (59%)
  Pallas kernels  5.43 us (21%)
  waiting for transfers between devices  3.8 us (15%)
  between operations  0.77 us (3%)
    ppermute x6, starting transfers between devices, shards(): gathered.append(lax.ppermute(payload, everyone, pairs))  7.44 us
    ppermute x1, starting transfers between devices, shards(): lax.ppermute(far_cols, 'lon', [(i, (i + 1 if i % 2 else i - 1) % lons) fo...  5.63 us
    pallas_call x7, Pallas kernels, call(): pl.pallas_call(kernel, out_shape=out, in_specs=specs, out_specs=jax.tree....  5.43 us
    ppermute x6, waiting for transfers between devices, shards(): gathered.append(lax.ppermute(payload, everyone, pairs))  2.53 us
    ppermute x4, starting transfers between devices, swap(): return lax.ppermute(x, everyone, [(i, i ^ mask) for i in range(devices)])  2 us
    ppermute x4, waiting for transfers between devices, swap(): return lax.ppermute(x, everyone, [(i, i ^ mask) for i in range(devices)])  1.03 us
  transfers between devices with their start and end apart: 12, of which 5 were waited for; matrix products, arithmetic and copies ran while one was open for 0% of the time, Pallas kernels for 17%

profile of v7, /device:TPU:0, one launch (start us, length us, event | category | flops | bytes accessed | tf_op | source)
XLA Modules:
  0.0 25.2 jit_solution(14262900782106457639)
XLA Ops:
  0.6 0.5 %collective-permute-start = (bf16[2,256,256]{2,1,0:T(8,128)(2,1)}, bf16[2,256,256]{2,1,0:T(8,128)(2,1)S(1)}, u32[]{:S(2)}, u32[]{:S(2)}) collective-permute-start(bf16[2,256,256]{2,1,0:T(8,128)(2,1)} %bitcast.21), channel_id=1, source_target_pairs={{0,1},{1,0},{2,3},{3,2},{4,5},{5,4},{6,7},{7,6},{8,9},{9,8},{10,11... | collective-permute-start | bytes 786440 | tf_op jit(solution)/shard_map/ppermute | solution.py:308
  1.1 1.2 %shard_map.77 = (bf16[2,256,256]{2,1,0:T(8,128)(2,1)S(1)}, bf16[256,256]{1,0:T(8,128)(2,1)S(1)}, bf16[2,96,256]{2,1,0:T(8,128)(2,1)S(1)}, bf16[2,96,256]{2,1,0:T(8,128)(2,1)S(1)}, f32[8,128]{1,0:T(8,128)S(1)}) custom-call(bf16[2,256,256]{2,1,0:T(8,128)(2,1)} %bitcast.22, bf16[256,256]{1,0:T(8,128)(2,1)} %queries_ref.1, s32[8]{0:T(128)} %pole_ref.1, ...), custom_call_target="tpu_custom_call" | custom-call | bytes 393760 | tf_op jit(solution)/shard_map/pallas_call | solution.py:50
  2.3 5.6 %collective-permute-start.5 = (bf16[2,96,256]{2,1,0:T(8,128)(2,1)S(1)}, bf16[2,96,256]{2,1,0:T(8,128)(2,1)S(1)}, u32[]{:S(2)}, u32[]{:S(2)}) collective-permute-start(bf16[2,96,256]{2,1,0:T(8,128)(2,1)S(1)} %get-tuple-element.31), channel_id=1, source_target_pairs={{0,28},{4,8},{8,4},{12,16},{16,12},{20,24},{24,20},{28,0},{1,29},{... | collective-permute-start | bytes 294920 | tf_op jit(solution)/shard_map/ppermute | solution.py:334
  8.0 0.0 copy-start
  8.0 0.0 copy-start.1
  8.0 0.7 %shard_map.79.refs_0_ = bf16[136,256]{1,0:T(8,128)(2,1)S(1)} custom-call(bf16[2,256,256]{2,1,0:T(8,128)(2,1)S(1)} %get-tuple-element.24.own, bf16[2,256,256]{2,1,0:T(8,128)(2,1)S(1)} %collective-permute-done.core.other, bf16[256,256]{1,0:T(8,128)(2,1)S(1)} %get-tuple-element.27.queries), custom_call_target="tpu_custom_call" | custom-call | flops 134217728 | bytes 655360 | tf_op jit(solution)/shard_map/pallas_call | solution.py:50
  8.7 0.1 collective-permute-start.1
  8.7 1.3 %collective-permute-start.2 = (bf16[136,256]{1,0:T(8,128)(2,1)S(1)}, bf16[136,256]{1,0:T(8,128)(2,1)S(1)}, u32[]{:S(2)}, u32[]{:S(2)}) collective-permute-start(bf16[136,256]{1,0:T(8,128)(2,1)S(1)} %shard_map.79.refs_0_), channel_id=1, source_target_pairs={{0,17},{1,4},{2,7},{3,18},{4,1},{5,20},{6,23},{7,2},{8,13},{9,24},... | collective-permute-start | bytes 208904 | tf_op jit(solution)/shard_map/ppermute | solution.py:405
  10.1 2.8 %collective-permute-start.3 = (bf16[136,256]{1,0:T(8,128)(2,1)S(1)}, bf16[136,256]{1,0:T(8,128)(2,1)S(1)}, u32[]{:S(2)}, u32[]{:S(2)}) collective-permute-start(bf16[136,256]{1,0:T(8,128)(2,1)S(1)} %shard_map.79.refs_0_), channel_id=1, source_target_pairs={{0,24},{1,7},{2,4},{3,27},{4,2},{5,29},{6,30},{7,1},{8,14},{9,17},... | collective-permute-start | bytes 208904 | tf_op jit(solution)/shard_map/ppermute | solution.py:405
  12.8 1.2 %shard_map.78 = (f32[256,256]{1,0:T(8,128)S(1)}, f32[256,256]{1,0:T(8,128)S(1)}, f32[256,256]{1,0:T(8,128)S(1)}, bf16[4,256,256]{2,1,0:T(8,128)(2,1)S(1)}) custom-call(bf16[256,256]{1,0:T(8,128)(2,1)S(1)} %bitcast.15, bf16[2,256,256]{2,1,0:T(8,128)(2,1)S(1)} %get-tuple-element.24.own, bf16[2,256,256]{2,1,0:T(8,128)(2,1)S(1)} %collective-permute-done.core.other, ...), custom_call_target="tpu_custom_call" | custom-call | flops 184549376 | bytes 790528 | tf_op jit(solution)/shard_map/pallas_call | solution.py:50
  14.1 0.1 collective-permute-start.7
  14.2 1.2 %collective-permute-start.6 = (bf16[2,96,256]{2,1,0:T(8,128)(2,1)S(1)}, bf16[2,96,256]{2,1,0:T(8,128)(2,1)S(1)}, u32[]{:S(2)}, u32[]{:S(2)}) collective-permute-start(bf16[2,96,256]{2,1,0:T(8,128)(2,1)S(1)} %pad_maximum_fusion.1), channel_id=1, source_target_pairs={{0,1},{1,0},{2,3},{3,2},{4,5},{5,4},{6,7},{7,6},{8,9},{9,8},{10,11... | collective-permute-start | bytes 294920 | tf_op jit(solution)/shard_map/ppermute | solution.py:308
  15.4 0.8 %collective-permute-done.3.refs_3_ = bf16[136,256]{1,0:T(8,128)(2,1)S(1)} collective-permute-done((bf16[136,256]{1,0:T(8,128)(2,1)S(1)}, bf16[136,256]{1,0:T(8,128)(2,1)S(1)}, u32[]{:S(2)}, u32[]{:S(2)}) %collective-permute-start.3) | collective-permute-done | bytes 69664 | tf_op jit(solution)/shard_map/ppermute | solution.py:405
  16.2 0.1 shard_map.80.refs_0_
  16.3 2.7 %collective-permute-start.10 = (bf16[136,256]{1,0:T(8,128)(2,1)S(1)}, bf16[136,256]{1,0:T(8,128)(2,1)S(1)}, u32[]{:S(2)}, u32[]{:S(2)}) collective-permute-start(bf16[136,256]{1,0:T(8,128)(2,1)S(1)} %shard_map.80.refs_0_), channel_id=1, source_target_pairs={{0,6},{1,25},{2,26},{3,5},{4,28},{5,3},{6,0},{7,31},{8,16},{9,15},... | collective-permute-start | bytes 208904 | tf_op jit(solution)/shard_map/ppermute | solution.py:405
  19.1 0.5 %collective-permute-start.9 = (bf16[136,256]{1,0:T(8,128)(2,1)S(1)}, bf16[136,256]{1,0:T(8,128)(2,1)S(1)}, u32[]{:S(2)}, u32[]{:S(2)}) collective-permute-start(bf16[136,256]{1,0:T(8,128)(2,1)S(1)} %shard_map.80.refs_0_), channel_id=1, source_target_pairs={{0,5},{1,16},{2,19},{3,6},{4,21},{5,0},{6,3},{7,22},{8,25},{9,12},... | collective-permute-start | bytes 208904 | tf_op jit(solution)/shard_map/ppermute | solution.py:405
  19.6 0.2 collective-permute-done.7.cross
  19.8 1.2 %shard_map.81 = (f32[256,256]{1,0:T(8,128)S(1)}, f32[256,256]{1,0:T(8,128)S(1)}) custom-call(bf16[256,256]{1,0:T(8,128)(2,1)S(1)} %bitcast.16, bf16[2,96,256]{2,1,0:T(8,128)(2,1)S(1)} %collective-permute-done.4.a, bf16[2,96,256]{2,1,0:T(8,128)(2,1)S(1)} %collective-permute-done.5.b, bf16[2,96,256]{2,1,0:T(8,128)(2,1)S(1)} %collective-permute-done.6.corner, ...), custom_call_target="tpu_custom_call" | custom-call | flops 251658240 | bytes 1150976 | tf_op jit(solution)/shard_map/pallas_call | solution.py:50
  21.0 0.6 %collective-permute-done.10.refs_3_ = bf16[136,256]{1,0:T(8,128)(2,1)S(1)} collective-permute-done((bf16[136,256]{1,0:T(8,128)(2,1)S(1)}, bf16[136,256]{1,0:T(8,128)(2,1)S(1)}, u32[]{:S(2)}, u32[]{:S(2)}) %collective-permute-start.10) | collective-permute-done | bytes 69664 | tf_op jit(solution)/shard_map/ppermute | solution.py:405
  21.6 1.2 %collective-permute-done.8.refs_1_ = bf16[136,256]{1,0:T(8,128)(2,1)S(1)} collective-permute-done((bf16[136,256]{1,0:T(8,128)(2,1)S(1)}, bf16[136,256]{1,0:T(8,128)(2,1)S(1)}, u32[]{:S(2)}, u32[]{:S(2)}) %collective-permute-start.8) | collective-permute-done | bytes 69664 | tf_op jit(solution)/shard_map/ppermute | solution.py:405
  22.8 0.1 shard_map.82.mine
  22.9 0.3 %collective-permute-start.11 = (bf16[128,256]{1,0:T(8,128)(2,1)S(1)}, bf16[128,256]{1,0:T(8,128)(2,1)S(1)}, u32[]{:S(2)}, u32[]{:S(2)}) collective-permute-start(bf16[128,256]{1,0:T(8,128)(2,1)S(1)} %shard_map.82.mine), channel_id=1, source_target_pairs={{0,1},{1,0},{2,3},{3,2},{4,5},{5,4},{6,7},{7,6},{8,9},{9,8},{10,11... | collective-permute-start | bytes 196616 | tf_op jit(solution)/shard_map/ppermute | solution.py:308
  23.2 1.0 %collective-permute-done.11.other = bf16[128,256]{1,0:T(8,128)(2,1)S(1)} collective-permute-done((bf16[128,256]{1,0:T(8,128)(2,1)S(1)}, bf16[128,256]{1,0:T(8,128)(2,1)S(1)}, u32[]{:S(2)}, u32[]{:S(2)}) %collective-permute-start.11) | collective-permute-done | bytes 65568 | tf_op jit(solution)/shard_map/ppermute | solution.py:308
  24.3 1.0 %shard_map.83 = (bf16[256,256]{1,0:T(8,128)(2,1)}, bf16[256,256]{1,0:T(8,128)(2,1)}) custom-call(f32[256,256]{1,0:T(8,128)S(1)} %get-tuple-element.26.inner, f32[256,256]{1,0:T(8,128)S(1)} %get-tuple-element.40.factor, f32[256,256]{1,0:T(8,128)S(1)} %get-tuple-element.41.rest, bf16[4,256,256]{2,1,0:T(8,128)(2,1)S(1)} %get-tuple-element.42.reg_weights, ...), custom_call_target="tpu_custom_call" | custom-call | flops 67108864 | bytes 1441792 | tf_op jit(solution)/shard_map/pallas_call | solution.py:50
  (16 shorter events, 0.1 us)
Async XLA Ops:
  0.6 7.3 %collective-permute-start = (bf16[2,256,256]{2,1,0:T(8,128)(2,1)}, bf16[2,256,256]{2,1,0:T(8,128)(2,1)S(1)}, u32[]{:S(2)}, u32[]{:S(2)}) collective-permute-start(bf16[2,256,256]{2,1,0:T(8,128)(2,1)} %bitcast.21), channel_id=1, source_target_pairs={{0,1},{1,0},{2,3},{3,2},{4,5},{5,4},{6,7},{7,6},{8,9},{9,8},{10,11... | collective-permute-start | bytes 786440 | tf_op jit(solution)/shard_map/ppermute | solution.py:308
  2.3 11.7 %collective-permute-start.5 = (bf16[2,96,256]{2,1,0:T(8,128)(2,1)S(1)}, bf16[2,96,256]{2,1,0:T(8,128)(2,1)S(1)}, u32[]{:S(2)}, u32[]{:S(2)}) collective-permute-start(bf16[2,96,256]{2,1,0:T(8,128)(2,1)S(1)} %get-tuple-element.31), channel_id=1, source_target_pairs={{0,28},{4,8},{8,4},{12,16},{16,12},{20,24},{24,20},{28,0},{1,29},{... | collective-permute-start | bytes 294920 | tf_op jit(solution)/shard_map/ppermute | solution.py:334
  7.9 6.1 %collective-permute-start.4 = (bf16[2,96,256]{2,1,0:T(8,128)(2,1)S(1)}, bf16[2,96,256]{2,1,0:T(8,128)(2,1)S(1)}, u32[]{:S(2)}, u32[]{:S(2)}) collective-permute-start(bf16[2,96,256]{2,1,0:T(8,128)(2,1)S(1)} %get-tuple-element.30), channel_id=1, source_target_pairs={{0,4},{1,5},{2,6},{3,7},{4,0},{5,1},{6,2},{7,3},{8,12},{9,13},{10,... | collective-permute-start | bytes 294920 | tf_op jit(solution)/shard_map/ppermute | solution.py:308
  8.0 4.9 %copy-start = (bf16[16,16,256]{2,1,0:T(8,128)(2,1)S(1)}, bf16[16,16,256]{2,1,0:T(8,128)(2,1)}, u32[]{:S(2)}) copy-start(bf16[16,16,256]{2,1,0:T(8,128)(2,1)} %param.6) | copy-start | bytes 393220
  8.0 4.9 %copy-start.1 = (bf16[256,256]{1,0:T(8,128)(2,1)S(1)}, bf16[256,256]{1,0:T(8,128)(2,1)}, u32[]{:S(2)}) copy-start(bf16[256,256]{1,0:T(8,128)(2,1)} %reg_keys.1) | copy-start | bytes 393220
  8.7 6.8 %collective-permute-start.1 = (bf16[136,256]{1,0:T(8,128)(2,1)S(1)}, bf16[136,256]{1,0:T(8,128)(2,1)S(1)}, u32[]{:S(2)}, u32[]{:S(2)}) collective-permute-start(bf16[136,256]{1,0:T(8,128)(2,1)S(1)} %shard_map.79.refs_0_), channel_id=1, source_target_pairs={{0,9},{1,2},{2,1},{3,10},{4,7},{5,12},{6,15},{7,4},{8,11},{9,0},{1... | collective-permute-start | bytes 208904 | tf_op jit(solution)/shard_map/ppermute | solution.py:405
  8.7 6.7 %collective-permute-start.2 = (bf16[136,256]{1,0:T(8,128)(2,1)S(1)}, bf16[136,256]{1,0:T(8,128)(2,1)S(1)}, u32[]{:S(2)}, u32[]{:S(2)}) collective-permute-start(bf16[136,256]{1,0:T(8,128)(2,1)S(1)} %shard_map.79.refs_0_), channel_id=1, source_target_pairs={{0,17},{1,4},{2,7},{3,18},{4,1},{5,20},{6,23},{7,2},{8,13},{9,24},... | collective-permute-start | bytes 208904 | tf_op jit(solution)/shard_map/ppermute | solution.py:405
  10.1 6.1 %collective-permute-start.3 = (bf16[136,256]{1,0:T(8,128)(2,1)S(1)}, bf16[136,256]{1,0:T(8,128)(2,1)S(1)}, u32[]{:S(2)}, u32[]{:S(2)}) collective-permute-start(bf16[136,256]{1,0:T(8,128)(2,1)S(1)} %shard_map.79.refs_0_), channel_id=1, source_target_pairs={{0,24},{1,7},{2,4},{3,27},{4,2},{5,29},{6,30},{7,1},{8,14},{9,17},... | collective-permute-start | bytes 208904 | tf_op jit(solution)/shard_map/ppermute | solution.py:405
  14.1 5.7 %collective-permute-start.7 = (bf16[2,192,256]{2,1,0:T(8,128)(2,1)S(1)}, bf16[2,192,256]{2,1,0:T(8,128)(2,1)S(1)}, u32[]{:S(2)}, u32[]{:S(2)}) collective-permute-start(bf16[2,192,256]{2,1,0:T(8,128)(2,1)S(1)} %pad_maximum_fusion), channel_id=1, source_target_pairs={{0,8},{1,2},{2,1},{3,11},{4,12},{5,6},{6,5},{7,15},{8,0},{9,10},{1... | collective-permute-start | bytes 589832 | tf_op jit(solution)/shard_map/ppermute | solution.py:375
  14.2 5.4 %collective-permute-start.6 = (bf16[2,96,256]{2,1,0:T(8,128)(2,1)S(1)}, bf16[2,96,256]{2,1,0:T(8,128)(2,1)S(1)}, u32[]{:S(2)}, u32[]{:S(2)}) collective-permute-start(bf16[2,96,256]{2,1,0:T(8,128)(2,1)S(1)} %pad_maximum_fusion.1), channel_id=1, source_target_pairs={{0,1},{1,0},{2,3},{3,2},{4,5},{5,4},{6,7},{7,6},{8,9},{9,8},{10,11... | collective-permute-start | bytes 294920 | tf_op jit(solution)/shard_map/ppermute | solution.py:308
  16.3 5.3 %collective-permute-start.10 = (bf16[136,256]{1,0:T(8,128)(2,1)S(1)}, bf16[136,256]{1,0:T(8,128)(2,1)S(1)}, u32[]{:S(2)}, u32[]{:S(2)}) collective-permute-start(bf16[136,256]{1,0:T(8,128)(2,1)S(1)} %shard_map.80.refs_0_), channel_id=1, source_target_pairs={{0,6},{1,25},{2,26},{3,5},{4,28},{5,3},{6,0},{7,31},{8,16},{9,15},... | collective-permute-start | bytes 208904 | tf_op jit(solution)/shard_map/ppermute | solution.py:405
  19.1 3.7 %collective-permute-start.8 = (bf16[136,256]{1,0:T(8,128)(2,1)S(1)}, bf16[136,256]{1,0:T(8,128)(2,1)S(1)}, u32[]{:S(2)}, u32[]{:S(2)}) collective-permute-start(bf16[136,256]{1,0:T(8,128)(2,1)S(1)} %shard_map.80.refs_0_), channel_id=1, source_target_pairs={{0,3},{1,8},{2,11},{3,0},{4,13},{5,6},{6,5},{7,14},{8,1},{9,10},{1... | collective-permute-start | bytes 208904 | tf_op jit(solution)/shard_map/ppermute | solution.py:405
  19.1 3.7 %collective-permute-start.9 = (bf16[136,256]{1,0:T(8,128)(2,1)S(1)}, bf16[136,256]{1,0:T(8,128)(2,1)S(1)}, u32[]{:S(2)}, u32[]{:S(2)}) collective-permute-start(bf16[136,256]{1,0:T(8,128)(2,1)S(1)} %shard_map.80.refs_0_), channel_id=1, source_target_pairs={{0,5},{1,16},{2,19},{3,6},{4,21},{5,0},{6,3},{7,22},{8,25},{9,12},... | collective-permute-start | bytes 208904 | tf_op jit(solution)/shard_map/ppermute | solution.py:405
  22.9 1.3 %collective-permute-start.11 = (bf16[128,256]{1,0:T(8,128)(2,1)S(1)}, bf16[128,256]{1,0:T(8,128)(2,1)S(1)}, u32[]{:S(2)}, u32[]{:S(2)}) collective-permute-start(bf16[128,256]{1,0:T(8,128)(2,1)S(1)} %shard_map.82.mine), channel_id=1, source_target_pairs={{0,1},{1,0},{2,3},{3,2},{4,5},{5,4},{6,7},{7,6},{8,9},{9,8},{10,11... | collective-permute-start | bytes 196616 | tf_op jit(solution)/shard_map/ppermute | solution.py:308

commit v8 on v7

--- a/solution.py
+++ b/solution.py
@@ -82,7 +82,7 @@
     for k in range(2):
         for lane in range(0, own.shape[2], 128):
             lanes = slice(lane, lane + 128)
-            wide[...] = own[k, :, lanes].astype(F32)
+            wide[: own.shape[1]] = own[k, :, lanes].astype(F32)
             for c in range(RADIUS):
                 low = wide[pl.ds(c, rows, stride=cols)]
                 high = wide[pl.ds(cols - RADIUS + c, rows, stride=cols)]
@@ -325,16 +325,17 @@
         tuple(pltpu.with_memory_space_constraint(x, pltpu.HBM) for x in inputs),
         [HBM] * 4,
         scratch=[
-            pltpu.VMEM((cells, 128), F32),
+            pltpu.VMEM((cells + cols, 128), F32),
             pltpu.SMEM(pole_mask.shape, jnp.int32),
             pltpu.SMEM(sea_mask.shape, jnp.int32),
             pltpu.SemaphoreType.DMA((4,)),
         ],
     )
+
+
     side_b = lax.ppermute(
         far_cols, "lon", [(i, (i + 1 if i % 2 else i - 1) % lons) for i in range(lons)]
     )
-
     near_cols, _ = lax.optimization_barrier((near_cols, core))
     side_a = swap(near_cols, lats)
 
@@ -381,7 +382,7 @@
             axis=1,
         ),
         everyone,
-        [(i, i ^ 3 if i % lats in (1, 2) else i ^ 2 * lats) for i in range(devices)],
+        [(i, i ^ 3 if i % lats in (1, 2) else i ^ lats) for i in range(devices)],
     )
     rest, factor = call(
         functools.partial(outer_kernel, rows, cols),
@@ -397,10 +398,12 @@
     for step in steps:
         first, last = step is steps[0], step is steps[-1]
         gathered = [payload]
-        for chosen in range(1, 4):
+        for slot in range(3):
             pairs = []
             for i in range(devices):
-                flips = [b for k, b in enumerate(step[bin(i).count("1") % 2]) if chosen >> k & 1]
+                stage = step[bin(i).count("1") % 2]
+                chosen = ((1, 2, 3) if stage == near_bits else (1, 2, 3))[slot]
+                flips = [b for k, b in enumerate(stage) if chosen >> k & 1]
                 pairs.append((i, i ^ (sum(1 << b for b in flips) + len(flips) % 2)))
             gathered.append(lax.ppermute(payload, everyone, pairs))
         if first:

time: 25.4 us -> 25.3 us (level)
    ppermute x1, starting transfers between devices: 0.07 us -> 1.18 us  [shards(): lax.ppermute(jnp.concatenate([take(own, cells, lat % 2 * (rows - RADIUS)...]
    ppermute x4, starting transfers between devices: 2 us -> 0.95 us  [swap(): return lax.ppermute(x, everyone, [(i, i ^ mask) for i in range(devices)])]
where the time goes in v8:
time: 25.3 us; the launch traced here: 25.2 us
  starting transfers between devices  15.2 us (60%)
  Pallas kernels  5.43 us (21%)
  waiting for transfers between devices  3.74 us (15%)
  between operations  0.75 us (3%)
    ppermute x6, starting transfers between devices, shards(): gathered.append(lax.ppermute(payload, everyone, pairs))  7.44 us
    ppermute x1, starting transfers between devices, shards(): lax.ppermute(far_cols, 'lon', [(i, (i + 1 if i % 2 else i - 1) % lons) fo...  5.63 us
    pallas_call x7, Pallas kernels, call(): pl.pallas_call(kernel, out_shape=out, in_specs=specs, out_specs=jax.tree....  5.43 us
    ppermute x6, waiting for transfers between devices, shards(): gathered.append(lax.ppermute(payload, everyone, pairs))  2.5 us
    ppermute x1, starting transfers between devices, shards(): lax.ppermute(jnp.concatenate([take(own, cells, lat % 2 * (rows - RADIUS)...  1.18 us
    ppermute x4, waiting for transfers between devices, swap(): return lax.ppermute(x, everyone, [(i, i ^ mask) for i in range(devices)])  1 us
    ppermute x4, starting transfers between devices, swap(): return lax.ppermute(x, everyone, [(i, i ^ mask) for i in range(devices)])  0.95 us
  transfers between devices with their start and end apart: 12, of which 5 were waited for; matrix products, arithmetic and copies ran while one was open for 0% of the time, Pallas kernels for 17%

profile of v8, /device:TPU:0, one launch (start us, length us, event | category | flops | bytes accessed | tf_op | source)
XLA Modules:
  0.0 25.2 jit_solution(15582294364914699048)
XLA Ops:
  0.6 0.5 %collective-permute-start = (bf16[2,256,256]{2,1,0:T(8,128)(2,1)}, bf16[2,256,256]{2,1,0:T(8,128)(2,1)S(1)}, u32[]{:S(2)}, u32[]{:S(2)}) collective-permute-start(bf16[2,256,256]{2,1,0:T(8,128)(2,1)} %bitcast.21), channel_id=1, source_target_pairs={{0,1},{1,0},{2,3},{3,2},{4,5},{5,4},{6,7},{7,6},{8,9},{9,8},{10,11... | collective-permute-start | bytes 786440 | tf_op jit(solution)/shard_map/ppermute | solution.py:308
  1.1 1.2 %shard_map.77 = (bf16[2,256,256]{2,1,0:T(8,128)(2,1)S(1)}, bf16[256,256]{1,0:T(8,128)(2,1)S(1)}, bf16[2,96,256]{2,1,0:T(8,128)(2,1)S(1)}, bf16[2,96,256]{2,1,0:T(8,128)(2,1)S(1)}, f32[8,128]{1,0:T(8,128)S(1)}) custom-call(bf16[2,256,256]{2,1,0:T(8,128)(2,1)} %bitcast.22, bf16[256,256]{1,0:T(8,128)(2,1)} %queries_ref.1, s32[8]{0:T(128)} %pole_ref.1, ...), custom_call_target="tpu_custom_call" | custom-call | bytes 393760 | tf_op jit(solution)/shard_map/pallas_call | solution.py:50
  2.3 5.6 %collective-permute-start.5 = (bf16[2,96,256]{2,1,0:T(8,128)(2,1)S(1)}, bf16[2,96,256]{2,1,0:T(8,128)(2,1)S(1)}, u32[]{:S(2)}, u32[]{:S(2)}) collective-permute-start(bf16[2,96,256]{2,1,0:T(8,128)(2,1)S(1)} %get-tuple-element.31), channel_id=1, source_target_pairs={{0,28},{4,8},{8,4},{12,16},{16,12},{20,24},{24,20},{28,0},{1,29},{... | collective-permute-start | bytes 294920 | tf_op jit(solution)/shard_map/ppermute | solution.py:336
  8.0 0.0 copy-start
  8.0 0.0 copy-start.1
  8.0 0.7 %shard_map.79.refs_0_ = bf16[136,256]{1,0:T(8,128)(2,1)S(1)} custom-call(bf16[2,256,256]{2,1,0:T(8,128)(2,1)S(1)} %get-tuple-element.24.own, bf16[2,256,256]{2,1,0:T(8,128)(2,1)S(1)} %collective-permute-done.core.other, bf16[256,256]{1,0:T(8,128)(2,1)S(1)} %get-tuple-element.27.queries), custom_call_target="tpu_custom_call" | custom-call | flops 134217728 | bytes 655360 | tf_op jit(solution)/shard_map/pallas_call | solution.py:50
  8.7 0.1 collective-permute-start.1
  8.7 1.3 %collective-permute-start.2 = (bf16[136,256]{1,0:T(8,128)(2,1)S(1)}, bf16[136,256]{1,0:T(8,128)(2,1)S(1)}, u32[]{:S(2)}, u32[]{:S(2)}) collective-permute-start(bf16[136,256]{1,0:T(8,128)(2,1)S(1)} %shard_map.79.refs_0_), channel_id=1, source_target_pairs={{0,17},{1,4},{2,7},{3,18},{4,1},{5,20},{6,23},{7,2},{8,13},{9,24},... | collective-permute-start | bytes 208904 | tf_op jit(solution)/shard_map/ppermute | solution.py:408
  10.1 2.8 %collective-permute-start.3 = (bf16[136,256]{1,0:T(8,128)(2,1)S(1)}, bf16[136,256]{1,0:T(8,128)(2,1)S(1)}, u32[]{:S(2)}, u32[]{:S(2)}) collective-permute-start(bf16[136,256]{1,0:T(8,128)(2,1)S(1)} %shard_map.79.refs_0_), channel_id=1, source_target_pairs={{0,24},{1,7},{2,4},{3,27},{4,2},{5,29},{6,30},{7,1},{8,14},{9,17},... | collective-permute-start | bytes 208904 | tf_op jit(solution)/shard_map/ppermute | solution.py:408
  12.8 1.2 %shard_map.78 = (f32[256,256]{1,0:T(8,128)S(1)}, f32[256,256]{1,0:T(8,128)S(1)}, f32[256,256]{1,0:T(8,128)S(1)}, bf16[4,256,256]{2,1,0:T(8,128)(2,1)S(1)}) custom-call(bf16[256,256]{1,0:T(8,128)(2,1)S(1)} %bitcast.15, bf16[2,256,256]{2,1,0:T(8,128)(2,1)S(1)} %get-tuple-element.24.own, bf16[2,256,256]{2,1,0:T(8,128)(2,1)S(1)} %collective-permute-done.core.other, ...), custom_call_target="tpu_custom_call" | custom-call | flops 184549376 | bytes 790528 | tf_op jit(solution)/shard_map/pallas_call | solution.py:50
  14.1 1.2 %collective-permute-start.7 = (bf16[2,192,256]{2,1,0:T(8,128)(2,1)S(1)}, bf16[2,192,256]{2,1,0:T(8,128)(2,1)S(1)}, u32[]{:S(2)}, u32[]{:S(2)}) collective-permute-start(bf16[2,192,256]{2,1,0:T(8,128)(2,1)S(1)} %pad_maximum_fusion), channel_id=1, source_target_pairs={{0,4},{1,2},{2,1},{3,7},{4,0},{5,6},{6,5},{7,3},{8,12},{9,10},{10,... | collective-permute-start | bytes 589832 | tf_op jit(solution)/shard_map/ppermute | solution.py:376
  15.3 0.1 collective-permute-start.6
  15.4 0.8 %collective-permute-done.3.refs_3_ = bf16[136,256]{1,0:T(8,128)(2,1)S(1)} collective-permute-done((bf16[136,256]{1,0:T(8,128)(2,1)S(1)}, bf16[136,256]{1,0:T(8,128)(2,1)S(1)}, u32[]{:S(2)}, u32[]{:S(2)}) %collective-permute-start.3) | collective-permute-done | bytes 69664 | tf_op jit(solution)/shard_map/ppermute | solution.py:408
  16.2 0.1 shard_map.80.refs_0_
  16.3 2.7 %collective-permute-start.10 = (bf16[136,256]{1,0:T(8,128)(2,1)S(1)}, bf16[136,256]{1,0:T(8,128)(2,1)S(1)}, u32[]{:S(2)}, u32[]{:S(2)}) collective-permute-start(bf16[136,256]{1,0:T(8,128)(2,1)S(1)} %shard_map.80.refs_0_), channel_id=1, source_target_pairs={{0,6},{1,25},{2,26},{3,5},{4,28},{5,3},{6,0},{7,31},{8,16},{9,15},... | collective-permute-start | bytes 208904 | tf_op jit(solution)/shard_map/ppermute | solution.py:408
  19.0 0.6 %collective-permute-start.9 = (bf16[136,256]{1,0:T(8,128)(2,1)S(1)}, bf16[136,256]{1,0:T(8,128)(2,1)S(1)}, u32[]{:S(2)}, u32[]{:S(2)}) collective-permute-start(bf16[136,256]{1,0:T(8,128)(2,1)S(1)} %shard_map.80.refs_0_), channel_id=1, source_target_pairs={{0,5},{1,16},{2,19},{3,6},{4,21},{5,0},{6,3},{7,22},{8,25},{9,12},... | collective-permute-start | bytes 208904 | tf_op jit(solution)/shard_map/ppermute | solution.py:408
  19.6 0.2 collective-permute-done.7.cross
  19.8 1.2 %shard_map.81 = (f32[256,256]{1,0:T(8,128)S(1)}, f32[256,256]{1,0:T(8,128)S(1)}) custom-call(bf16[256,256]{1,0:T(8,128)(2,1)S(1)} %bitcast.16, bf16[2,96,256]{2,1,0:T(8,128)(2,1)S(1)} %collective-permute-done.4.a, bf16[2,96,256]{2,1,0:T(8,128)(2,1)S(1)} %collective-permute-done.5.b, bf16[2,96,256]{2,1,0:T(8,128)(2,1)S(1)} %collective-permute-done.6.corner, ...), custom_call_target="tpu_custom_call" | custom-call | flops 251658240 | bytes 1150976 | tf_op jit(solution)/shard_map/pallas_call | solution.py:50
  21.0 0.6 %collective-permute-done.10.refs_3_ = bf16[136,256]{1,0:T(8,128)(2,1)S(1)} collective-permute-done((bf16[136,256]{1,0:T(8,128)(2,1)S(1)}, bf16[136,256]{1,0:T(8,128)(2,1)S(1)}, u32[]{:S(2)}, u32[]{:S(2)}) %collective-permute-start.10) | collective-permute-done | bytes 69664 | tf_op jit(solution)/shard_map/ppermute | solution.py:408
  21.6 1.2 %collective-permute-done.8.refs_1_ = bf16[136,256]{1,0:T(8,128)(2,1)S(1)} collective-permute-done((bf16[136,256]{1,0:T(8,128)(2,1)S(1)}, bf16[136,256]{1,0:T(8,128)(2,1)S(1)}, u32[]{:S(2)}, u32[]{:S(2)}) %collective-permute-start.8) | collective-permute-done | bytes 69664 | tf_op jit(solution)/shard_map/ppermute | solution.py:408
  22.8 0.1 shard_map.82.mine
  22.9 0.3 %collective-permute-start.11 = (bf16[128,256]{1,0:T(8,128)(2,1)S(1)}, bf16[128,256]{1,0:T(8,128)(2,1)S(1)}, u32[]{:S(2)}, u32[]{:S(2)}) collective-permute-start(bf16[128,256]{1,0:T(8,128)(2,1)S(1)} %shard_map.82.mine), channel_id=1, source_target_pairs={{0,1},{1,0},{2,3},{3,2},{4,5},{5,4},{6,7},{7,6},{8,9},{9,8},{10,11... | collective-permute-start | bytes 196616 | tf_op jit(solution)/shard_map/ppermute | solution.py:308
  23.2 1.0 %collective-permute-done.11.other = bf16[128,256]{1,0:T(8,128)(2,1)S(1)} collective-permute-done((bf16[128,256]{1,0:T(8,128)(2,1)S(1)}, bf16[128,256]{1,0:T(8,128)(2,1)S(1)}, u32[]{:S(2)}, u32[]{:S(2)}) %collective-permute-start.11) | collective-permute-done | bytes 65568 | tf_op jit(solution)/shard_map/ppermute | solution.py:308
  24.2 1.0 %shard_map.83 = (bf16[256,256]{1,0:T(8,128)(2,1)}, bf16[256,256]{1,0:T(8,128)(2,1)}) custom-call(f32[256,256]{1,0:T(8,128)S(1)} %get-tuple-element.26.inner, f32[256,256]{1,0:T(8,128)S(1)} %get-tuple-element.40.factor, f32[256,256]{1,0:T(8,128)S(1)} %get-tuple-element.41.rest, bf16[4,256,256]{2,1,0:T(8,128)(2,1)S(1)} %get-tuple-element.42.reg_weights, ...), custom_call_target="tpu_custom_call" | custom-call | flops 67108864 | bytes 1441792 | tf_op jit(solution)/shard_map/pallas_call | solution.py:50
  (16 shorter events, 0.1 us)
Async XLA Ops:
  0.6 7.3 %collective-permute-start = (bf16[2,256,256]{2,1,0:T(8,128)(2,1)}, bf16[2,256,256]{2,1,0:T(8,128)(2,1)S(1)}, u32[]{:S(2)}, u32[]{:S(2)}) collective-permute-start(bf16[2,256,256]{2,1,0:T(8,128)(2,1)} %bitcast.21), channel_id=1, source_target_pairs={{0,1},{1,0},{2,3},{3,2},{4,5},{5,4},{6,7},{7,6},{8,9},{9,8},{10,11... | collective-permute-start | bytes 786440 | tf_op jit(solution)/shard_map/ppermute | solution.py:308
  2.3 11.7 %collective-permute-start.5 = (bf16[2,96,256]{2,1,0:T(8,128)(2,1)S(1)}, bf16[2,96,256]{2,1,0:T(8,128)(2,1)S(1)}, u32[]{:S(2)}, u32[]{:S(2)}) collective-permute-start(bf16[2,96,256]{2,1,0:T(8,128)(2,1)S(1)} %get-tuple-element.31), channel_id=1, source_target_pairs={{0,28},{4,8},{8,4},{12,16},{16,12},{20,24},{24,20},{28,0},{1,29},{... | collective-permute-start | bytes 294920 | tf_op jit(solution)/shard_map/ppermute | solution.py:336
  7.9 6.1 %collective-permute-start.4 = (bf16[2,96,256]{2,1,0:T(8,128)(2,1)S(1)}, bf16[2,96,256]{2,1,0:T(8,128)(2,1)S(1)}, u32[]{:S(2)}, u32[]{:S(2)}) collective-permute-start(bf16[2,96,256]{2,1,0:T(8,128)(2,1)S(1)} %get-tuple-element.30), channel_id=1, source_target_pairs={{0,4},{1,5},{2,6},{3,7},{4,0},{5,1},{6,2},{7,3},{8,12},{9,13},{10,... | collective-permute-start | bytes 294920 | tf_op jit(solution)/shard_map/ppermute | solution.py:308
  8.0 4.9 %copy-start = (bf16[16,16,256]{2,1,0:T(8,128)(2,1)S(1)}, bf16[16,16,256]{2,1,0:T(8,128)(2,1)}, u32[]{:S(2)}) copy-start(bf16[16,16,256]{2,1,0:T(8,128)(2,1)} %param.6) | copy-start | bytes 393220
  8.0 4.9 %copy-start.1 = (bf16[256,256]{1,0:T(8,128)(2,1)S(1)}, bf16[256,256]{1,0:T(8,128)(2,1)}, u32[]{:S(2)}) copy-start(bf16[256,256]{1,0:T(8,128)(2,1)} %reg_keys.1) | copy-start | bytes 393220
  8.7 6.8 %collective-permute-start.1 = (bf16[136,256]{1,0:T(8,128)(2,1)S(1)}, bf16[136,256]{1,0:T(8,128)(2,1)S(1)}, u32[]{:S(2)}, u32[]{:S(2)}) collective-permute-start(bf16[136,256]{1,0:T(8,128)(2,1)S(1)} %shard_map.79.refs_0_), channel_id=1, source_target_pairs={{0,9},{1,2},{2,1},{3,10},{4,7},{5,12},{6,15},{7,4},{8,11},{9,0},{1... | collective-permute-start | bytes 208904 | tf_op jit(solution)/shard_map/ppermute | solution.py:408
  8.7 6.7 %collective-permute-start.2 = (bf16[136,256]{1,0:T(8,128)(2,1)S(1)}, bf16[136,256]{1,0:T(8,128)(2,1)S(1)}, u32[]{:S(2)}, u32[]{:S(2)}) collective-permute-start(bf16[136,256]{1,0:T(8,128)(2,1)S(1)} %shard_map.79.refs_0_), channel_id=1, source_target_pairs={{0,17},{1,4},{2,7},{3,18},{4,1},{5,20},{6,23},{7,2},{8,13},{9,24},... | collective-permute-start | bytes 208904 | tf_op jit(solution)/shard_map/ppermute | solution.py:408
  10.1 6.1 %collective-permute-start.3 = (bf16[136,256]{1,0:T(8,128)(2,1)S(1)}, bf16[136,256]{1,0:T(8,128)(2,1)S(1)}, u32[]{:S(2)}, u32[]{:S(2)}) collective-permute-start(bf16[136,256]{1,0:T(8,128)(2,1)S(1)} %shard_map.79.refs_0_), channel_id=1, source_target_pairs={{0,24},{1,7},{2,4},{3,27},{4,2},{5,29},{6,30},{7,1},{8,14},{9,17},... | collective-permute-start | bytes 208904 | tf_op jit(solution)/shard_map/ppermute | solution.py:408
  14.1 5.7 %collective-permute-start.7 = (bf16[2,192,256]{2,1,0:T(8,128)(2,1)S(1)}, bf16[2,192,256]{2,1,0:T(8,128)(2,1)S(1)}, u32[]{:S(2)}, u32[]{:S(2)}) collective-permute-start(bf16[2,192,256]{2,1,0:T(8,128)(2,1)S(1)} %pad_maximum_fusion), channel_id=1, source_target_pairs={{0,4},{1,2},{2,1},{3,7},{4,0},{5,6},{6,5},{7,3},{8,12},{9,10},{10,... | collective-permute-start | bytes 589832 | tf_op jit(solution)/shard_map/ppermute | solution.py:376
  15.3 4.3 %collective-permute-start.6 = (bf16[2,96,256]{2,1,0:T(8,128)(2,1)S(1)}, bf16[2,96,256]{2,1,0:T(8,128)(2,1)S(1)}, u32[]{:S(2)}, u32[]{:S(2)}) collective-permute-start(bf16[2,96,256]{2,1,0:T(8,128)(2,1)S(1)} %pad_maximum_fusion.1), channel_id=1, source_target_pairs={{0,1},{1,0},{2,3},{3,2},{4,5},{5,4},{6,7},{7,6},{8,9},{9,8},{10,11... | collective-permute-start | bytes 294920 | tf_op jit(solution)/shard_map/ppermute | solution.py:308
  16.3 5.3 %collective-permute-start.10 = (bf16[136,256]{1,0:T(8,128)(2,1)S(1)}, bf16[136,256]{1,0:T(8,128)(2,1)S(1)}, u32[]{:S(2)}, u32[]{:S(2)}) collective-permute-start(bf16[136,256]{1,0:T(8,128)(2,1)S(1)} %shard_map.80.refs_0_), channel_id=1, source_target_pairs={{0,6},{1,25},{2,26},{3,5},{4,28},{5,3},{6,0},{7,31},{8,16},{9,15},... | collective-permute-start | bytes 208904 | tf_op jit(solution)/shard_map/ppermute | solution.py:408
  19.0 3.7 %collective-permute-start.8 = (bf16[136,256]{1,0:T(8,128)(2,1)S(1)}, bf16[136,256]{1,0:T(8,128)(2,1)S(1)}, u32[]{:S(2)}, u32[]{:S(2)}) collective-permute-start(bf16[136,256]{1,0:T(8,128)(2,1)S(1)} %shard_map.80.refs_0_), channel_id=1, source_target_pairs={{0,3},{1,8},{2,11},{3,0},{4,13},{5,6},{6,5},{7,14},{8,1},{9,10},{1... | collective-permute-start | bytes 208904 | tf_op jit(solution)/shard_map/ppermute | solution.py:408
  19.0 3.7 %collective-permute-start.9 = (bf16[136,256]{1,0:T(8,128)(2,1)S(1)}, bf16[136,256]{1,0:T(8,128)(2,1)S(1)}, u32[]{:S(2)}, u32[]{:S(2)}) collective-permute-start(bf16[136,256]{1,0:T(8,128)(2,1)S(1)} %shard_map.80.refs_0_), channel_id=1, source_target_pairs={{0,5},{1,16},{2,19},{3,6},{4,21},{5,0},{6,3},{7,22},{8,25},{9,12},... | collective-permute-start | bytes 208904 | tf_op jit(solution)/shard_map/ppermute | solution.py:408
  22.9 1.3 %collective-permute-start.11 = (bf16[128,256]{1,0:T(8,128)(2,1)S(1)}, bf16[128,256]{1,0:T(8,128)(2,1)S(1)}, u32[]{:S(2)}, u32[]{:S(2)}) collective-permute-start(bf16[128,256]{1,0:T(8,128)(2,1)S(1)} %shard_map.82.mine), channel_id=1, source_target_pairs={{0,1},{1,0},{2,3},{3,2},{4,5},{5,4},{6,7},{7,6},{8,9},{9,8},{10,11... | collective-permute-start | bytes 196616 | tf_op jit(solution)/shard_map/ppermute | solution.py:308

commit v9 on v8

--- a/solution.py
+++ b/solution.py
@@ -331,8 +331,6 @@
             pltpu.SemaphoreType.DMA((4,)),
         ],
     )
-
-
     side_b = lax.ppermute(
         far_cols, "lon", [(i, (i + 1 if i % 2 else i - 1) % lons) for i in range(lons)]
     )
@@ -398,12 +396,10 @@
     for step in steps:
         first, last = step is steps[0], step is steps[-1]
         gathered = [payload]
-        for slot in range(3):
+        for chosen in range(1, 4):
             pairs = []
             for i in range(devices):
-                stage = step[bin(i).count("1") % 2]
-                chosen = ((1, 2, 3) if stage == near_bits else (1, 2, 3))[slot]
-                flips = [b for k, b in enumerate(stage) if chosen >> k & 1]
+                flips = [b for k, b in enumerate(step[bin(i).count("1") % 2]) if chosen >> k & 1]
                 pairs.append((i, i ^ (sum(1 << b for b in flips) + len(flips) % 2)))
             gathered.append(lax.ppermute(payload, everyone, pairs))
         if first:

time: 25.3 us -> 25.3 us (level)
  no operation moved by 1% of the time
where the time goes in v9:
time: 25.3 us; the launch traced here: 25.2 us
  starting transfers between devices  15.2 us (60%)
  Pallas kernels  5.43 us (21%)
  waiting for transfers between devices  3.74 us (15%)
  between operations  0.75 us (3%)
    ppermute x6, starting transfers between devices, shards(): gathered.append(lax.ppermute(payload, everyone, pairs))  7.44 us
    ppermute x1, starting transfers between devices, shards(): lax.ppermute(far_cols, 'lon', [(i, (i + 1 if i % 2 else i - 1) % lons) fo...  5.63 us
    pallas_call x7, Pallas kernels, call(): pl.pallas_call(kernel, out_shape=out, in_specs=specs, out_specs=jax.tree....  5.43 us
    ppermute x6, waiting for transfers between devices, shards(): gathered.append(lax.ppermute(payload, everyone, pairs))  2.5 us
    ppermute x1, starting transfers between devices, shards(): lax.ppermute(jnp.concatenate([take(own, cells, lat % 2 * (rows - RADIUS)...  1.18 us
    ppermute x4, waiting for transfers between devices, swap(): return lax.ppermute(x, everyone, [(i, i ^ mask) for i in range(devices)])  1 us
    ppermute x4, starting transfers between devices, swap(): return lax.ppermute(x, everyone, [(i, i ^ mask) for i in range(devices)])  0.95 us
  transfers between devices with their start and end apart: 12, of which 5 were waited for; matrix products, arithmetic and copies ran while one was open for 0% of the time, Pallas kernels for 17%

profile of v9, /device:TPU:0, one launch (start us, length us, event | category | flops | bytes accessed | tf_op | source)
XLA Modules:
  0.0 25.2 jit_solution(15582294364914699048)
XLA Ops:
  0.6 0.5 %collective-permute-start = (bf16[2,256,256]{2,1,0:T(8,128)(2,1)}, bf16[2,256,256]{2,1,0:T(8,128)(2,1)S(1)}, u32[]{:S(2)}, u32[]{:S(2)}) collective-permute-start(bf16[2,256,256]{2,1,0:T(8,128)(2,1)} %bitcast.21), channel_id=1, source_target_pairs={{0,1},{1,0},{2,3},{3,2},{4,5},{5,4},{6,7},{7,6},{8,9},{9,8},{10,11... | collective-permute-start | bytes 786440 | tf_op jit(solution)/shard_map/ppermute | solution.py:308
  1.1 1.2 %shard_map.77 = (bf16[2,256,256]{2,1,0:T(8,128)(2,1)S(1)}, bf16[256,256]{1,0:T(8,128)(2,1)S(1)}, bf16[2,96,256]{2,1,0:T(8,128)(2,1)S(1)}, bf16[2,96,256]{2,1,0:T(8,128)(2,1)S(1)}, f32[8,128]{1,0:T(8,128)S(1)}) custom-call(bf16[2,256,256]{2,1,0:T(8,128)(2,1)} %bitcast.22, bf16[256,256]{1,0:T(8,128)(2,1)} %queries_ref.1, s32[8]{0:T(128)} %pole_ref.1, ...), custom_call_target="tpu_custom_call" | custom-call | bytes 393760 | tf_op jit(solution)/shard_map/pallas_call | solution.py:50
  2.3 5.6 %collective-permute-start.5 = (bf16[2,96,256]{2,1,0:T(8,128)(2,1)S(1)}, bf16[2,96,256]{2,1,0:T(8,128)(2,1)S(1)}, u32[]{:S(2)}, u32[]{:S(2)}) collective-permute-start(bf16[2,96,256]{2,1,0:T(8,128)(2,1)S(1)} %get-tuple-element.31), channel_id=1, source_target_pairs={{0,28},{4,8},{8,4},{12,16},{16,12},{20,24},{24,20},{28,0},{1,29},{... | collective-permute-start | bytes 294920 | tf_op jit(solution)/shard_map/ppermute | solution.py:334
  8.0 0.0 copy-start
  8.0 0.0 copy-start.1
  8.0 0.7 %shard_map.79.refs_0_ = bf16[136,256]{1,0:T(8,128)(2,1)S(1)} custom-call(bf16[2,256,256]{2,1,0:T(8,128)(2,1)S(1)} %get-tuple-element.24.own, bf16[2,256,256]{2,1,0:T(8,128)(2,1)S(1)} %collective-permute-done.core.other, bf16[256,256]{1,0:T(8,128)(2,1)S(1)} %get-tuple-element.27.queries), custom_call_target="tpu_custom_call" | custom-call | flops 134217728 | bytes 655360 | tf_op jit(solution)/shard_map/pallas_call | solution.py:50
  8.7 0.1 collective-permute-start.1
  8.7 1.3 %collective-permute-start.2 = (bf16[136,256]{1,0:T(8,128)(2,1)S(1)}, bf16[136,256]{1,0:T(8,128)(2,1)S(1)}, u32[]{:S(2)}, u32[]{:S(2)}) collective-permute-start(bf16[136,256]{1,0:T(8,128)(2,1)S(1)} %shard_map.79.refs_0_), channel_id=1, source_target_pairs={{0,17},{1,4},{2,7},{3,18},{4,1},{5,20},{6,23},{7,2},{8,13},{9,24},... | collective-permute-start | bytes 208904 | tf_op jit(solution)/shard_map/ppermute | solution.py:404
  10.1 2.8 %collective-permute-start.3 = (bf16[136,256]{1,0:T(8,128)(2,1)S(1)}, bf16[136,256]{1,0:T(8,128)(2,1)S(1)}, u32[]{:S(2)}, u32[]{:S(2)}) collective-permute-start(bf16[136,256]{1,0:T(8,128)(2,1)S(1)} %shard_map.79.refs_0_), channel_id=1, source_target_pairs={{0,24},{1,7},{2,4},{3,27},{4,2},{5,29},{6,30},{7,1},{8,14},{9,17},... | collective-permute-start | bytes 208904 | tf_op jit(solution)/shard_map/ppermute | solution.py:404
  12.8 1.2 %shard_map.78 = (f32[256,256]{1,0:T(8,128)S(1)}, f32[256,256]{1,0:T(8,128)S(1)}, f32[256,256]{1,0:T(8,128)S(1)}, bf16[4,256,256]{2,1,0:T(8,128)(2,1)S(1)}) custom-call(bf16[256,256]{1,0:T(8,128)(2,1)S(1)} %bitcast.15, bf16[2,256,256]{2,1,0:T(8,128)(2,1)S(1)} %get-tuple-element.24.own, bf16[2,256,256]{2,1,0:T(8,128)(2,1)S(1)} %collective-permute-done.core.other, ...), custom_call_target="tpu_custom_call" | custom-call | flops 184549376 | bytes 790528 | tf_op jit(solution)/shard_map/pallas_call | solution.py:50
  14.1 1.2 %collective-permute-start.7 = (bf16[2,192,256]{2,1,0:T(8,128)(2,1)S(1)}, bf16[2,192,256]{2,1,0:T(8,128)(2,1)S(1)}, u32[]{:S(2)}, u32[]{:S(2)}) collective-permute-start(bf16[2,192,256]{2,1,0:T(8,128)(2,1)S(1)} %pad_maximum_fusion), channel_id=1, source_target_pairs={{0,4},{1,2},{2,1},{3,7},{4,0},{5,6},{6,5},{7,3},{8,12},{9,10},{10,... | collective-permute-start | bytes 589832 | tf_op jit(solution)/shard_map/ppermute | solution.py:374
  15.3 0.1 collective-permute-start.6
  15.4 0.8 %collective-permute-done.3.refs_3_ = bf16[136,256]{1,0:T(8,128)(2,1)S(1)} collective-permute-done((bf16[136,256]{1,0:T(8,128)(2,1)S(1)}, bf16[136,256]{1,0:T(8,128)(2,1)S(1)}, u32[]{:S(2)}, u32[]{:S(2)}) %collective-permute-start.3) | collective-permute-done | bytes 69664 | tf_op jit(solution)/shard_map/ppermute | solution.py:404
  16.2 0.1 shard_map.80.refs_0_
  16.3 2.7 %collective-permute-start.10 = (bf16[136,256]{1,0:T(8,128)(2,1)S(1)}, bf16[136,256]{1,0:T(8,128)(2,1)S(1)}, u32[]{:S(2)}, u32[]{:S(2)}) collective-permute-start(bf16[136,256]{1,0:T(8,128)(2,1)S(1)} %shard_map.80.refs_0_), channel_id=1, source_target_pairs={{0,6},{1,25},{2,26},{3,5},{4,28},{5,3},{6,0},{7,31},{8,16},{9,15},... | collective-permute-start | bytes 208904 | tf_op jit(solution)/shard_map/ppermute | solution.py:404
  19.0 0.6 %collective-permute-start.9 = (bf16[136,256]{1,0:T(8,128)(2,1)S(1)}, bf16[136,256]{1,0:T(8,128)(2,1)S(1)}, u32[]{:S(2)}, u32[]{:S(2)}) collective-permute-start(bf16[136,256]{1,0:T(8,128)(2,1)S(1)} %shard_map.80.refs_0_), channel_id=1, source_target_pairs={{0,5},{1,16},{2,19},{3,6},{4,21},{5,0},{6,3},{7,22},{8,25},{9,12},... | collective-permute-start | bytes 208904 | tf_op jit(solution)/shard_map/ppermute | solution.py:404
  19.6 0.2 collective-permute-done.7.cross
  19.8 1.2 %shard_map.81 = (f32[256,256]{1,0:T(8,128)S(1)}, f32[256,256]{1,0:T(8,128)S(1)}) custom-call(bf16[256,256]{1,0:T(8,128)(2,1)S(1)} %bitcast.16, bf16[2,96,256]{2,1,0:T(8,128)(2,1)S(1)} %collective-permute-done.4.a, bf16[2,96,256]{2,1,0:T(8,128)(2,1)S(1)} %collective-permute-done.5.b, bf16[2,96,256]{2,1,0:T(8,128)(2,1)S(1)} %collective-permute-done.6.corner, ...), custom_call_target="tpu_custom_call" | custom-call | flops 251658240 | bytes 1150976 | tf_op jit(solution)/shard_map/pallas_call | solution.py:50
  21.0 0.6 %collective-permute-done.10.refs_3_ = bf16[136,256]{1,0:T(8,128)(2,1)S(1)} collective-permute-done((bf16[136,256]{1,0:T(8,128)(2,1)S(1)}, bf16[136,256]{1,0:T(8,128)(2,1)S(1)}, u32[]{:S(2)}, u32[]{:S(2)}) %collective-permute-start.10) | collective-permute-done | bytes 69664 | tf_op jit(solution)/shard_map/ppermute | solution.py:404
  21.6 1.2 %collective-permute-done.8.refs_1_ = bf16[136,256]{1,0:T(8,128)(2,1)S(1)} collective-permute-done((bf16[136,256]{1,0:T(8,128)(2,1)S(1)}, bf16[136,256]{1,0:T(8,128)(2,1)S(1)}, u32[]{:S(2)}, u32[]{:S(2)}) %collective-permute-start.8) | collective-permute-done | bytes 69664 | tf_op jit(solution)/shard_map/ppermute | solution.py:404
  22.8 0.1 shard_map.82.mine
  22.9 0.3 %collective-permute-start.11 = (bf16[128,256]{1,0:T(8,128)(2,1)S(1)}, bf16[128,256]{1,0:T(8,128)(2,1)S(1)}, u32[]{:S(2)}, u32[]{:S(2)}) collective-permute-start(bf16[128,256]{1,0:T(8,128)(2,1)S(1)} %shard_map.82.mine), channel_id=1, source_target_pairs={{0,1},{1,0},{2,3},{3,2},{4,5},{5,4},{6,7},{7,6},{8,9},{9,8},{10,11... | collective-permute-start | bytes 196616 | tf_op jit(solution)/shard_map/ppermute | solution.py:308
  23.2 1.0 %collective-permute-done.11.other = bf16[128,256]{1,0:T(8,128)(2,1)S(1)} collective-permute-done((bf16[128,256]{1,0:T(8,128)(2,1)S(1)}, bf16[128,256]{1,0:T(8,128)(2,1)S(1)}, u32[]{:S(2)}, u32[]{:S(2)}) %collective-permute-start.11) | collective-permute-done | bytes 65568 | tf_op jit(solution)/shard_map/ppermute | solution.py:308
  24.2 1.0 %shard_map.83 = (bf16[256,256]{1,0:T(8,128)(2,1)}, bf16[256,256]{1,0:T(8,128)(2,1)}) custom-call(f32[256,256]{1,0:T(8,128)S(1)} %get-tuple-element.26.inner, f32[256,256]{1,0:T(8,128)S(1)} %get-tuple-element.40.factor, f32[256,256]{1,0:T(8,128)S(1)} %get-tuple-element.41.rest, bf16[4,256,256]{2,1,0:T(8,128)(2,1)S(1)} %get-tuple-element.42.reg_weights, ...), custom_call_target="tpu_custom_call" | custom-call | flops 67108864 | bytes 1441792 | tf_op jit(solution)/shard_map/pallas_call | solution.py:50
  (16 shorter events, 0.1 us)
Async XLA Ops:
  0.6 7.3 %collective-permute-start = (bf16[2,256,256]{2,1,0:T(8,128)(2,1)}, bf16[2,256,256]{2,1,0:T(8,128)(2,1)S(1)}, u32[]{:S(2)}, u32[]{:S(2)}) collective-permute-start(bf16[2,256,256]{2,1,0:T(8,128)(2,1)} %bitcast.21), channel_id=1, source_target_pairs={{0,1},{1,0},{2,3},{3,2},{4,5},{5,4},{6,7},{7,6},{8,9},{9,8},{10,11... | collective-permute-start | bytes 786440 | tf_op jit(solution)/shard_map/ppermute | solution.py:308
  2.3 11.7 %collective-permute-start.5 = (bf16[2,96,256]{2,1,0:T(8,128)(2,1)S(1)}, bf16[2,96,256]{2,1,0:T(8,128)(2,1)S(1)}, u32[]{:S(2)}, u32[]{:S(2)}) collective-permute-start(bf16[2,96,256]{2,1,0:T(8,128)(2,1)S(1)} %get-tuple-element.31), channel_id=1, source_target_pairs={{0,28},{4,8},{8,4},{12,16},{16,12},{20,24},{24,20},{28,0},{1,29},{... | collective-permute-start | bytes 294920 | tf_op jit(solution)/shard_map/ppermute | solution.py:334
  7.9 6.1 %collective-permute-start.4 = (bf16[2,96,256]{2,1,0:T(8,128)(2,1)S(1)}, bf16[2,96,256]{2,1,0:T(8,128)(2,1)S(1)}, u32[]{:S(2)}, u32[]{:S(2)}) collective-permute-start(bf16[2,96,256]{2,1,0:T(8,128)(2,1)S(1)} %get-tuple-element.30), channel_id=1, source_target_pairs={{0,4},{1,5},{2,6},{3,7},{4,0},{5,1},{6,2},{7,3},{8,12},{9,13},{10,... | collective-permute-start | bytes 294920 | tf_op jit(solution)/shard_map/ppermute | solution.py:308
  8.0 4.9 %copy-start = (bf16[16,16,256]{2,1,0:T(8,128)(2,1)S(1)}, bf16[16,16,256]{2,1,0:T(8,128)(2,1)}, u32[]{:S(2)}) copy-start(bf16[16,16,256]{2,1,0:T(8,128)(2,1)} %param.6) | copy-start | bytes 393220
  8.0 4.9 %copy-start.1 = (bf16[256,256]{1,0:T(8,128)(2,1)S(1)}, bf16[256,256]{1,0:T(8,128)(2,1)}, u32[]{:S(2)}) copy-start(bf16[256,256]{1,0:T(8,128)(2,1)} %reg_keys.1) | copy-start | bytes 393220
  8.7 6.8 %collective-permute-start.1 = (bf16[136,256]{1,0:T(8,128)(2,1)S(1)}, bf16[136,256]{1,0:T(8,128)(2,1)S(1)}, u32[]{:S(2)}, u32[]{:S(2)}) collective-permute-start(bf16[136,256]{1,0:T(8,128)(2,1)S(1)} %shard_map.79.refs_0_), channel_id=1, source_target_pairs={{0,9},{1,2},{2,1},{3,10},{4,7},{5,12},{6,15},{7,4},{8,11},{9,0},{1... | collective-permute-start | bytes 208904 | tf_op jit(solution)/shard_map/ppermute | solution.py:404
  8.7 6.7 %collective-permute-start.2 = (bf16[136,256]{1,0:T(8,128)(2,1)S(1)}, bf16[136,256]{1,0:T(8,128)(2,1)S(1)}, u32[]{:S(2)}, u32[]{:S(2)}) collective-permute-start(bf16[136,256]{1,0:T(8,128)(2,1)S(1)} %shard_map.79.refs_0_), channel_id=1, source_target_pairs={{0,17},{1,4},{2,7},{3,18},{4,1},{5,20},{6,23},{7,2},{8,13},{9,24},... | collective-permute-start | bytes 208904 | tf_op jit(solution)/shard_map/ppermute | solution.py:404
  10.1 6.1 %collective-permute-start.3 = (bf16[136,256]{1,0:T(8,128)(2,1)S(1)}, bf16[136,256]{1,0:T(8,128)(2,1)S(1)}, u32[]{:S(2)}, u32[]{:S(2)}) collective-permute-start(bf16[136,256]{1,0:T(8,128)(2,1)S(1)} %shard_map.79.refs_0_), channel_id=1, source_target_pairs={{0,24},{1,7},{2,4},{3,27},{4,2},{5,29},{6,30},{7,1},{8,14},{9,17},... | collective-permute-start | bytes 208904 | tf_op jit(solution)/shard_map/ppermute | solution.py:404
  14.1 5.7 %collective-permute-start.7 = (bf16[2,192,256]{2,1,0:T(8,128)(2,1)S(1)}, bf16[2,192,256]{2,1,0:T(8,128)(2,1)S(1)}, u32[]{:S(2)}, u32[]{:S(2)}) collective-permute-start(bf16[2,192,256]{2,1,0:T(8,128)(2,1)S(1)} %pad_maximum_fusion), channel_id=1, source_target_pairs={{0,4},{1,2},{2,1},{3,7},{4,0},{5,6},{6,5},{7,3},{8,12},{9,10},{10,... | collective-permute-start | bytes 589832 | tf_op jit(solution)/shard_map/ppermute | solution.py:374
  15.3 4.3 %collective-permute-start.6 = (bf16[2,96,256]{2,1,0:T(8,128)(2,1)S(1)}, bf16[2,96,256]{2,1,0:T(8,128)(2,1)S(1)}, u32[]{:S(2)}, u32[]{:S(2)}) collective-permute-start(bf16[2,96,256]{2,1,0:T(8,128)(2,1)S(1)} %pad_maximum_fusion.1), channel_id=1, source_target_pairs={{0,1},{1,0},{2,3},{3,2},{4,5},{5,4},{6,7},{7,6},{8,9},{9,8},{10,11... | collective-permute-start | bytes 294920 | tf_op jit(solution)/shard_map/ppermute | solution.py:308
  16.3 5.3 %collective-permute-start.10 = (bf16[136,256]{1,0:T(8,128)(2,1)S(1)}, bf16[136,256]{1,0:T(8,128)(2,1)S(1)}, u32[]{:S(2)}, u32[]{:S(2)}) collective-permute-start(bf16[136,256]{1,0:T(8,128)(2,1)S(1)} %shard_map.80.refs_0_), channel_id=1, source_target_pairs={{0,6},{1,25},{2,26},{3,5},{4,28},{5,3},{6,0},{7,31},{8,16},{9,15},... | collective-permute-start | bytes 208904 | tf_op jit(solution)/shard_map/ppermute | solution.py:404
  19.0 3.7 %collective-permute-start.8 = (bf16[136,256]{1,0:T(8,128)(2,1)S(1)}, bf16[136,256]{1,0:T(8,128)(2,1)S(1)}, u32[]{:S(2)}, u32[]{:S(2)}) collective-permute-start(bf16[136,256]{1,0:T(8,128)(2,1)S(1)} %shard_map.80.refs_0_), channel_id=1, source_target_pairs={{0,3},{1,8},{2,11},{3,0},{4,13},{5,6},{6,5},{7,14},{8,1},{9,10},{1... | collective-permute-start | bytes 208904 | tf_op jit(solution)/shard_map/ppermute | solution.py:404
  19.0 3.7 %collective-permute-start.9 = (bf16[136,256]{1,0:T(8,128)(2,1)S(1)}, bf16[136,256]{1,0:T(8,128)(2,1)S(1)}, u32[]{:S(2)}, u32[]{:S(2)}) collective-permute-start(bf16[136,256]{1,0:T(8,128)(2,1)S(1)} %shard_map.80.refs_0_), channel_id=1, source_target_pairs={{0,5},{1,16},{2,19},{3,6},{4,21},{5,0},{6,3},{7,22},{8,25},{9,12},... | collective-permute-start | bytes 208904 | tf_op jit(solution)/shard_map/ppermute | solution.py:404
  22.9 1.3 %collective-permute-start.11 = (bf16[128,256]{1,0:T(8,128)(2,1)S(1)}, bf16[128,256]{1,0:T(8,128)(2,1)S(1)}, u32[]{:S(2)}, u32[]{:S(2)}) collective-permute-start(bf16[128,256]{1,0:T(8,128)(2,1)S(1)} %shard_map.82.mine), channel_id=1, source_target_pairs={{0,1},{1,0},{2,3},{3,2},{4,5},{5,4},{6,7},{7,6},{8,9},{9,8},{10,11... | collective-permute-start | bytes 196616 | tf_op jit(solution)/shard_map/ppermute | solution.py:308

commit v10 on v9

--- a/solution.py
+++ b/solution.py
@@ -15,6 +15,7 @@
 PAIR = 2 * HEAD_DIM
 DEEP = 8
 STATS = 8
+TURN = 2
 AUG = 128
 MASKED = -8192.0
 SCALE = HEAD_DIM ** (-0.5)
@@ -38,7 +39,8 @@
 
 
 def half():
-    return functools.reduce(jnp.bitwise_xor, place())
+    bits = place()
+    return bits[0] ^ bits[TURN]
 
 
 def iota(shape, axis):
@@ -399,8 +401,8 @@
         for chosen in range(1, 4):
             pairs = []
             for i in range(devices):
-                flips = [b for k, b in enumerate(step[bin(i).count("1") % 2]) if chosen >> k & 1]
-                pairs.append((i, i ^ (sum(1 << b for b in flips) + len(flips) % 2)))
+                flips = [b for k, b in enumerate(step[(i ^ i >> TURN) & 1]) if chosen >> k & 1]
+                pairs.append((i, i ^ (sum(1 << b for b in flips) + (TURN in flips))))
             gathered.append(lax.ppermute(payload, everyone, pairs))
         if first:
             gathered[0], _ = lax.optimization_barrier((gathered[0], mixed))

time: 25.3 us -> 25.1 us (level)
  waiting for transfers between devices: 3.74 us -> 2.55 us
  starting transfers between devices: 15.2 us -> 16.2 us
    ppermute x6, waiting for transfers between devices: 2.5 us -> 1.17 us  [shards(): gathered.append(lax.ppermute(payload, everyone, pairs))]
    ppermute x4, starting transfers between devices: 0.95 us -> 2.2 us  [swap(): return lax.ppermute(x, everyone, [(i, i ^ mask) for i in range(devices)])]
    ppermute x1, starting transfers between devices: 1.18 us -> 0.9 us  [shards(): lax.ppermute(jnp.concatenate([take(own, cells, lat % 2 * (rows - RADIUS)...]
  transfers between devices with their start and end apart: 12 -> 12, of which waited for: 5 -> 6; matrix products, arithmetic and copies ran while one was open for 0% -> 0% of each run, Pallas kernels for 17% -> 17%
where the time goes in v10:
time: 25.1 us; the launch traced here: 25 us
  starting transfers between devices  16.2 us (65%)
  Pallas kernels  5.44 us (22%)
  waiting for transfers between devices  2.55 us (10%)
  between operations  0.74 us (3%)
    ppermute x6, starting transfers between devices, shards(): gathered.append(lax.ppermute(payload, everyone, pairs))  7.45 us
    ppermute x1, starting transfers between devices, shards(): lax.ppermute(far_cols, 'lon', [(i, (i + 1 if i % 2 else i - 1) % lons) fo...  5.63 us
    pallas_call x7, Pallas kernels, call(): pl.pallas_call(kernel, out_shape=out, in_specs=specs, out_specs=jax.tree....  5.44 us
    ppermute x4, starting transfers between devices, swap(): return lax.ppermute(x, everyone, [(i, i ^ mask) for i in range(devices)])  2.2 us
    ppermute x6, waiting for transfers between devices, shards(): gathered.append(lax.ppermute(payload, everyone, pairs))  1.17 us
    ppermute x4, waiting for transfers between devices, swap(): return lax.ppermute(x, everyone, [(i, i ^ mask) for i in range(devices)])  0.91 us
    ppermute x1, starting transfers between devices, shards(): lax.ppermute(jnp.concatenate([take(own, cells, lat % 2 * (rows - RADIUS)...  0.9 us
  transfers between devices with their start and end apart: 12, of which 6 were waited for; matrix products, arithmetic and copies ran while one was open for 0% of the time, Pallas kernels for 17%

profile of v10, /device:TPU:0, one launch (start us, length us, event | category | flops | bytes accessed | tf_op | source)
XLA Modules:
  0.0 25.0 jit_solution(5486372728500269139)
XLA Ops:
  0.6 0.5 %collective-permute-start = (bf16[2,256,256]{2,1,0:T(8,128)(2,1)}, bf16[2,256,256]{2,1,0:T(8,128)(2,1)S(1)}, u32[]{:S(2)}, u32[]{:S(2)}) collective-permute-start(bf16[2,256,256]{2,1,0:T(8,128)(2,1)} %bitcast.21), channel_id=1, source_target_pairs={{0,1},{1,0},{2,3},{3,2},{4,5},{5,4},{6,7},{7,6},{8,9},{9,8},{10,11... | collective-permute-start | bytes 786440 | tf_op jit(solution)/shard_map/ppermute | solution.py:310
  1.1 1.2 %shard_map.77 = (bf16[2,256,256]{2,1,0:T(8,128)(2,1)S(1)}, bf16[256,256]{1,0:T(8,128)(2,1)S(1)}, bf16[2,96,256]{2,1,0:T(8,128)(2,1)S(1)}, bf16[2,96,256]{2,1,0:T(8,128)(2,1)S(1)}, f32[8,128]{1,0:T(8,128)S(1)}) custom-call(bf16[2,256,256]{2,1,0:T(8,128)(2,1)} %bitcast.22, bf16[256,256]{1,0:T(8,128)(2,1)} %queries_ref.1, s32[8]{0:T(128)} %pole_ref.1, ...), custom_call_target="tpu_custom_call" | custom-call | bytes 393760 | tf_op jit(solution)/shard_map/pallas_call | solution.py:52
  2.3 5.6 %collective-permute-start.5 = (bf16[2,96,256]{2,1,0:T(8,128)(2,1)S(1)}, bf16[2,96,256]{2,1,0:T(8,128)(2,1)S(1)}, u32[]{:S(2)}, u32[]{:S(2)}) collective-permute-start(bf16[2,96,256]{2,1,0:T(8,128)(2,1)S(1)} %get-tuple-element.31), channel_id=1, source_target_pairs={{0,28},{4,8},{8,4},{12,16},{16,12},{20,24},{24,20},{28,0},{1,29},{... | collective-permute-start | bytes 294920 | tf_op jit(solution)/shard_map/ppermute | solution.py:336
  8.0 0.7 %shard_map.79.refs_0_ = bf16[136,256]{1,0:T(8,128)(2,1)S(1)} custom-call(bf16[2,256,256]{2,1,0:T(8,128)(2,1)S(1)} %get-tuple-element.24.own, bf16[2,256,256]{2,1,0:T(8,128)(2,1)S(1)} %collective-permute-done.core.other, bf16[256,256]{1,0:T(8,128)(2,1)S(1)} %get-tuple-element.27.queries), custom_call_target="tpu_custom_call" | custom-call | flops 134217728 | bytes 655360 | tf_op jit(solution)/shard_map/pallas_call | solution.py:52
  8.7 0.1 collective-permute-start.1
  8.8 1.6 %collective-permute-start.2 = (bf16[136,256]{1,0:T(8,128)(2,1)S(1)}, bf16[136,256]{1,0:T(8,128)(2,1)S(1)}, u32[]{:S(2)}, u32[]{:S(2)}) collective-permute-start(bf16[136,256]{1,0:T(8,128)(2,1)S(1)} %shard_map.79.refs_0_), channel_id=1, source_target_pairs={{0,16},{1,4},{2,18},{3,6},{4,1},{5,21},{6,3},{7,23},{8,24},{9,12},... | collective-permute-start | bytes 208904 | tf_op jit(solution)/shard_map/ppermute | solution.py:406
  10.3 2.8 %collective-permute-start.3 = (bf16[136,256]{1,0:T(8,128)(2,1)S(1)}, bf16[136,256]{1,0:T(8,128)(2,1)S(1)}, u32[]{:S(2)}, u32[]{:S(2)}) collective-permute-start(bf16[136,256]{1,0:T(8,128)(2,1)S(1)} %shard_map.79.refs_0_), channel_id=1, source_target_pairs={{0,24},{1,6},{2,26},{3,4},{4,3},{5,29},{6,1},{7,31},{8,16},{9,14},... | collective-permute-start | bytes 208904 | tf_op jit(solution)/shard_map/ppermute | solution.py:406
  13.1 1.2 %shard_map.78 = (f32[256,256]{1,0:T(8,128)S(1)}, f32[256,256]{1,0:T(8,128)S(1)}, f32[256,256]{1,0:T(8,128)S(1)}, bf16[4,256,256]{2,1,0:T(8,128)(2,1)S(1)}) custom-call(bf16[256,256]{1,0:T(8,128)(2,1)S(1)} %bitcast.15, bf16[2,256,256]{2,1,0:T(8,128)(2,1)S(1)} %get-tuple-element.24.own, bf16[2,256,256]{2,1,0:T(8,128)(2,1)S(1)} %collective-permute-done.core.other, ...), custom_call_target="tpu_custom_call" | custom-call | flops 184549376 | bytes 790528 | tf_op jit(solution)/shard_map/pallas_call | solution.py:52
  14.4 0.9 %collective-permute-start.7 = (bf16[2,192,256]{2,1,0:T(8,128)(2,1)S(1)}, bf16[2,192,256]{2,1,0:T(8,128)(2,1)S(1)}, u32[]{:S(2)}, u32[]{:S(2)}) collective-permute-start(bf16[2,192,256]{2,1,0:T(8,128)(2,1)S(1)} %pad_maximum_fusion), channel_id=1, source_target_pairs={{0,4},{1,2},{2,1},{3,7},{4,0},{5,6},{6,5},{7,3},{8,12},{9,10},{10,... | collective-permute-start | bytes 589832 | tf_op jit(solution)/shard_map/ppermute | solution.py:376
  15.3 0.8 %collective-permute-start.6 = (bf16[2,96,256]{2,1,0:T(8,128)(2,1)S(1)}, bf16[2,96,256]{2,1,0:T(8,128)(2,1)S(1)}, u32[]{:S(2)}, u32[]{:S(2)}) collective-permute-start(bf16[2,96,256]{2,1,0:T(8,128)(2,1)S(1)} %pad_maximum_fusion.1), channel_id=1, source_target_pairs={{0,1},{1,0},{2,3},{3,2},{4,5},{5,4},{6,7},{7,6},{8,9},{9,8},{10,11... | collective-permute-start | bytes 294920 | tf_op jit(solution)/shard_map/ppermute | solution.py:310
  16.1 0.4 %collective-permute-done.3.refs_3_ = bf16[136,256]{1,0:T(8,128)(2,1)S(1)} collective-permute-done((bf16[136,256]{1,0:T(8,128)(2,1)S(1)}, bf16[136,256]{1,0:T(8,128)(2,1)S(1)}, u32[]{:S(2)}, u32[]{:S(2)}) %collective-permute-start.3) | collective-permute-done | bytes 69664 | tf_op jit(solution)/shard_map/ppermute | solution.py:406
  16.5 0.1 shard_map.80.refs_0_
  16.7 0.9 %collective-permute-start.10 = (bf16[136,256]{1,0:T(8,128)(2,1)S(1)}, bf16[136,256]{1,0:T(8,128)(2,1)S(1)}, u32[]{:S(2)}, u32[]{:S(2)}) collective-permute-start(bf16[136,256]{1,0:T(8,128)(2,1)S(1)} %shard_map.80.refs_0_), channel_id=1, source_target_pairs={{0,7},{1,25},{2,5},{3,27},{4,28},{5,2},{6,30},{7,0},{8,15},{9,17},... | collective-permute-start | bytes 208904 | tf_op jit(solution)/shard_map/ppermute | solution.py:406
  17.5 0.8 %collective-permute-start.8 = (bf16[136,256]{1,0:T(8,128)(2,1)S(1)}, bf16[136,256]{1,0:T(8,128)(2,1)S(1)}, u32[]{:S(2)}, u32[]{:S(2)}) collective-permute-start(bf16[136,256]{1,0:T(8,128)(2,1)S(1)} %shard_map.80.refs_0_), channel_id=1, source_target_pairs={{0,2},{1,9},{2,0},{3,11},{4,12},{5,7},{6,14},{7,5},{8,10},{9,1},{1... | collective-permute-start | bytes 208904 | tf_op jit(solution)/shard_map/ppermute | solution.py:406
  18.4 1.3 %collective-permute-start.9 = (bf16[136,256]{1,0:T(8,128)(2,1)S(1)}, bf16[136,256]{1,0:T(8,128)(2,1)S(1)}, u32[]{:S(2)}, u32[]{:S(2)}) collective-permute-start(bf16[136,256]{1,0:T(8,128)(2,1)S(1)} %shard_map.80.refs_0_), channel_id=1, source_target_pairs={{0,5},{1,17},{2,7},{3,19},{4,20},{5,0},{6,22},{7,2},{8,13},{9,25},... | collective-permute-start | bytes 208904 | tf_op jit(solution)/shard_map/ppermute | solution.py:406
  19.7 0.5 %collective-permute-done.7.cross = bf16[2,192,256]{2,1,0:T(8,128)(2,1)S(1)} collective-permute-done((bf16[2,192,256]{2,1,0:T(8,128)(2,1)S(1)}, bf16[2,192,256]{2,1,0:T(8,128)(2,1)S(1)}, u32[]{:S(2)}, u32[]{:S(2)}) %collective-permute-start.7) | collective-permute-done | bytes 196640 | tf_op jit(solution)/shard_map/ppermute | solution.py:376
  20.1 1.2 %shard_map.81 = (f32[256,256]{1,0:T(8,128)S(1)}, f32[256,256]{1,0:T(8,128)S(1)}) custom-call(bf16[256,256]{1,0:T(8,128)(2,1)S(1)} %bitcast.16, bf16[2,96,256]{2,1,0:T(8,128)(2,1)S(1)} %collective-permute-done.4.a, bf16[2,96,256]{2,1,0:T(8,128)(2,1)S(1)} %collective-permute-done.5.b, bf16[2,96,256]{2,1,0:T(8,128)(2,1)S(1)} %collective-permute-done.6.corner, ...), custom_call_target="tpu_custom_call" | custom-call | flops 251658240 | bytes 1150976 | tf_op jit(solution)/shard_map/pallas_call | solution.py:52
  21.3 0.1 collective-permute-done.10.refs_3_
  21.4 0.5 %collective-permute-done.8.refs_1_ = bf16[136,256]{1,0:T(8,128)(2,1)S(1)} collective-permute-done((bf16[136,256]{1,0:T(8,128)(2,1)S(1)}, bf16[136,256]{1,0:T(8,128)(2,1)S(1)}, u32[]{:S(2)}, u32[]{:S(2)}) %collective-permute-start.8) | collective-permute-done | bytes 69664 | tf_op jit(solution)/shard_map/ppermute | solution.py:406
  21.8 0.3 %collective-permute-done.9.refs_2_ = bf16[136,256]{1,0:T(8,128)(2,1)S(1)} collective-permute-done((bf16[136,256]{1,0:T(8,128)(2,1)S(1)}, bf16[136,256]{1,0:T(8,128)(2,1)S(1)}, u32[]{:S(2)}, u32[]{:S(2)}) %collective-permute-start.9) | collective-permute-done | bytes 69664 | tf_op jit(solution)/shard_map/ppermute | solution.py:406
  22.1 0.1 shard_map.82.mine
  22.2 0.9 %collective-permute-start.11 = (bf16[128,256]{1,0:T(8,128)(2,1)S(1)}, bf16[128,256]{1,0:T(8,128)(2,1)S(1)}, u32[]{:S(2)}, u32[]{:S(2)}) collective-permute-start(bf16[128,256]{1,0:T(8,128)(2,1)S(1)} %shard_map.82.mine), channel_id=1, source_target_pairs={{0,1},{1,0},{2,3},{3,2},{4,5},{5,4},{6,7},{7,6},{8,9},{9,8},{10,11... | collective-permute-start | bytes 196616 | tf_op jit(solution)/shard_map/ppermute | solution.py:310
  23.1 0.9 %collective-permute-done.11.other = bf16[128,256]{1,0:T(8,128)(2,1)S(1)} collective-permute-done((bf16[128,256]{1,0:T(8,128)(2,1)S(1)}, bf16[128,256]{1,0:T(8,128)(2,1)S(1)}, u32[]{:S(2)}, u32[]{:S(2)}) %collective-permute-start.11) | collective-permute-done | bytes 65568 | tf_op jit(solution)/shard_map/ppermute | solution.py:310
  24.0 1.0 %shard_map.83 = (bf16[256,256]{1,0:T(8,128)(2,1)}, bf16[256,256]{1,0:T(8,128)(2,1)}) custom-call(f32[256,256]{1,0:T(8,128)S(1)} %get-tuple-element.26.inner, f32[256,256]{1,0:T(8,128)S(1)} %get-tuple-element.40.factor, f32[256,256]{1,0:T(8,128)S(1)} %get-tuple-element.41.rest, bf16[4,256,256]{2,1,0:T(8,128)(2,1)S(1)} %get-tuple-element.42.reg_weights, ...), custom_call_target="tpu_custom_call" | custom-call | flops 67108864 | bytes 1441792 | tf_op jit(solution)/shard_map/pallas_call | solution.py:52
  (16 shorter events, 0.1 us)
Async XLA Ops:
  0.6 7.3 %collective-permute-start = (bf16[2,256,256]{2,1,0:T(8,128)(2,1)}, bf16[2,256,256]{2,1,0:T(8,128)(2,1)S(1)}, u32[]{:S(2)}, u32[]{:S(2)}) collective-permute-start(bf16[2,256,256]{2,1,0:T(8,128)(2,1)} %bitcast.21), channel_id=1, source_target_pairs={{0,1},{1,0},{2,3},{3,2},{4,5},{5,4},{6,7},{7,6},{8,9},{9,8},{10,11... | collective-permute-start | bytes 786440 | tf_op jit(solution)/shard_map/ppermute | solution.py:310
  2.3 12.0 %collective-permute-start.5 = (bf16[2,96,256]{2,1,0:T(8,128)(2,1)S(1)}, bf16[2,96,256]{2,1,0:T(8,128)(2,1)S(1)}, u32[]{:S(2)}, u32[]{:S(2)}) collective-permute-start(bf16[2,96,256]{2,1,0:T(8,128)(2,1)S(1)} %get-tuple-element.31), channel_id=1, source_target_pairs={{0,28},{4,8},{8,4},{12,16},{16,12},{20,24},{24,20},{28,0},{1,29},{... | collective-permute-start | bytes 294920 | tf_op jit(solution)/shard_map/ppermute | solution.py:336
  7.9 6.4 %collective-permute-start.4 = (bf16[2,96,256]{2,1,0:T(8,128)(2,1)S(1)}, bf16[2,96,256]{2,1,0:T(8,128)(2,1)S(1)}, u32[]{:S(2)}, u32[]{:S(2)}) collective-permute-start(bf16[2,96,256]{2,1,0:T(8,128)(2,1)S(1)} %get-tuple-element.30), channel_id=1, source_target_pairs={{0,4},{1,5},{2,6},{3,7},{4,0},{5,1},{6,2},{7,3},{8,12},{9,13},{10,... | collective-permute-start | bytes 294920 | tf_op jit(solution)/shard_map/ppermute | solution.py:310
  8.0 5.2 %copy-start = (bf16[16,16,256]{2,1,0:T(8,128)(2,1)S(1)}, bf16[16,16,256]{2,1,0:T(8,128)(2,1)}, u32[]{:S(2)}) copy-start(bf16[16,16,256]{2,1,0:T(8,128)(2,1)} %param.6) | copy-start | bytes 393220
  8.0 5.1 %copy-start.1 = (bf16[256,256]{1,0:T(8,128)(2,1)S(1)}, bf16[256,256]{1,0:T(8,128)(2,1)}, u32[]{:S(2)}) copy-start(bf16[256,256]{1,0:T(8,128)(2,1)} %reg_keys.1) | copy-start | bytes 393220
  8.7 7.5 %collective-permute-start.1 = (bf16[136,256]{1,0:T(8,128)(2,1)S(1)}, bf16[136,256]{1,0:T(8,128)(2,1)S(1)}, u32[]{:S(2)}, u32[]{:S(2)}) collective-permute-start(bf16[136,256]{1,0:T(8,128)(2,1)S(1)} %shard_map.79.refs_0_), channel_id=1, source_target_pairs={{0,8},{1,3},{2,10},{3,1},{4,6},{5,13},{6,4},{7,15},{8,0},{9,11},{1... | collective-permute-start | bytes 208904 | tf_op jit(solution)/shard_map/ppermute | solution.py:406
  8.8 7.4 %collective-permute-start.2 = (bf16[136,256]{1,0:T(8,128)(2,1)S(1)}, bf16[136,256]{1,0:T(8,128)(2,1)S(1)}, u32[]{:S(2)}, u32[]{:S(2)}) collective-permute-start(bf16[136,256]{1,0:T(8,128)(2,1)S(1)} %shard_map.79.refs_0_), channel_id=1, source_target_pairs={{0,16},{1,4},{2,18},{3,6},{4,1},{5,21},{6,3},{7,23},{8,24},{9,12},... | collective-permute-start | bytes 208904 | tf_op jit(solution)/shard_map/ppermute | solution.py:406
  10.3 6.2 %collective-permute-start.3 = (bf16[136,256]{1,0:T(8,128)(2,1)S(1)}, bf16[136,256]{1,0:T(8,128)(2,1)S(1)}, u32[]{:S(2)}, u32[]{:S(2)}) collective-permute-start(bf16[136,256]{1,0:T(8,128)(2,1)S(1)} %shard_map.79.refs_0_), channel_id=1, source_target_pairs={{0,24},{1,6},{2,26},{3,4},{4,3},{5,29},{6,1},{7,31},{8,16},{9,14},... | collective-permute-start | bytes 208904 | tf_op jit(solution)/shard_map/ppermute | solution.py:406
  14.4 5.7 %collective-permute-start.7 = (bf16[2,192,256]{2,1,0:T(8,128)(2,1)S(1)}, bf16[2,192,256]{2,1,0:T(8,128)(2,1)S(1)}, u32[]{:S(2)}, u32[]{:S(2)}) collective-permute-start(bf16[2,192,256]{2,1,0:T(8,128)(2,1)S(1)} %pad_maximum_fusion), channel_id=1, source_target_pairs={{0,4},{1,2},{2,1},{3,7},{4,0},{5,6},{6,5},{7,3},{8,12},{9,10},{10,... | collective-permute-start | bytes 589832 | tf_op jit(solution)/shard_map/ppermute | solution.py:376
  15.3 4.3 %collective-permute-start.6 = (bf16[2,96,256]{2,1,0:T(8,128)(2,1)S(1)}, bf16[2,96,256]{2,1,0:T(8,128)(2,1)S(1)}, u32[]{:S(2)}, u32[]{:S(2)}) collective-permute-start(bf16[2,96,256]{2,1,0:T(8,128)(2,1)S(1)} %pad_maximum_fusion.1), channel_id=1, source_target_pairs={{0,1},{1,0},{2,3},{3,2},{4,5},{5,4},{6,7},{7,6},{8,9},{9,8},{10,11... | collective-permute-start | bytes 294920 | tf_op jit(solution)/shard_map/ppermute | solution.py:310
  16.7 4.7 %collective-permute-start.10 = (bf16[136,256]{1,0:T(8,128)(2,1)S(1)}, bf16[136,256]{1,0:T(8,128)(2,1)S(1)}, u32[]{:S(2)}, u32[]{:S(2)}) collective-permute-start(bf16[136,256]{1,0:T(8,128)(2,1)S(1)} %shard_map.80.refs_0_), channel_id=1, source_target_pairs={{0,7},{1,25},{2,5},{3,27},{4,28},{5,2},{6,30},{7,0},{8,15},{9,17},... | collective-permute-start | bytes 208904 | tf_op jit(solution)/shard_map/ppermute | solution.py:406
  17.5 4.3 %collective-permute-start.8 = (bf16[136,256]{1,0:T(8,128)(2,1)S(1)}, bf16[136,256]{1,0:T(8,128)(2,1)S(1)}, u32[]{:S(2)}, u32[]{:S(2)}) collective-permute-start(bf16[136,256]{1,0:T(8,128)(2,1)S(1)} %shard_map.80.refs_0_), channel_id=1, source_target_pairs={{0,2},{1,9},{2,0},{3,11},{4,12},{5,7},{6,14},{7,5},{8,10},{9,1},{1... | collective-permute-start | bytes 208904 | tf_op jit(solution)/shard_map/ppermute | solution.py:406
  18.4 3.7 %collective-permute-start.9 = (bf16[136,256]{1,0:T(8,128)(2,1)S(1)}, bf16[136,256]{1,0:T(8,128)(2,1)S(1)}, u32[]{:S(2)}, u32[]{:S(2)}) collective-permute-start(bf16[136,256]{1,0:T(8,128)(2,1)S(1)} %shard_map.80.refs_0_), channel_id=1, source_target_pairs={{0,5},{1,17},{2,7},{3,19},{4,20},{5,0},{6,22},{7,2},{8,13},{9,25},... | collective-permute-start | bytes 208904 | tf_op jit(solution)/shard_map/ppermute | solution.py:406
  22.2 1.8 %collective-permute-start.11 = (bf16[128,256]{1,0:T(8,128)(2,1)S(1)}, bf16[128,256]{1,0:T(8,128)(2,1)S(1)}, u32[]{:S(2)}, u32[]{:S(2)}) collective-permute-start(bf16[128,256]{1,0:T(8,128)(2,1)S(1)} %shard_map.82.mine), channel_id=1, source_target_pairs={{0,1},{1,0},{2,3},{3,2},{4,5},{5,4},{6,7},{7,6},{8,9},{9,8},{10,11... | collective-permute-start | bytes 196616 | tf_op jit(solution)/shard_map/ppermute | solution.py:310

commit v11 on v10

--- a/solution.py
+++ b/solution.py
@@ -15,6 +15,7 @@
 PAIR = 2 * HEAD_DIM
 DEEP = 8
 STATS = 8
+NEAR = (1, 2)
 TURN = 2
 AUG = 128
 MASKED = -8192.0
@@ -117,8 +118,13 @@
     payloads, out_ref = refs[:-1], refs[-1]
     here = place()
     found = [(r[:PAIR].astype(F32), r[PAIR:].astype(F32)) for r in payloads]
-    for level, (first, second) in enumerate(zip(*stages)):
-        swap = jnp.where(half() == 0, here[first], here[second]) == 1
+
+    def turned(bits):
+        low, high = (here[b] for b in bits)
+        return (low, high) if bits == NEAR else (high, low ^ high)
+
+    for level, (first, second) in enumerate(zip(*map(turned, stages))):
+        swap = jnp.where(half() == 0, first, second) == 1
         step = 1 << level
         for low in range(len(found)):
             if not low & step:
@@ -284,15 +290,26 @@
         rest_ref[:, lanes] = mixed * (outer * scale)
 
 
-def final_kernel(inner, factor, rest, reg_weights, mine, other, out_ref, reg_out_ref):
-    here = half() == 0
+def shares(inner, factor, rest, reg_weights, vals, which):
+    lanes = pl.ds(pl.multiple_of(which * PAIR, PAIR), PAIR)
     first = iota((inner.shape[0], PAIR), 1) < HEAD_DIM
-    for p in range(2):
-        lanes = slice(p * PAIR, (p + 1) * PAIR)
-        vals = jnp.where(here == (p == 0), mine[...], other[...])
-        added = jnp.where(first, dot(reg_weights[2 * p], vals, NT), dot(reg_weights[2 * p + 1], vals, NT))
-        out_ref[:, lanes] = ((inner[:, lanes] + added) * factor[:, lanes] + rest[:, lanes]).astype(BF16)
-        reg_out_ref[:, lanes] = vals.astype(F32).T.astype(BF16)
+    added = [dot(reg_weights[2 * which + j], vals, NT) for j in range(2)]
+    return (inner[:, lanes] + jnp.where(first, *added)) * factor[:, lanes] + rest[:, lanes]
+
+
+def own_share_kernel(inner, factor, rest, reg_weights, mine, out_ref, reg_out_ref):
+    out_ref[...] = shares(inner, factor, rest, reg_weights, mine[...], half()).astype(BF16)
+    reg_out_ref[...] = mine[...].astype(F32).T.astype(BF16)
+
+
+def final_kernel(inner, factor, rest, reg_weights, own_out, own_reg_out, other, out_ref, reg_out_ref):
+    which = half()
+    own = pl.ds(pl.multiple_of(which * PAIR, PAIR), PAIR)
+    lanes = pl.ds(pl.multiple_of((1 - which) * PAIR, PAIR), PAIR)
+    out_ref[:, own] = own_out[...]
+    reg_out_ref[:, own] = own_reg_out[...]
+    out_ref[:, lanes] = shares(inner, factor, rest, reg_weights, other[...], 1 - which).astype(BF16)
+    reg_out_ref[:, lanes] = other[...].astype(F32).T.astype(BF16)
 
 
 def shards(queries, key_values, pole_mask, sea_mask, reg_queries, reg_keys):
@@ -393,15 +410,17 @@
         flops=2 * 2 * cells * outer * channels * 2,
     )
 
-    near_bits, far_bits = (1, 2), [(b, b + 1) for b in range(3, nbits, 2)]
+    near_bits, far_bits = NEAR, [(b, b + 1) for b in range(3, nbits, 2)]
     steps = list(zip([*far_bits, near_bits], [near_bits, *far_bits]))
     for step in steps:
         first, last = step is steps[0], step is steps[-1]
         gathered = [payload]
-        for chosen in range(1, 4):
+        for slot in range(3):
             pairs = []
             for i in range(devices):
-                flips = [b for k, b in enumerate(step[(i ^ i >> TURN) & 1]) if chosen >> k & 1]
+                stage = step[(i ^ i >> TURN) & 1]
+                chosen = slot + 1 if stage == near_bits else (3, 1, 2)[slot]
+                flips = [b for k, b in enumerate(stage) if chosen >> k & 1]
                 pairs.append((i, i ^ (sum(1 << b for b in flips) + (TURN in flips))))
             gathered.append(lax.ppermute(payload, everyone, pairs))
         if first:
@@ -415,14 +434,21 @@
             [VMEM] * len(gathered),
         )
 
+    other = swap(payload, 1)
+    own_out, own_reg_out = call(
+        own_share_kernel,
+        (jax.ShapeDtypeStruct((cells, PAIR), BF16), jax.ShapeDtypeStruct((NREG, PAIR), BF16)),
+        (mixed, factor, rest, reg_weights, payload),
+        [VMEM] * 5,
+    )
     attended, reg_out = call(
         final_kernel,
         (
             jax.ShapeDtypeStruct((cells, channels), BF16),
             jax.ShapeDtypeStruct((NREG, channels), BF16),
         ),
-        (mixed, factor, rest, reg_weights, payload, swap(payload, 1)),
-        [VMEM] * 6,
+        (mixed, factor, rest, reg_weights, own_out, own_reg_out, other),
+        [VMEM] * 7,
         flops=2 * cells * NREG * channels * 2,
     )
     return attended.reshape(rows, cols, channels), reg_out

time: 25.1 us -> 24.9 us (level)
    ppermute x6, waiting for transfers between devices: 1.17 us -> 0.8 us  [shards(): gathered.append(lax.ppermute(payload, everyone, pairs))]
    ppermute x1, waiting for transfers between devices: 0.46 us -> 0.82 us  [shards(): lax.ppermute(jnp.concatenate([take(own, cells, lat % 2 * (rows - RADIUS)...]
    pallas_call x7 -> x8, Pallas kernels: 5.44 us -> 5.6 us  [call(): pl.pallas_call(kernel, out_shape=out, in_specs=specs, out_specs=jax.tree....]
  transfers between devices with their start and end apart: 12 -> 12, of which waited for: 6 -> 4; matrix products, arithmetic and copies ran while one was open for 0% -> 0% of each run, Pallas kernels for 17% -> 18%
where the time goes in v11:
time: 24.9 us; the launch traced here: 24.8 us
  starting transfers between devices  16 us (64%)
  Pallas kernels  5.6 us (22%)
  waiting for transfers between devices  2.3 us (9%)
  between operations  0.75 us (3%)
    ppermute x6, starting transfers between devices, shards(): gathered.append(lax.ppermute(payload, everyone, pairs))  7.45 us
    ppermute x1, starting transfers between devices, shards(): lax.ppermute(far_cols, 'lon', [(i, (i + 1 if i % 2 else i - 1) % lons) fo...  5.63 us
    pallas_call x8, Pallas kernels, call(): pl.pallas_call(kernel, out_shape=out, in_specs=specs, out_specs=jax.tree....  5.6 us
    ppermute x4, starting transfers between devices, swap(): return lax.ppermute(x, everyone, [(i, i ^ mask) for i in range(devices)])  2.05 us
    ppermute x1, starting transfers between devices, shards(): lax.ppermute(jnp.concatenate([take(own, cells, lat % 2 * (rows - RADIUS)...  0.9 us
    ppermute x1, waiting for transfers between devices, shards(): lax.ppermute(jnp.concatenate([take(own, cells, lat % 2 * (rows - RADIUS)...  0.82 us
    ppermute x6, waiting for transfers between devices, shards(): gathered.append(lax.ppermute(payload, everyone, pairs))  0.8 us
    ppermute x4, waiting for transfers between devices, swap(): return lax.ppermute(x, everyone, [(i, i ^ mask) for i in range(devices)])  0.68 us
  transfers between devices with their start and end apart: 12, of which 4 were waited for; matrix products, arithmetic and copies ran while one was open for 0% of the time, Pallas kernels for 18%

profile of v11, /device:TPU:0, one launch (start us, length us, event | category | flops | bytes accessed | tf_op | source)
XLA Modules:
  0.0 24.8 jit_solution(11031804641852113804)
XLA Ops:
  0.6 0.5 %collective-permute-start = (bf16[2,256,256]{2,1,0:T(8,128)(2,1)}, bf16[2,256,256]{2,1,0:T(8,128)(2,1)S(1)}, u32[]{:S(2)}, u32[]{:S(2)}) collective-permute-start(bf16[2,256,256]{2,1,0:T(8,128)(2,1)} %bitcast.21), channel_id=1, source_target_pairs={{0,1},{1,0},{2,3},{3,2},{4,5},{5,4},{6,7},{7,6},{8,9},{9,8},{10,11... | collective-permute-start | bytes 786440 | tf_op jit(solution)/shard_map/ppermute | solution.py:327
  1.1 1.2 %shard_map.77 = (bf16[2,256,256]{2,1,0:T(8,128)(2,1)S(1)}, bf16[256,256]{1,0:T(8,128)(2,1)S(1)}, bf16[2,96,256]{2,1,0:T(8,128)(2,1)S(1)}, bf16[2,96,256]{2,1,0:T(8,128)(2,1)S(1)}, f32[8,128]{1,0:T(8,128)S(1)}) custom-call(bf16[2,256,256]{2,1,0:T(8,128)(2,1)} %bitcast.22, bf16[256,256]{1,0:T(8,128)(2,1)} %queries_ref.1, s32[8]{0:T(128)} %pole_ref.1, ...), custom_call_target="tpu_custom_call" | custom-call | bytes 393760 | tf_op jit(solution)/shard_map/pallas_call | solution.py:53
  2.3 5.6 %collective-permute-start.5 = (bf16[2,96,256]{2,1,0:T(8,128)(2,1)S(1)}, bf16[2,96,256]{2,1,0:T(8,128)(2,1)S(1)}, u32[]{:S(2)}, u32[]{:S(2)}) collective-permute-start(bf16[2,96,256]{2,1,0:T(8,128)(2,1)S(1)} %get-tuple-element.33), channel_id=1, source_target_pairs={{0,28},{4,8},{8,4},{12,16},{16,12},{20,24},{24,20},{28,0},{1,29},{... | collective-permute-start | bytes 294920 | tf_op jit(solution)/shard_map/ppermute | solution.py:353
  8.0 0.0 copy-start.1
  8.0 0.7 %shard_map.79.refs_0_ = bf16[136,256]{1,0:T(8,128)(2,1)S(1)} custom-call(bf16[2,256,256]{2,1,0:T(8,128)(2,1)S(1)} %get-tuple-element.26.own, bf16[2,256,256]{2,1,0:T(8,128)(2,1)S(1)} %collective-permute-done.core.other, bf16[256,256]{1,0:T(8,128)(2,1)S(1)} %get-tuple-element.29.queries), custom_call_target="tpu_custom_call" | custom-call | flops 134217728 | bytes 655360 | tf_op jit(solution)/shard_map/pallas_call | solution.py:53
  8.7 1.1 %collective-permute-start.1 = (bf16[136,256]{1,0:T(8,128)(2,1)S(1)}, bf16[136,256]{1,0:T(8,128)(2,1)S(1)}, u32[]{:S(2)}, u32[]{:S(2)}) collective-permute-start(bf16[136,256]{1,0:T(8,128)(2,1)S(1)} %shard_map.79.refs_0_), channel_id=1, source_target_pairs={{0,24},{1,3},{2,26},{3,1},{4,6},{5,29},{6,4},{7,31},{8,16},{9,11},... | collective-permute-start | bytes 208904 | tf_op jit(solution)/shard_map/ppermute | solution.py:425
  9.8 0.6 %collective-permute-start.2 = (bf16[136,256]{1,0:T(8,128)(2,1)S(1)}, bf16[136,256]{1,0:T(8,128)(2,1)S(1)}, u32[]{:S(2)}, u32[]{:S(2)}) collective-permute-start(bf16[136,256]{1,0:T(8,128)(2,1)S(1)} %shard_map.79.refs_0_), channel_id=1, source_target_pairs={{0,8},{1,4},{2,10},{3,6},{4,1},{5,13},{6,3},{7,15},{8,0},{9,12},{1... | collective-permute-start | bytes 208904 | tf_op jit(solution)/shard_map/ppermute | solution.py:425
  10.3 2.8 %collective-permute-start.3 = (bf16[136,256]{1,0:T(8,128)(2,1)S(1)}, bf16[136,256]{1,0:T(8,128)(2,1)S(1)}, u32[]{:S(2)}, u32[]{:S(2)}) collective-permute-start(bf16[136,256]{1,0:T(8,128)(2,1)S(1)} %shard_map.79.refs_0_), channel_id=1, source_target_pairs={{0,16},{1,6},{2,18},{3,4},{4,3},{5,21},{6,1},{7,23},{8,24},{9,14},... | collective-permute-start | bytes 208904 | tf_op jit(solution)/shard_map/ppermute | solution.py:425
  13.1 1.2 %shard_map.78 = (f32[256,256]{1,0:T(8,128)S(1)}, f32[256,256]{1,0:T(8,128)S(1)}, f32[256,256]{1,0:T(8,128)S(1)}, bf16[4,256,256]{2,1,0:T(8,128)(2,1)S(1)}) custom-call(bf16[256,256]{1,0:T(8,128)(2,1)S(1)} %bitcast.15, bf16[2,256,256]{2,1,0:T(8,128)(2,1)S(1)} %get-tuple-element.26.own, bf16[2,256,256]{2,1,0:T(8,128)(2,1)S(1)} %collective-permute-done.core.other, ...), custom_call_target="tpu_custom_call" | custom-call | flops 184549376 | bytes 790528 | tf_op jit(solution)/shard_map/pallas_call | solution.py:53
  14.4 0.9 %collective-permute-start.7 = (bf16[2,192,256]{2,1,0:T(8,128)(2,1)S(1)}, bf16[2,192,256]{2,1,0:T(8,128)(2,1)S(1)}, u32[]{:S(2)}, u32[]{:S(2)}) collective-permute-start(bf16[2,192,256]{2,1,0:T(8,128)(2,1)S(1)} %pad_maximum_fusion), channel_id=1, source_target_pairs={{0,4},{1,2},{2,1},{3,7},{4,0},{5,6},{6,5},{7,3},{8,12},{9,10},{10,... | collective-permute-start | bytes 589832 | tf_op jit(solution)/shard_map/ppermute | solution.py:393
  15.3 0.8 %collective-permute-start.6 = (bf16[2,96,256]{2,1,0:T(8,128)(2,1)S(1)}, bf16[2,96,256]{2,1,0:T(8,128)(2,1)S(1)}, u32[]{:S(2)}, u32[]{:S(2)}) collective-permute-start(bf16[2,96,256]{2,1,0:T(8,128)(2,1)S(1)} %pad_maximum_fusion.1), channel_id=1, source_target_pairs={{0,1},{1,0},{2,3},{3,2},{4,5},{5,4},{6,7},{7,6},{8,9},{9,8},{10,11... | collective-permute-start | bytes 294920 | tf_op jit(solution)/shard_map/ppermute | solution.py:327
  16.1 0.2 shard_map.80.refs_0_
  16.3 0.8 %collective-permute-start.10 = (bf16[136,256]{1,0:T(8,128)(2,1)S(1)}, bf16[136,256]{1,0:T(8,128)(2,1)S(1)}, u32[]{:S(2)}, u32[]{:S(2)}) collective-permute-start(bf16[136,256]{1,0:T(8,128)(2,1)S(1)} %shard_map.80.refs_0_), channel_id=1, source_target_pairs={{0,7},{1,17},{2,5},{3,19},{4,20},{5,2},{6,22},{7,0},{8,15},{9,25},... | collective-permute-start | bytes 208904 | tf_op jit(solution)/shard_map/ppermute | solution.py:425
  17.1 1.2 %collective-permute-start.8 = (bf16[136,256]{1,0:T(8,128)(2,1)S(1)}, bf16[136,256]{1,0:T(8,128)(2,1)S(1)}, u32[]{:S(2)}, u32[]{:S(2)}) collective-permute-start(bf16[136,256]{1,0:T(8,128)(2,1)S(1)} %shard_map.80.refs_0_), channel_id=1, source_target_pairs={{0,2},{1,25},{2,0},{3,27},{4,28},{5,7},{6,30},{7,5},{8,10},{9,17},... | collective-permute-start | bytes 208904 | tf_op jit(solution)/shard_map/ppermute | solution.py:425
  18.4 0.9 %collective-permute-start.9 = (bf16[136,256]{1,0:T(8,128)(2,1)S(1)}, bf16[136,256]{1,0:T(8,128)(2,1)S(1)}, u32[]{:S(2)}, u32[]{:S(2)}) collective-permute-start(bf16[136,256]{1,0:T(8,128)(2,1)S(1)} %shard_map.80.refs_0_), channel_id=1, source_target_pairs={{0,5},{1,9},{2,7},{3,11},{4,12},{5,0},{6,14},{7,2},{8,13},{9,1},{1... | collective-permute-start | bytes 208904 | tf_op jit(solution)/shard_map/ppermute | solution.py:425
  19.3 0.8 %collective-permute-done.7.cross = bf16[2,192,256]{2,1,0:T(8,128)(2,1)S(1)} collective-permute-done((bf16[2,192,256]{2,1,0:T(8,128)(2,1)S(1)}, bf16[2,192,256]{2,1,0:T(8,128)(2,1)S(1)}, u32[]{:S(2)}, u32[]{:S(2)}) %collective-permute-start.7) | collective-permute-done | bytes 196640 | tf_op jit(solution)/shard_map/ppermute | solution.py:393
  20.1 1.2 %shard_map.81 = (f32[256,256]{1,0:T(8,128)S(1)}, f32[256,256]{1,0:T(8,128)S(1)}) custom-call(bf16[256,256]{1,0:T(8,128)(2,1)S(1)} %bitcast.16, bf16[2,96,256]{2,1,0:T(8,128)(2,1)S(1)} %collective-permute-done.4.a, bf16[2,96,256]{2,1,0:T(8,128)(2,1)S(1)} %collective-permute-done.5.b, bf16[2,96,256]{2,1,0:T(8,128)(2,1)S(1)} %collective-permute-done.6.corner, ...), custom_call_target="tpu_custom_call" | custom-call | flops 251658240 | bytes 1150976 | tf_op jit(solution)/shard_map/pallas_call | solution.py:53
  21.3 0.1 collective-permute-done.8.refs_1_
  21.4 0.7 %collective-permute-done.9.refs_2_ = bf16[136,256]{1,0:T(8,128)(2,1)S(1)} collective-permute-done((bf16[136,256]{1,0:T(8,128)(2,1)S(1)}, bf16[136,256]{1,0:T(8,128)(2,1)S(1)}, u32[]{:S(2)}, u32[]{:S(2)}) %collective-permute-start.9) | collective-permute-done | bytes 69664 | tf_op jit(solution)/shard_map/ppermute | solution.py:425
  22.1 0.1 shard_map.82.mine
  22.3 0.7 %collective-permute-start.11 = (bf16[128,256]{1,0:T(8,128)(2,1)S(1)}, bf16[128,256]{1,0:T(8,128)(2,1)S(1)}, u32[]{:S(2)}, u32[]{:S(2)}) collective-permute-start(bf16[128,256]{1,0:T(8,128)(2,1)S(1)} %shard_map.82.mine), channel_id=1, source_target_pairs={{0,1},{1,0},{2,3},{3,2},{4,5},{5,4},{6,7},{7,6},{8,9},{9,8},{10,11... | collective-permute-start | bytes 196616 | tf_op jit(solution)/shard_map/ppermute | solution.py:327
  23.0 0.2 shard_map.83
  23.2 0.7 %collective-permute-done.11.other = bf16[128,256]{1,0:T(8,128)(2,1)S(1)} collective-permute-done((bf16[128,256]{1,0:T(8,128)(2,1)S(1)}, bf16[128,256]{1,0:T(8,128)(2,1)S(1)}, u32[]{:S(2)}, u32[]{:S(2)}) %collective-permute-start.11) | collective-permute-done | bytes 65568 | tf_op jit(solution)/shard_map/ppermute | solution.py:327
  23.9 0.9 %shard_map.84 = (bf16[256,256]{1,0:T(8,128)(2,1)}, bf16[256,256]{1,0:T(8,128)(2,1)}) custom-call(f32[256,256]{1,0:T(8,128)S(1)} %get-tuple-element.28.inner, f32[256,256]{1,0:T(8,128)S(1)} %get-tuple-element.42.factor, f32[256,256]{1,0:T(8,128)S(1)} %get-tuple-element.43.rest, bf16[4,256,256]{2,1,0:T(8,128)(2,1)S(1)} %get-tuple-element.44.reg_weights, ...), custom_call_target="tpu_custom_call" | custom-call | flops 67108864 | bytes 1507328 | tf_op jit(solution)/shard_map/pallas_call | solution.py:53
  (17 shorter events, 0.1 us)
Async XLA Ops:
  0.6 7.3 %collective-permute-start = (bf16[2,256,256]{2,1,0:T(8,128)(2,1)}, bf16[2,256,256]{2,1,0:T(8,128)(2,1)S(1)}, u32[]{:S(2)}, u32[]{:S(2)}) collective-permute-start(bf16[2,256,256]{2,1,0:T(8,128)(2,1)} %bitcast.21), channel_id=1, source_target_pairs={{0,1},{1,0},{2,3},{3,2},{4,5},{5,4},{6,7},{7,6},{8,9},{9,8},{10,11... | collective-permute-start | bytes 786440 | tf_op jit(solution)/shard_map/ppermute | solution.py:327
  2.3 12.0 %collective-permute-start.5 = (bf16[2,96,256]{2,1,0:T(8,128)(2,1)S(1)}, bf16[2,96,256]{2,1,0:T(8,128)(2,1)S(1)}, u32[]{:S(2)}, u32[]{:S(2)}) collective-permute-start(bf16[2,96,256]{2,1,0:T(8,128)(2,1)S(1)} %get-tuple-element.33), channel_id=1, source_target_pairs={{0,28},{4,8},{8,4},{12,16},{16,12},{20,24},{24,20},{28,0},{1,29},{... | collective-permute-start | bytes 294920 | tf_op jit(solution)/shard_map/ppermute | solution.py:353
  7.9 6.4 %collective-permute-start.4 = (bf16[2,96,256]{2,1,0:T(8,128)(2,1)S(1)}, bf16[2,96,256]{2,1,0:T(8,128)(2,1)S(1)}, u32[]{:S(2)}, u32[]{:S(2)}) collective-permute-start(bf16[2,96,256]{2,1,0:T(8,128)(2,1)S(1)} %get-tuple-element.32), channel_id=1, source_target_pairs={{0,4},{1,5},{2,6},{3,7},{4,0},{5,1},{6,2},{7,3},{8,12},{9,13},{10,... | collective-permute-start | bytes 294920 | tf_op jit(solution)/shard_map/ppermute | solution.py:327
  8.0 5.2 %copy-start = (bf16[16,16,256]{2,1,0:T(8,128)(2,1)S(1)}, bf16[16,16,256]{2,1,0:T(8,128)(2,1)}, u32[]{:S(2)}) copy-start(bf16[16,16,256]{2,1,0:T(8,128)(2,1)} %param.6) | copy-start | bytes 393220
  8.0 5.1 %copy-start.1 = (bf16[256,256]{1,0:T(8,128)(2,1)S(1)}, bf16[256,256]{1,0:T(8,128)(2,1)}, u32[]{:S(2)}) copy-start(bf16[256,256]{1,0:T(8,128)(2,1)} %reg_keys.1) | copy-start | bytes 393220
  8.7 7.5 %collective-permute-start.1 = (bf16[136,256]{1,0:T(8,128)(2,1)S(1)}, bf16[136,256]{1,0:T(8,128)(2,1)S(1)}, u32[]{:S(2)}, u32[]{:S(2)}) collective-permute-start(bf16[136,256]{1,0:T(8,128)(2,1)S(1)} %shard_map.79.refs_0_), channel_id=1, source_target_pairs={{0,24},{1,3},{2,26},{3,1},{4,6},{5,29},{6,4},{7,31},{8,16},{9,11},... | collective-permute-start | bytes 208904 | tf_op jit(solution)/shard_map/ppermute | solution.py:425
  9.8 6.4 %collective-permute-start.2 = (bf16[136,256]{1,0:T(8,128)(2,1)S(1)}, bf16[136,256]{1,0:T(8,128)(2,1)S(1)}, u32[]{:S(2)}, u32[]{:S(2)}) collective-permute-start(bf16[136,256]{1,0:T(8,128)(2,1)S(1)} %shard_map.79.refs_0_), channel_id=1, source_target_pairs={{0,8},{1,4},{2,10},{3,6},{4,1},{5,13},{6,3},{7,15},{8,0},{9,12},{1... | collective-permute-start | bytes 208904 | tf_op jit(solution)/shard_map/ppermute | solution.py:425
  10.3 5.8 %collective-permute-start.3 = (bf16[136,256]{1,0:T(8,128)(2,1)S(1)}, bf16[136,256]{1,0:T(8,128)(2,1)S(1)}, u32[]{:S(2)}, u32[]{:S(2)}) collective-permute-start(bf16[136,256]{1,0:T(8,128)(2,1)S(1)} %shard_map.79.refs_0_), channel_id=1, source_target_pairs={{0,16},{1,6},{2,18},{3,4},{4,3},{5,21},{6,1},{7,23},{8,24},{9,14},... | collective-permute-start | bytes 208904 | tf_op jit(solution)/shard_map/ppermute | solution.py:425
  14.4 5.7 %collective-permute-start.7 = (bf16[2,192,256]{2,1,0:T(8,128)(2,1)S(1)}, bf16[2,192,256]{2,1,0:T(8,128)(2,1)S(1)}, u32[]{:S(2)}, u32[]{:S(2)}) collective-permute-start(bf16[2,192,256]{2,1,0:T(8,128)(2,1)S(1)} %pad_maximum_fusion), channel_id=1, source_target_pairs={{0,4},{1,2},{2,1},{3,7},{4,0},{5,6},{6,5},{7,3},{8,12},{9,10},{10,... | collective-permute-start | bytes 589832 | tf_op jit(solution)/shard_map/ppermute | solution.py:393
  15.3 4.0 %collective-permute-start.6 = (bf16[2,96,256]{2,1,0:T(8,128)(2,1)S(1)}, bf16[2,96,256]{2,1,0:T(8,128)(2,1)S(1)}, u32[]{:S(2)}, u32[]{:S(2)}) collective-permute-start(bf16[2,96,256]{2,1,0:T(8,128)(2,1)S(1)} %pad_maximum_fusion.1), channel_id=1, source_target_pairs={{0,1},{1,0},{2,3},{3,2},{4,5},{5,4},{6,7},{7,6},{8,9},{9,8},{10,11... | collective-permute-start | bytes 294920 | tf_op jit(solution)/shard_map/ppermute | solution.py:327
  16.3 5.0 %collective-permute-start.10 = (bf16[136,256]{1,0:T(8,128)(2,1)S(1)}, bf16[136,256]{1,0:T(8,128)(2,1)S(1)}, u32[]{:S(2)}, u32[]{:S(2)}) collective-permute-start(bf16[136,256]{1,0:T(8,128)(2,1)S(1)} %shard_map.80.refs_0_), channel_id=1, source_target_pairs={{0,7},{1,17},{2,5},{3,19},{4,20},{5,2},{6,22},{7,0},{8,15},{9,25},... | collective-permute-start | bytes 208904 | tf_op jit(solution)/shard_map/ppermute | solution.py:425
  17.1 4.3 %collective-permute-start.8 = (bf16[136,256]{1,0:T(8,128)(2,1)S(1)}, bf16[136,256]{1,0:T(8,128)(2,1)S(1)}, u32[]{:S(2)}, u32[]{:S(2)}) collective-permute-start(bf16[136,256]{1,0:T(8,128)(2,1)S(1)} %shard_map.80.refs_0_), channel_id=1, source_target_pairs={{0,2},{1,25},{2,0},{3,27},{4,28},{5,7},{6,30},{7,5},{8,10},{9,17},... | collective-permute-start | bytes 208904 | tf_op jit(solution)/shard_map/ppermute | solution.py:425
  18.4 3.7 %collective-permute-start.9 = (bf16[136,256]{1,0:T(8,128)(2,1)S(1)}, bf16[136,256]{1,0:T(8,128)(2,1)S(1)}, u32[]{:S(2)}, u32[]{:S(2)}) collective-permute-start(bf16[136,256]{1,0:T(8,128)(2,1)S(1)} %shard_map.80.refs_0_), channel_id=1, source_target_pairs={{0,5},{1,9},{2,7},{3,11},{4,12},{5,0},{6,14},{7,2},{8,13},{9,1},{1... | collective-permute-start | bytes 208904 | tf_op jit(solution)/shard_map/ppermute | solution.py:425
  22.3 1.6 %collective-permute-start.11 = (bf16[128,256]{1,0:T(8,128)(2,1)S(1)}, bf16[128,256]{1,0:T(8,128)(2,1)S(1)}, u32[]{:S(2)}, u32[]{:S(2)}) collective-permute-start(bf16[128,256]{1,0:T(8,128)(2,1)S(1)} %shard_map.82.mine), channel_id=1, source_target_pairs={{0,1},{1,0},{2,3},{3,2},{4,5},{5,4},{6,7},{7,6},{8,9},{9,8},{10,11... | collective-permute-start | bytes 196616 | tf_op jit(solution)/shard_map/ppermute | solution.py:327

commit v12 on v11

--- a/solution.py
+++ b/solution.py
@@ -117,7 +117,7 @@
 def merge_kernel(stages, last, *refs):
     payloads, out_ref = refs[:-1], refs[-1]
     here = place()
-    found = [(r[:PAIR].astype(F32), r[PAIR:].astype(F32)) for r in payloads]
+    found = [r[...] for r in payloads]
 
     def turned(bits):
         low, high = (here[b] for b in bits)
@@ -129,8 +129,8 @@
         for low in range(len(found)):
             if not low & step:
                 a, b = found[low], found[low + step]
-                found[low] = tuple(jnp.where(swap, v, u) for u, v in zip(a, b))
-                found[low + step] = tuple(jnp.where(swap, u, v) for u, v in zip(a, b))
+                found[low], found[low + step] = jnp.where(swap, b, a), jnp.where(swap, a, b)
+    found = [(x[:PAIR].astype(F32), x[PAIR:].astype(F32)) for x in found]
     upper = iota((PAIR, found[0][0].shape[1]), 0) < HEAD_DIM
     tops, sums, factors = [], [], []
     for j in range(2):

time: 24.9 us -> 24.8 us (level)
  no operation moved by 1% of the time
where the time goes in v12:
time: 24.8 us; the launch traced here: 24.7 us
  starting transfers between devices  16 us (65%)
  Pallas kernels  5.53 us (22%)
  waiting for transfers between devices  2.3 us (9%)
  between operations  0.75 us (3%)
    ppermute x6, starting transfers between devices, shards(): gathered.append(lax.ppermute(payload, everyone, pairs))  7.45 us
    ppermute x1, starting transfers between devices, shards(): lax.ppermute(far_cols, 'lon', [(i, (i + 1 if i % 2 else i - 1) % lons) fo...  5.63 us
    pallas_call x8, Pallas kernels, call(): pl.pallas_call(kernel, out_shape=out, in_specs=specs, out_specs=jax.tree....  5.53 us
    ppermute x4, starting transfers between devices, swap(): return lax.ppermute(x, everyone, [(i, i ^ mask) for i in range(devices)])  2.04 us
    ppermute x1, starting transfers between devices, shards(): lax.ppermute(jnp.concatenate([take(own, cells, lat % 2 * (rows - RADIUS)...  0.9 us
    ppermute x1, waiting for transfers between devices, shards(): lax.ppermute(jnp.concatenate([take(own, cells, lat % 2 * (rows - RADIUS)...  0.85 us
    ppermute x6, waiting for transfers between devices, shards(): gathered.append(lax.ppermute(payload, everyone, pairs))  0.77 us
    ppermute x4, waiting for transfers between devices, swap(): return lax.ppermute(x, everyone, [(i, i ^ mask) for i in range(devices)])  0.67 us
  transfers between devices with their start and end apart: 12, of which 4 were waited for; matrix products, arithmetic and copies ran while one was open for 0% of the time, Pallas kernels for 18%

profile of v12, /device:TPU:0, one launch (start us, length us, event | category | flops | bytes accessed | tf_op | source)
XLA Modules:
  0.0 24.7 jit_solution(3997907081844140877)
XLA Ops:
  0.6 0.5 %collective-permute-start = (bf16[2,256,256]{2,1,0:T(8,128)(2,1)}, bf16[2,256,256]{2,1,0:T(8,128)(2,1)S(1)}, u32[]{:S(2)}, u32[]{:S(2)}) collective-permute-start(bf16[2,256,256]{2,1,0:T(8,128)(2,1)} %bitcast.21), channel_id=1, source_target_pairs={{0,1},{1,0},{2,3},{3,2},{4,5},{5,4},{6,7},{7,6},{8,9},{9,8},{10,11... | collective-permute-start | bytes 786440 | tf_op jit(solution)/shard_map/ppermute | solution.py:327
  1.1 1.2 %shard_map.77 = (bf16[2,256,256]{2,1,0:T(8,128)(2,1)S(1)}, bf16[256,256]{1,0:T(8,128)(2,1)S(1)}, bf16[2,96,256]{2,1,0:T(8,128)(2,1)S(1)}, bf16[2,96,256]{2,1,0:T(8,128)(2,1)S(1)}, f32[8,128]{1,0:T(8,128)S(1)}) custom-call(bf16[2,256,256]{2,1,0:T(8,128)(2,1)} %bitcast.22, bf16[256,256]{1,0:T(8,128)(2,1)} %queries_ref.1, s32[8]{0:T(128)} %pole_ref.1, ...), custom_call_target="tpu_custom_call" | custom-call | bytes 393760 | tf_op jit(solution)/shard_map/pallas_call | solution.py:53
  2.3 5.6 %collective-permute-start.5 = (bf16[2,96,256]{2,1,0:T(8,128)(2,1)S(1)}, bf16[2,96,256]{2,1,0:T(8,128)(2,1)S(1)}, u32[]{:S(2)}, u32[]{:S(2)}) collective-permute-start(bf16[2,96,256]{2,1,0:T(8,128)(2,1)S(1)} %get-tuple-element.33), channel_id=1, source_target_pairs={{0,28},{4,8},{8,4},{12,16},{16,12},{20,24},{24,20},{28,0},{1,29},{... | collective-permute-start | bytes 294920 | tf_op jit(solution)/shard_map/ppermute | solution.py:353
  8.0 0.0 copy-start
  8.0 0.7 %shard_map.79.refs_0_ = bf16[136,256]{1,0:T(8,128)(2,1)S(1)} custom-call(bf16[2,256,256]{2,1,0:T(8,128)(2,1)S(1)} %get-tuple-element.26.own, bf16[2,256,256]{2,1,0:T(8,128)(2,1)S(1)} %collective-permute-done.core.other, bf16[256,256]{1,0:T(8,128)(2,1)S(1)} %get-tuple-element.29.queries), custom_call_target="tpu_custom_call" | custom-call | flops 134217728 | bytes 655360 | tf_op jit(solution)/shard_map/pallas_call | solution.py:53
  8.7 1.1 %collective-permute-start.1 = (bf16[136,256]{1,0:T(8,128)(2,1)S(1)}, bf16[136,256]{1,0:T(8,128)(2,1)S(1)}, u32[]{:S(2)}, u32[]{:S(2)}) collective-permute-start(bf16[136,256]{1,0:T(8,128)(2,1)S(1)} %shard_map.79.refs_0_), channel_id=1, source_target_pairs={{0,24},{1,3},{2,26},{3,1},{4,6},{5,29},{6,4},{7,31},{8,16},{9,11},... | collective-permute-start | bytes 208904 | tf_op jit(solution)/shard_map/ppermute | solution.py:425
  9.8 0.6 %collective-permute-start.2 = (bf16[136,256]{1,0:T(8,128)(2,1)S(1)}, bf16[136,256]{1,0:T(8,128)(2,1)S(1)}, u32[]{:S(2)}, u32[]{:S(2)}) collective-permute-start(bf16[136,256]{1,0:T(8,128)(2,1)S(1)} %shard_map.79.refs_0_), channel_id=1, source_target_pairs={{0,8},{1,4},{2,10},{3,6},{4,1},{5,13},{6,3},{7,15},{8,0},{9,12},{1... | collective-permute-start | bytes 208904 | tf_op jit(solution)/shard_map/ppermute | solution.py:425
  10.3 2.8 %collective-permute-start.3 = (bf16[136,256]{1,0:T(8,128)(2,1)S(1)}, bf16[136,256]{1,0:T(8,128)(2,1)S(1)}, u32[]{:S(2)}, u32[]{:S(2)}) collective-permute-start(bf16[136,256]{1,0:T(8,128)(2,1)S(1)} %shard_map.79.refs_0_), channel_id=1, source_target_pairs={{0,16},{1,6},{2,18},{3,4},{4,3},{5,21},{6,1},{7,23},{8,24},{9,14},... | collective-permute-start | bytes 208904 | tf_op jit(solution)/shard_map/ppermute | solution.py:425
  13.1 1.2 %shard_map.78 = (f32[256,256]{1,0:T(8,128)S(1)}, f32[256,256]{1,0:T(8,128)S(1)}, f32[256,256]{1,0:T(8,128)S(1)}, bf16[4,256,256]{2,1,0:T(8,128)(2,1)S(1)}) custom-call(bf16[256,256]{1,0:T(8,128)(2,1)S(1)} %bitcast.15, bf16[2,256,256]{2,1,0:T(8,128)(2,1)S(1)} %get-tuple-element.26.own, bf16[2,256,256]{2,1,0:T(8,128)(2,1)S(1)} %collective-permute-done.core.other, ...), custom_call_target="tpu_custom_call" | custom-call | flops 184549376 | bytes 790528 | tf_op jit(solution)/shard_map/pallas_call | solution.py:53
  14.4 0.9 %collective-permute-start.7 = (bf16[2,192,256]{2,1,0:T(8,128)(2,1)S(1)}, bf16[2,192,256]{2,1,0:T(8,128)(2,1)S(1)}, u32[]{:S(2)}, u32[]{:S(2)}) collective-permute-start(bf16[2,192,256]{2,1,0:T(8,128)(2,1)S(1)} %pad_maximum_fusion), channel_id=1, source_target_pairs={{0,4},{1,2},{2,1},{3,7},{4,0},{5,6},{6,5},{7,3},{8,12},{9,10},{10,... | collective-permute-start | bytes 589832 | tf_op jit(solution)/shard_map/ppermute | solution.py:393
  15.3 0.8 %collective-permute-start.6 = (bf16[2,96,256]{2,1,0:T(8,128)(2,1)S(1)}, bf16[2,96,256]{2,1,0:T(8,128)(2,1)S(1)}, u32[]{:S(2)}, u32[]{:S(2)}) collective-permute-start(bf16[2,96,256]{2,1,0:T(8,128)(2,1)S(1)} %pad_maximum_fusion.1), channel_id=1, source_target_pairs={{0,1},{1,0},{2,3},{3,2},{4,5},{5,4},{6,7},{7,6},{8,9},{9,8},{10,11... | collective-permute-start | bytes 294920 | tf_op jit(solution)/shard_map/ppermute | solution.py:327
  16.1 0.1 shard_map.80.refs_0_
  16.3 0.8 %collective-permute-start.10 = (bf16[136,256]{1,0:T(8,128)(2,1)S(1)}, bf16[136,256]{1,0:T(8,128)(2,1)S(1)}, u32[]{:S(2)}, u32[]{:S(2)}) collective-permute-start(bf16[136,256]{1,0:T(8,128)(2,1)S(1)} %shard_map.80.refs_0_), channel_id=1, source_target_pairs={{0,7},{1,17},{2,5},{3,19},{4,20},{5,2},{6,22},{7,0},{8,15},{9,25},... | collective-permute-start | bytes 208904 | tf_op jit(solution)/shard_map/ppermute | solution.py:425
  17.1 1.3 %collective-permute-start.8 = (bf16[136,256]{1,0:T(8,128)(2,1)S(1)}, bf16[136,256]{1,0:T(8,128)(2,1)S(1)}, u32[]{:S(2)}, u32[]{:S(2)}) collective-permute-start(bf16[136,256]{1,0:T(8,128)(2,1)S(1)} %shard_map.80.refs_0_), channel_id=1, source_target_pairs={{0,2},{1,25},{2,0},{3,27},{4,28},{5,7},{6,30},{7,5},{8,10},{9,17},... | collective-permute-start | bytes 208904 | tf_op jit(solution)/shard_map/ppermute | solution.py:425
  18.3 0.9 %collective-permute-start.9 = (bf16[136,256]{1,0:T(8,128)(2,1)S(1)}, bf16[136,256]{1,0:T(8,128)(2,1)S(1)}, u32[]{:S(2)}, u32[]{:S(2)}) collective-permute-start(bf16[136,256]{1,0:T(8,128)(2,1)S(1)} %shard_map.80.refs_0_), channel_id=1, source_target_pairs={{0,5},{1,9},{2,7},{3,11},{4,12},{5,0},{6,14},{7,2},{8,13},{9,1},{1... | collective-permute-start | bytes 208904 | tf_op jit(solution)/shard_map/ppermute | solution.py:425
  19.3 0.9 %collective-permute-done.7.cross = bf16[2,192,256]{2,1,0:T(8,128)(2,1)S(1)} collective-permute-done((bf16[2,192,256]{2,1,0:T(8,128)(2,1)S(1)}, bf16[2,192,256]{2,1,0:T(8,128)(2,1)S(1)}, u32[]{:S(2)}, u32[]{:S(2)}) %collective-permute-start.7) | collective-permute-done | bytes 196640 | tf_op jit(solution)/shard_map/ppermute | solution.py:393
  20.1 1.2 %shard_map.81 = (f32[256,256]{1,0:T(8,128)S(1)}, f32[256,256]{1,0:T(8,128)S(1)}) custom-call(bf16[256,256]{1,0:T(8,128)(2,1)S(1)} %bitcast.16, bf16[2,96,256]{2,1,0:T(8,128)(2,1)S(1)} %collective-permute-done.4.a, bf16[2,96,256]{2,1,0:T(8,128)(2,1)S(1)} %collective-permute-done.5.b, bf16[2,96,256]{2,1,0:T(8,128)(2,1)S(1)} %collective-permute-done.6.corner, ...), custom_call_target="tpu_custom_call" | custom-call | flops 251658240 | bytes 1150976 | tf_op jit(solution)/shard_map/pallas_call | solution.py:53
  21.3 0.1 collective-permute-done.8.refs_1_
  21.4 0.7 %collective-permute-done.9.refs_2_ = bf16[136,256]{1,0:T(8,128)(2,1)S(1)} collective-permute-done((bf16[136,256]{1,0:T(8,128)(2,1)S(1)}, bf16[136,256]{1,0:T(8,128)(2,1)S(1)}, u32[]{:S(2)}, u32[]{:S(2)}) %collective-permute-start.9) | collective-permute-done | bytes 69664 | tf_op jit(solution)/shard_map/ppermute | solution.py:425
  22.1 0.1 shard_map.82.mine
  22.2 0.7 %collective-permute-start.11 = (bf16[128,256]{1,0:T(8,128)(2,1)S(1)}, bf16[128,256]{1,0:T(8,128)(2,1)S(1)}, u32[]{:S(2)}, u32[]{:S(2)}) collective-permute-start(bf16[128,256]{1,0:T(8,128)(2,1)S(1)} %shard_map.82.mine), channel_id=1, source_target_pairs={{0,1},{1,0},{2,3},{3,2},{4,5},{5,4},{6,7},{7,6},{8,9},{9,8},{10,11... | collective-permute-start | bytes 196616 | tf_op jit(solution)/shard_map/ppermute | solution.py:327
  22.9 0.2 shard_map.83
  23.1 0.7 %collective-permute-done.11.other = bf16[128,256]{1,0:T(8,128)(2,1)S(1)} collective-permute-done((bf16[128,256]{1,0:T(8,128)(2,1)S(1)}, bf16[128,256]{1,0:T(8,128)(2,1)S(1)}, u32[]{:S(2)}, u32[]{:S(2)}) %collective-permute-start.11) | collective-permute-done | bytes 65568 | tf_op jit(solution)/shard_map/ppermute | solution.py:327
  23.8 0.9 %shard_map.84 = (bf16[256,256]{1,0:T(8,128)(2,1)}, bf16[256,256]{1,0:T(8,128)(2,1)}) custom-call(f32[256,256]{1,0:T(8,128)S(1)} %get-tuple-element.28.inner, f32[256,256]{1,0:T(8,128)S(1)} %get-tuple-element.42.factor, f32[256,256]{1,0:T(8,128)S(1)} %get-tuple-element.43.rest, bf16[4,256,256]{2,1,0:T(8,128)(2,1)S(1)} %get-tuple-element.44.reg_weights, ...), custom_call_target="tpu_custom_call" | custom-call | flops 67108864 | bytes 1507328 | tf_op jit(solution)/shard_map/pallas_call | solution.py:53
  (17 shorter events, 0.1 us)
Async XLA Ops:
  0.6 7.3 %collective-permute-start = (bf16[2,256,256]{2,1,0:T(8,128)(2,1)}, bf16[2,256,256]{2,1,0:T(8,128)(2,1)S(1)}, u32[]{:S(2)}, u32[]{:S(2)}) collective-permute-start(bf16[2,256,256]{2,1,0:T(8,128)(2,1)} %bitcast.21), channel_id=1, source_target_pairs={{0,1},{1,0},{2,3},{3,2},{4,5},{5,4},{6,7},{7,6},{8,9},{9,8},{10,11... | collective-permute-start | bytes 786440 | tf_op jit(solution)/shard_map/ppermute | solution.py:327
  2.3 12.0 %collective-permute-start.5 = (bf16[2,96,256]{2,1,0:T(8,128)(2,1)S(1)}, bf16[2,96,256]{2,1,0:T(8,128)(2,1)S(1)}, u32[]{:S(2)}, u32[]{:S(2)}) collective-permute-start(bf16[2,96,256]{2,1,0:T(8,128)(2,1)S(1)} %get-tuple-element.33), channel_id=1, source_target_pairs={{0,28},{4,8},{8,4},{12,16},{16,12},{20,24},{24,20},{28,0},{1,29},{... | collective-permute-start | bytes 294920 | tf_op jit(solution)/shard_map/ppermute | solution.py:353
  7.9 6.4 %collective-permute-start.4 = (bf16[2,96,256]{2,1,0:T(8,128)(2,1)S(1)}, bf16[2,96,256]{2,1,0:T(8,128)(2,1)S(1)}, u32[]{:S(2)}, u32[]{:S(2)}) collective-permute-start(bf16[2,96,256]{2,1,0:T(8,128)(2,1)S(1)} %get-tuple-element.32), channel_id=1, source_target_pairs={{0,4},{1,5},{2,6},{3,7},{4,0},{5,1},{6,2},{7,3},{8,12},{9,13},{10,... | collective-permute-start | bytes 294920 | tf_op jit(solution)/shard_map/ppermute | solution.py:327
  8.0 5.2 %copy-start = (bf16[16,16,256]{2,1,0:T(8,128)(2,1)S(1)}, bf16[16,16,256]{2,1,0:T(8,128)(2,1)}, u32[]{:S(2)}) copy-start(bf16[16,16,256]{2,1,0:T(8,128)(2,1)} %param.6) | copy-start | bytes 393220
  8.0 5.1 %copy-start.1 = (bf16[256,256]{1,0:T(8,128)(2,1)S(1)}, bf16[256,256]{1,0:T(8,128)(2,1)}, u32[]{:S(2)}) copy-start(bf16[256,256]{1,0:T(8,128)(2,1)} %reg_keys.1) | copy-start | bytes 393220
  8.7 7.5 %collective-permute-start.1 = (bf16[136,256]{1,0:T(8,128)(2,1)S(1)}, bf16[136,256]{1,0:T(8,128)(2,1)S(1)}, u32[]{:S(2)}, u32[]{:S(2)}) collective-permute-start(bf16[136,256]{1,0:T(8,128)(2,1)S(1)} %shard_map.79.refs_0_), channel_id=1, source_target_pairs={{0,24},{1,3},{2,26},{3,1},{4,6},{5,29},{6,4},{7,31},{8,16},{9,11},... | collective-permute-start | bytes 208904 | tf_op jit(solution)/shard_map/ppermute | solution.py:425
  9.8 6.4 %collective-permute-start.2 = (bf16[136,256]{1,0:T(8,128)(2,1)S(1)}, bf16[136,256]{1,0:T(8,128)(2,1)S(1)}, u32[]{:S(2)}, u32[]{:S(2)}) collective-permute-start(bf16[136,256]{1,0:T(8,128)(2,1)S(1)} %shard_map.79.refs_0_), channel_id=1, source_target_pairs={{0,8},{1,4},{2,10},{3,6},{4,1},{5,13},{6,3},{7,15},{8,0},{9,12},{1... | collective-permute-start | bytes 208904 | tf_op jit(solution)/shard_map/ppermute | solution.py:425
  10.3 5.8 %collective-permute-start.3 = (bf16[136,256]{1,0:T(8,128)(2,1)S(1)}, bf16[136,256]{1,0:T(8,128)(2,1)S(1)}, u32[]{:S(2)}, u32[]{:S(2)}) collective-permute-start(bf16[136,256]{1,0:T(8,128)(2,1)S(1)} %shard_map.79.refs_0_), channel_id=1, source_target_pairs={{0,16},{1,6},{2,18},{3,4},{4,3},{5,21},{6,1},{7,23},{8,24},{9,14},... | collective-permute-start | bytes 208904 | tf_op jit(solution)/shard_map/ppermute | solution.py:425
  14.4 5.7 %collective-permute-start.7 = (bf16[2,192,256]{2,1,0:T(8,128)(2,1)S(1)}, bf16[2,192,256]{2,1,0:T(8,128)(2,1)S(1)}, u32[]{:S(2)}, u32[]{:S(2)}) collective-permute-start(bf16[2,192,256]{2,1,0:T(8,128)(2,1)S(1)} %pad_maximum_fusion), channel_id=1, source_target_pairs={{0,4},{1,2},{2,1},{3,7},{4,0},{5,6},{6,5},{7,3},{8,12},{9,10},{10,... | collective-permute-start | bytes 589832 | tf_op jit(solution)/shard_map/ppermute | solution.py:393
  15.3 4.0 %collective-permute-start.6 = (bf16[2,96,256]{2,1,0:T(8,128)(2,1)S(1)}, bf16[2,96,256]{2,1,0:T(8,128)(2,1)S(1)}, u32[]{:S(2)}, u32[]{:S(2)}) collective-permute-start(bf16[2,96,256]{2,1,0:T(8,128)(2,1)S(1)} %pad_maximum_fusion.1), channel_id=1, source_target_pairs={{0,1},{1,0},{2,3},{3,2},{4,5},{5,4},{6,7},{7,6},{8,9},{9,8},{10,11... | collective-permute-start | bytes 294920 | tf_op jit(solution)/shard_map/ppermute | solution.py:327
  16.3 5.0 %collective-permute-start.10 = (bf16[136,256]{1,0:T(8,128)(2,1)S(1)}, bf16[136,256]{1,0:T(8,128)(2,1)S(1)}, u32[]{:S(2)}, u32[]{:S(2)}) collective-permute-start(bf16[136,256]{1,0:T(8,128)(2,1)S(1)} %shard_map.80.refs_0_), channel_id=1, source_target_pairs={{0,7},{1,17},{2,5},{3,19},{4,20},{5,2},{6,22},{7,0},{8,15},{9,25},... | collective-permute-start | bytes 208904 | tf_op jit(solution)/shard_map/ppermute | solution.py:425
  17.1 4.3 %collective-permute-start.8 = (bf16[136,256]{1,0:T(8,128)(2,1)S(1)}, bf16[136,256]{1,0:T(8,128)(2,1)S(1)}, u32[]{:S(2)}, u32[]{:S(2)}) collective-permute-start(bf16[136,256]{1,0:T(8,128)(2,1)S(1)} %shard_map.80.refs_0_), channel_id=1, source_target_pairs={{0,2},{1,25},{2,0},{3,27},{4,28},{5,7},{6,30},{7,5},{8,10},{9,17},... | collective-permute-start | bytes 208904 | tf_op jit(solution)/shard_map/ppermute | solution.py:425
  18.3 3.7 %collective-permute-start.9 = (bf16[136,256]{1,0:T(8,128)(2,1)S(1)}, bf16[136,256]{1,0:T(8,128)(2,1)S(1)}, u32[]{:S(2)}, u32[]{:S(2)}) collective-permute-start(bf16[136,256]{1,0:T(8,128)(2,1)S(1)} %shard_map.80.refs_0_), channel_id=1, source_target_pairs={{0,5},{1,9},{2,7},{3,11},{4,12},{5,0},{6,14},{7,2},{8,13},{9,1},{1... | collective-permute-start | bytes 208904 | tf_op jit(solution)/shard_map/ppermute | solution.py:425
  22.2 1.6 %collective-permute-start.11 = (bf16[128,256]{1,0:T(8,128)(2,1)S(1)}, bf16[128,256]{1,0:T(8,128)(2,1)S(1)}, u32[]{:S(2)}, u32[]{:S(2)}) collective-permute-start(bf16[128,256]{1,0:T(8,128)(2,1)S(1)} %shard_map.82.mine), channel_id=1, source_target_pairs={{0,1},{1,0},{2,3},{3,2},{4,5},{5,4},{6,7},{7,6},{8,9},{9,8},{10,11... | collective-permute-start | bytes 196616 | tf_op jit(solution)/shard_map/ppermute | solution.py:327

commit v13 on v12

--- a/solution.py
+++ b/solution.py
@@ -353,8 +353,6 @@
     side_b = lax.ppermute(
         far_cols, "lon", [(i, (i + 1 if i % 2 else i - 1) % lons) for i in range(lons)]
     )
-    near_cols, _ = lax.optimization_barrier((near_cols, core))
-    side_a = swap(near_cols, lats)
 
     payload = call(
         register_kernel,
@@ -364,6 +362,8 @@
         flops=4 * 2 * cells * NREG * 2 * PAIR,
     )
 
+    near_cols, _ = lax.optimization_barrier((near_cols, payload))
+    side_a = swap(near_cols, lats)
     queries = queries.reshape(cells, channels)
     square = jax.ShapeDtypeStruct((cells, channels), F32)
     inner, outer = (count(parts) for parts in segments(rows, cols))

time: 24.8 us -> 24.9 us (level)
  transfers between devices with their start and end apart: 12 -> 12, of which waited for: 4 -> 3; matrix products, arithmetic and copies ran while one was open for 0% -> 0% of each run, Pallas kernels for 18% -> 18%
where the time goes in v13:
time: 24.9 us; the launch traced here: 24.7 us
  starting transfers between devices  16.1 us (65%)
  Pallas kernels  5.53 us (22%)
  waiting for transfers between devices  2.3 us (9%)
  between operations  0.75 us (3%)
    ppermute x6, starting transfers between devices, shards(): gathered.append(lax.ppermute(payload, everyone, pairs))  7.45 us
    ppermute x1, starting transfers between devices, shards(): lax.ppermute(far_cols, 'lon', [(i, (i + 1 if i % 2 else i - 1) % lons) fo...  5.63 us
    pallas_call x8, Pallas kernels, call(): pl.pallas_call(kernel, out_shape=out, in_specs=specs, out_specs=jax.tree....  5.53 us
    ppermute x4, starting transfers between devices, swap(): return lax.ppermute(x, everyone, [(i, i ^ mask) for i in range(devices)])  2.1 us
    ppermute x1, starting transfers between devices, shards(): lax.ppermute(jnp.concatenate([take(own, cells, lat % 2 * (rows - RADIUS)...  0.88 us
    ppermute x1, waiting for transfers between devices, shards(): lax.ppermute(jnp.concatenate([take(own, cells, lat % 2 * (rows - RADIUS)...  0.86 us
    ppermute x6, waiting for transfers between devices, shards(): gathered.append(lax.ppermute(payload, everyone, pairs))  0.76 us
    ppermute x4, waiting for transfers between devices, swap(): return lax.ppermute(x, everyone, [(i, i ^ mask) for i in range(devices)])  0.67 us
  transfers between devices with their start and end apart: 12, of which 3 were waited for; matrix products, arithmetic and copies ran while one was open for 0% of the time, Pallas kernels for 18%

profile of v13, /device:TPU:0, one launch (start us, length us, event | category | flops | bytes accessed | tf_op | source)
XLA Modules:
  0.0 24.7 jit_solution(8547703167019771732)
XLA Ops:
  0.6 0.5 %collective-permute-start = (bf16[2,256,256]{2,1,0:T(8,128)(2,1)}, bf16[2,256,256]{2,1,0:T(8,128)(2,1)S(1)}, u32[]{:S(2)}, u32[]{:S(2)}) collective-permute-start(bf16[2,256,256]{2,1,0:T(8,128)(2,1)} %bitcast.21), channel_id=1, source_target_pairs={{0,1},{1,0},{2,3},{3,2},{4,5},{5,4},{6,7},{7,6},{8,9},{9,8},{10,11... | collective-permute-start | bytes 786440 | tf_op jit(solution)/shard_map/ppermute | solution.py:327
  1.1 1.2 %shard_map.77 = (bf16[2,256,256]{2,1,0:T(8,128)(2,1)S(1)}, bf16[256,256]{1,0:T(8,128)(2,1)S(1)}, bf16[2,96,256]{2,1,0:T(8,128)(2,1)S(1)}, bf16[2,96,256]{2,1,0:T(8,128)(2,1)S(1)}, f32[8,128]{1,0:T(8,128)S(1)}) custom-call(bf16[2,256,256]{2,1,0:T(8,128)(2,1)} %bitcast.22, bf16[256,256]{1,0:T(8,128)(2,1)} %queries_ref.1, s32[8]{0:T(128)} %pole_ref.1, ...), custom_call_target="tpu_custom_call" | custom-call | bytes 393760 | tf_op jit(solution)/shard_map/pallas_call | solution.py:53
  2.3 5.6 %collective-permute-start.5 = (bf16[2,96,256]{2,1,0:T(8,128)(2,1)S(1)}, bf16[2,96,256]{2,1,0:T(8,128)(2,1)S(1)}, u32[]{:S(2)}, u32[]{:S(2)}) collective-permute-start(bf16[2,96,256]{2,1,0:T(8,128)(2,1)S(1)} %get-tuple-element.33), channel_id=1, source_target_pairs={{0,28},{4,8},{8,4},{12,16},{16,12},{20,24},{24,20},{28,0},{1,29},{... | collective-permute-start | bytes 294920 | tf_op jit(solution)/shard_map/ppermute | solution.py:353
  7.9 0.7 %shard_map.79.refs_0_ = bf16[136,256]{1,0:T(8,128)(2,1)S(1)} custom-call(bf16[2,256,256]{2,1,0:T(8,128)(2,1)S(1)} %get-tuple-element.26.own, bf16[2,256,256]{2,1,0:T(8,128)(2,1)S(1)} %collective-permute-done.core.other, bf16[256,256]{1,0:T(8,128)(2,1)S(1)} %get-tuple-element.29.queries), custom_call_target="tpu_custom_call" | custom-call | flops 134217728 | bytes 655360 | tf_op jit(solution)/shard_map/pallas_call | solution.py:53
  8.6 0.1 collective-permute-start.4
  8.7 1.1 %collective-permute-start.1 = (bf16[136,256]{1,0:T(8,128)(2,1)S(1)}, bf16[136,256]{1,0:T(8,128)(2,1)S(1)}, u32[]{:S(2)}, u32[]{:S(2)}) collective-permute-start(bf16[136,256]{1,0:T(8,128)(2,1)S(1)} %shard_map.79.refs_0_), channel_id=1, source_target_pairs={{0,24},{1,3},{2,26},{3,1},{4,6},{5,29},{6,4},{7,31},{8,16},{9,11},... | collective-permute-start | bytes 208904 | tf_op jit(solution)/shard_map/ppermute | solution.py:425
  9.8 0.6 %collective-permute-start.2 = (bf16[136,256]{1,0:T(8,128)(2,1)S(1)}, bf16[136,256]{1,0:T(8,128)(2,1)S(1)}, u32[]{:S(2)}, u32[]{:S(2)}) collective-permute-start(bf16[136,256]{1,0:T(8,128)(2,1)S(1)} %shard_map.79.refs_0_), channel_id=1, source_target_pairs={{0,8},{1,4},{2,10},{3,6},{4,1},{5,13},{6,3},{7,15},{8,0},{9,12},{1... | collective-permute-start | bytes 208904 | tf_op jit(solution)/shard_map/ppermute | solution.py:425
  10.4 2.8 %collective-permute-start.3 = (bf16[136,256]{1,0:T(8,128)(2,1)S(1)}, bf16[136,256]{1,0:T(8,128)(2,1)S(1)}, u32[]{:S(2)}, u32[]{:S(2)}) collective-permute-start(bf16[136,256]{1,0:T(8,128)(2,1)S(1)} %shard_map.79.refs_0_), channel_id=1, source_target_pairs={{0,16},{1,6},{2,18},{3,4},{4,3},{5,21},{6,1},{7,23},{8,24},{9,14},... | collective-permute-start | bytes 208904 | tf_op jit(solution)/shard_map/ppermute | solution.py:425
  13.2 1.2 %shard_map.78 = (f32[256,256]{1,0:T(8,128)S(1)}, f32[256,256]{1,0:T(8,128)S(1)}, f32[256,256]{1,0:T(8,128)S(1)}, bf16[4,256,256]{2,1,0:T(8,128)(2,1)S(1)}) custom-call(bf16[256,256]{1,0:T(8,128)(2,1)S(1)} %bitcast.15, bf16[2,256,256]{2,1,0:T(8,128)(2,1)S(1)} %get-tuple-element.26.own, bf16[2,256,256]{2,1,0:T(8,128)(2,1)S(1)} %collective-permute-done.core.other, ...), custom_call_target="tpu_custom_call" | custom-call | flops 184549376 | bytes 790528 | tf_op jit(solution)/shard_map/pallas_call | solution.py:53
  14.5 0.9 %collective-permute-start.7 = (bf16[2,192,256]{2,1,0:T(8,128)(2,1)S(1)}, bf16[2,192,256]{2,1,0:T(8,128)(2,1)S(1)}, u32[]{:S(2)}, u32[]{:S(2)}) collective-permute-start(bf16[2,192,256]{2,1,0:T(8,128)(2,1)S(1)} %pad_maximum_fusion), channel_id=1, source_target_pairs={{0,4},{1,2},{2,1},{3,7},{4,0},{5,6},{6,5},{7,3},{8,12},{9,10},{10,... | collective-permute-start | bytes 589832 | tf_op jit(solution)/shard_map/ppermute | solution.py:393
  15.4 0.8 %collective-permute-start.6 = (bf16[2,96,256]{2,1,0:T(8,128)(2,1)S(1)}, bf16[2,96,256]{2,1,0:T(8,128)(2,1)S(1)}, u32[]{:S(2)}, u32[]{:S(2)}) collective-permute-start(bf16[2,96,256]{2,1,0:T(8,128)(2,1)S(1)} %pad_maximum_fusion.1), channel_id=1, source_target_pairs={{0,1},{1,0},{2,3},{3,2},{4,5},{5,4},{6,7},{7,6},{8,9},{9,8},{10,11... | collective-permute-start | bytes 294920 | tf_op jit(solution)/shard_map/ppermute | solution.py:327
  16.2 0.1 shard_map.80.refs_0_
  16.3 0.8 %collective-permute-start.10 = (bf16[136,256]{1,0:T(8,128)(2,1)S(1)}, bf16[136,256]{1,0:T(8,128)(2,1)S(1)}, u32[]{:S(2)}, u32[]{:S(2)}) collective-permute-start(bf16[136,256]{1,0:T(8,128)(2,1)S(1)} %shard_map.80.refs_0_), channel_id=1, source_target_pairs={{0,7},{1,17},{2,5},{3,19},{4,20},{5,2},{6,22},{7,0},{8,15},{9,25},... | collective-permute-start | bytes 208904 | tf_op jit(solution)/shard_map/ppermute | solution.py:425
  17.1 1.3 %collective-permute-start.8 = (bf16[136,256]{1,0:T(8,128)(2,1)S(1)}, bf16[136,256]{1,0:T(8,128)(2,1)S(1)}, u32[]{:S(2)}, u32[]{:S(2)}) collective-permute-start(bf16[136,256]{1,0:T(8,128)(2,1)S(1)} %shard_map.80.refs_0_), channel_id=1, source_target_pairs={{0,2},{1,25},{2,0},{3,27},{4,28},{5,7},{6,30},{7,5},{8,10},{9,17},... | collective-permute-start | bytes 208904 | tf_op jit(solution)/shard_map/ppermute | solution.py:425
  18.4 0.9 %collective-permute-start.9 = (bf16[136,256]{1,0:T(8,128)(2,1)S(1)}, bf16[136,256]{1,0:T(8,128)(2,1)S(1)}, u32[]{:S(2)}, u32[]{:S(2)}) collective-permute-start(bf16[136,256]{1,0:T(8,128)(2,1)S(1)} %shard_map.80.refs_0_), channel_id=1, source_target_pairs={{0,5},{1,9},{2,7},{3,11},{4,12},{5,0},{6,14},{7,2},{8,13},{9,1},{1... | collective-permute-start | bytes 208904 | tf_op jit(solution)/shard_map/ppermute | solution.py:425
  19.3 0.9 %collective-permute-done.7.cross = bf16[2,192,256]{2,1,0:T(8,128)(2,1)S(1)} collective-permute-done((bf16[2,192,256]{2,1,0:T(8,128)(2,1)S(1)}, bf16[2,192,256]{2,1,0:T(8,128)(2,1)S(1)}, u32[]{:S(2)}, u32[]{:S(2)}) %collective-permute-start.7) | collective-permute-done | bytes 196640 | tf_op jit(solution)/shard_map/ppermute | solution.py:393
  20.2 1.2 %shard_map.81 = (f32[256,256]{1,0:T(8,128)S(1)}, f32[256,256]{1,0:T(8,128)S(1)}) custom-call(bf16[256,256]{1,0:T(8,128)(2,1)S(1)} %bitcast.16, bf16[2,96,256]{2,1,0:T(8,128)(2,1)S(1)} %collective-permute-done.4.a, bf16[2,96,256]{2,1,0:T(8,128)(2,1)S(1)} %collective-permute-done.5.b, bf16[2,96,256]{2,1,0:T(8,128)(2,1)S(1)} %collective-permute-done.6.corner, ...), custom_call_target="tpu_custom_call" | custom-call | flops 251658240 | bytes 1150976 | tf_op jit(solution)/shard_map/pallas_call | solution.py:53
  21.4 0.0 collective-permute-done.8.refs_1_
  21.4 0.7 %collective-permute-done.9.refs_2_ = bf16[136,256]{1,0:T(8,128)(2,1)S(1)} collective-permute-done((bf16[136,256]{1,0:T(8,128)(2,1)S(1)}, bf16[136,256]{1,0:T(8,128)(2,1)S(1)}, u32[]{:S(2)}, u32[]{:S(2)}) %collective-permute-start.9) | collective-permute-done | bytes 69664 | tf_op jit(solution)/shard_map/ppermute | solution.py:425
  22.2 0.1 shard_map.82.mine
  22.3 0.7 %collective-permute-start.11 = (bf16[128,256]{1,0:T(8,128)(2,1)S(1)}, bf16[128,256]{1,0:T(8,128)(2,1)S(1)}, u32[]{:S(2)}, u32[]{:S(2)}) collective-permute-start(bf16[128,256]{1,0:T(8,128)(2,1)S(1)} %shard_map.82.mine), channel_id=1, source_target_pairs={{0,1},{1,0},{2,3},{3,2},{4,5},{5,4},{6,7},{7,6},{8,9},{9,8},{10,11... | collective-permute-start | bytes 196616 | tf_op jit(solution)/shard_map/ppermute | solution.py:327
  22.9 0.2 shard_map.83
  23.2 0.7 %collective-permute-done.11.other = bf16[128,256]{1,0:T(8,128)(2,1)S(1)} collective-permute-done((bf16[128,256]{1,0:T(8,128)(2,1)S(1)}, bf16[128,256]{1,0:T(8,128)(2,1)S(1)}, u32[]{:S(2)}, u32[]{:S(2)}) %collective-permute-start.11) | collective-permute-done | bytes 65568 | tf_op jit(solution)/shard_map/ppermute | solution.py:327
  23.8 0.9 %shard_map.84 = (bf16[256,256]{1,0:T(8,128)(2,1)}, bf16[256,256]{1,0:T(8,128)(2,1)}) custom-call(f32[256,256]{1,0:T(8,128)S(1)} %get-tuple-element.28.inner, f32[256,256]{1,0:T(8,128)S(1)} %get-tuple-element.42.factor, f32[256,256]{1,0:T(8,128)S(1)} %get-tuple-element.43.rest, bf16[4,256,256]{2,1,0:T(8,128)(2,1)S(1)} %get-tuple-element.44.reg_weights, ...), custom_call_target="tpu_custom_call" | custom-call | flops 67108864 | bytes 1507328 | tf_op jit(solution)/shard_map/pallas_call | solution.py:53
  (17 shorter events, 0.1 us)
Async XLA Ops:
  0.6 7.3 %collective-permute-start = (bf16[2,256,256]{2,1,0:T(8,128)(2,1)}, bf16[2,256,256]{2,1,0:T(8,128)(2,1)S(1)}, u32[]{:S(2)}, u32[]{:S(2)}) collective-permute-start(bf16[2,256,256]{2,1,0:T(8,128)(2,1)} %bitcast.21), channel_id=1, source_target_pairs={{0,1},{1,0},{2,3},{3,2},{4,5},{5,4},{6,7},{7,6},{8,9},{9,8},{10,11... | collective-permute-start | bytes 786440 | tf_op jit(solution)/shard_map/ppermute | solution.py:327
  2.3 12.1 %collective-permute-start.5 = (bf16[2,96,256]{2,1,0:T(8,128)(2,1)S(1)}, bf16[2,96,256]{2,1,0:T(8,128)(2,1)S(1)}, u32[]{:S(2)}, u32[]{:S(2)}) collective-permute-start(bf16[2,96,256]{2,1,0:T(8,128)(2,1)S(1)} %get-tuple-element.33), channel_id=1, source_target_pairs={{0,28},{4,8},{8,4},{12,16},{16,12},{20,24},{24,20},{28,0},{1,29},{... | collective-permute-start | bytes 294920 | tf_op jit(solution)/shard_map/ppermute | solution.py:353
  7.9 5.2 %copy-start.1 = (bf16[256,256]{1,0:T(8,128)(2,1)S(1)}, bf16[256,256]{1,0:T(8,128)(2,1)}, u32[]{:S(2)}) copy-start(bf16[256,256]{1,0:T(8,128)(2,1)} %reg_keys.1) | copy-start | bytes 393220
  8.6 4.6 %copy-start = (bf16[16,16,256]{2,1,0:T(8,128)(2,1)S(1)}, bf16[16,16,256]{2,1,0:T(8,128)(2,1)}, u32[]{:S(2)}) copy-start(bf16[16,16,256]{2,1,0:T(8,128)(2,1)} %param.6) | copy-start | bytes 393220
  8.6 5.8 %collective-permute-start.4 = (bf16[2,96,256]{2,1,0:T(8,128)(2,1)S(1)}, bf16[2,96,256]{2,1,0:T(8,128)(2,1)S(1)}, u32[]{:S(2)}, u32[]{:S(2)}) collective-permute-start(bf16[2,96,256]{2,1,0:T(8,128)(2,1)S(1)} %get-tuple-element.32), channel_id=1, source_target_pairs={{0,4},{1,5},{2,6},{3,7},{4,0},{5,1},{6,2},{7,3},{8,12},{9,13},{10,... | collective-permute-start | bytes 294920 | tf_op jit(solution)/shard_map/ppermute | solution.py:327
  8.7 7.5 %collective-permute-start.1 = (bf16[136,256]{1,0:T(8,128)(2,1)S(1)}, bf16[136,256]{1,0:T(8,128)(2,1)S(1)}, u32[]{:S(2)}, u32[]{:S(2)}) collective-permute-start(bf16[136,256]{1,0:T(8,128)(2,1)S(1)} %shard_map.79.refs_0_), channel_id=1, source_target_pairs={{0,24},{1,3},{2,26},{3,1},{4,6},{5,29},{6,4},{7,31},{8,16},{9,11},... | collective-permute-start | bytes 208904 | tf_op jit(solution)/shard_map/ppermute | solution.py:425
  9.8 6.4 %collective-permute-start.2 = (bf16[136,256]{1,0:T(8,128)(2,1)S(1)}, bf16[136,256]{1,0:T(8,128)(2,1)S(1)}, u32[]{:S(2)}, u32[]{:S(2)}) collective-permute-start(bf16[136,256]{1,0:T(8,128)(2,1)S(1)} %shard_map.79.refs_0_), channel_id=1, source_target_pairs={{0,8},{1,4},{2,10},{3,6},{4,1},{5,13},{6,3},{7,15},{8,0},{9,12},{1... | collective-permute-start | bytes 208904 | tf_op jit(solution)/shard_map/ppermute | solution.py:425
  10.4 5.8 %collective-permute-start.3 = (bf16[136,256]{1,0:T(8,128)(2,1)S(1)}, bf16[136,256]{1,0:T(8,128)(2,1)S(1)}, u32[]{:S(2)}, u32[]{:S(2)}) collective-permute-start(bf16[136,256]{1,0:T(8,128)(2,1)S(1)} %shard_map.79.refs_0_), channel_id=1, source_target_pairs={{0,16},{1,6},{2,18},{3,4},{4,3},{5,21},{6,1},{7,23},{8,24},{9,14},... | collective-permute-start | bytes 208904 | tf_op jit(solution)/shard_map/ppermute | solution.py:425
  14.5 5.7 %collective-permute-start.7 = (bf16[2,192,256]{2,1,0:T(8,128)(2,1)S(1)}, bf16[2,192,256]{2,1,0:T(8,128)(2,1)S(1)}, u32[]{:S(2)}, u32[]{:S(2)}) collective-permute-start(bf16[2,192,256]{2,1,0:T(8,128)(2,1)S(1)} %pad_maximum_fusion), channel_id=1, source_target_pairs={{0,4},{1,2},{2,1},{3,7},{4,0},{5,6},{6,5},{7,3},{8,12},{9,10},{10,... | collective-permute-start | bytes 589832 | tf_op jit(solution)/shard_map/ppermute | solution.py:393
  15.4 4.0 %collective-permute-start.6 = (bf16[2,96,256]{2,1,0:T(8,128)(2,1)S(1)}, bf16[2,96,256]{2,1,0:T(8,128)(2,1)S(1)}, u32[]{:S(2)}, u32[]{:S(2)}) collective-permute-start(bf16[2,96,256]{2,1,0:T(8,128)(2,1)S(1)} %pad_maximum_fusion.1), channel_id=1, source_target_pairs={{0,1},{1,0},{2,3},{3,2},{4,5},{5,4},{6,7},{7,6},{8,9},{9,8},{10,11... | collective-permute-start | bytes 294920 | tf_op jit(solution)/shard_map/ppermute | solution.py:327
  16.3 5.0 %collective-permute-start.10 = (bf16[136,256]{1,0:T(8,128)(2,1)S(1)}, bf16[136,256]{1,0:T(8,128)(2,1)S(1)}, u32[]{:S(2)}, u32[]{:S(2)}) collective-permute-start(bf16[136,256]{1,0:T(8,128)(2,1)S(1)} %shard_map.80.refs_0_), channel_id=1, source_target_pairs={{0,7},{1,17},{2,5},{3,19},{4,20},{5,2},{6,22},{7,0},{8,15},{9,25},... | collective-permute-start | bytes 208904 | tf_op jit(solution)/shard_map/ppermute | solution.py:425
  17.1 4.3 %collective-permute-start.8 = (bf16[136,256]{1,0:T(8,128)(2,1)S(1)}, bf16[136,256]{1,0:T(8,128)(2,1)S(1)}, u32[]{:S(2)}, u32[]{:S(2)}) collective-permute-start(bf16[136,256]{1,0:T(8,128)(2,1)S(1)} %shard_map.80.refs_0_), channel_id=1, source_target_pairs={{0,2},{1,25},{2,0},{3,27},{4,28},{5,7},{6,30},{7,5},{8,10},{9,17},... | collective-permute-start | bytes 208904 | tf_op jit(solution)/shard_map/ppermute | solution.py:425
  18.4 3.7 %collective-permute-start.9 = (bf16[136,256]{1,0:T(8,128)(2,1)S(1)}, bf16[136,256]{1,0:T(8,128)(2,1)S(1)}, u32[]{:S(2)}, u32[]{:S(2)}) collective-permute-start(bf16[136,256]{1,0:T(8,128)(2,1)S(1)} %shard_map.80.refs_0_), channel_id=1, source_target_pairs={{0,5},{1,9},{2,7},{3,11},{4,12},{5,0},{6,14},{7,2},{8,13},{9,1},{1... | collective-permute-start | bytes 208904 | tf_op jit(solution)/shard_map/ppermute | solution.py:425
  22.3 1.6 %collective-permute-start.11 = (bf16[128,256]{1,0:T(8,128)(2,1)S(1)}, bf16[128,256]{1,0:T(8,128)(2,1)S(1)}, u32[]{:S(2)}, u32[]{:S(2)}) collective-permute-start(bf16[128,256]{1,0:T(8,128)(2,1)S(1)} %shard_map.82.mine), channel_id=1, source_target_pairs={{0,1},{1,0},{2,3},{3,2},{4,5},{5,4},{6,7},{7,6},{8,9},{9,8},{10,11... | collective-permute-start | bytes 196616 | tf_op jit(solution)/shard_map/ppermute | solution.py:327
